TPU v7x, 256 devices: a whole 4x4x8 slice. The times are simulated.
256 devices in a mesh: rep: 32 (over x, y, core), tp: 8 (over z).
Axes of the slice: x: 4, y: 4, z: 8, core: 2. Of those that a mesh axis runs over, the one named last changes fastest.
Arguments:
- cache_keys: bfloat16 [1024, 8, 256, 128], P('rep', 'tp'), may hold values from -3 to 3
- cache_values: bfloat16 [1024, 8, 256, 128], P('rep', 'tp'), may hold values from -6 to 6
- cache_lengths: int32 [1024], P('rep'), may hold values from 2 to 256, as said below
- dest_replica: int32 [1024], P('rep'), may hold values from 0 to 31, as said below
- dest_slot: int32 [1024], P('rep'), may hold values from 0 to 31
- queries: bfloat16 [1024, 4, 8192], P('rep', None, 'tp'), may hold values from -7 to 7
- new_keys: bfloat16 [1024, 4, 1024], P('rep', None, 'tp'), may hold values from -6 to 6
- new_values: bfloat16 [1024, 4, 1024], P('rep', None, 'tp'), may hold values from -12 to 12
- out_weight: bfloat16 [8192, 4096], P('tp'), may hold values from -0.75 to 0.75
Outputs:
- layer_out: bfloat16 [1024, 4, 4096], P('rep', None, 'tp')
Inputs may be any that keep to these rules, and one draw needn't show every extreme that they name: `cache_lengths`: every row has at least two cached tokens; some row has exactly 256. Row r moves to slot dest_slot[r] of replica dest_replica[r]; together they give a permutation of all places. Each replica receives exactly 32 rows and sends to each replica either none or exactly 2 of its rows.
All inputs are finite; a program needn't handle non-finite values.
Results may differ from a plain program's by a relative error of at most 0.02.
Values may be sent and summed in bfloat16 or wider, within the bound.
No kernel may reach another device: no remote copies, remote signals or barrier semaphores. Data moves between devices by JAX's collectives and lax.ppermute only.
A program may use at most 128 MiB of HBM per device.

v0:
```python
import math

import jax
import jax.numpy as jnp
from jax import lax
from jax.sharding import PartitionSpec as P

MASKED = -1e30


def cached_part(queries, cache_keys, cache_values, cache_lengths):
    row_count, step_count, feature_count = queries.shape
    kv_heads = cache_keys.shape[1]
    cache_len = cache_keys.shape[2]
    head_size = cache_keys.shape[3]
    group_size = feature_count // (kv_heads * head_size)
    grouped = queries.reshape(row_count, step_count, kv_heads, group_size, head_size)
    scores = jnp.einsum(
        "stkgd,skcd->stkgc", grouped, cache_keys, preferred_element_type=jnp.float32
    ) * (1.0 / math.sqrt(head_size))
    live_keys = jnp.arange(cache_len)[None, :] < cache_lengths[:, None]
    scores = jnp.where(live_keys[:, None, None, None, :], scores, MASKED)
    peak = jnp.max(scores, axis=-1)
    weights = jnp.exp(scores - peak[..., None]).astype(jnp.bfloat16)
    weight_sum = jnp.sum(weights.astype(jnp.float32), axis=-1)
    summed = jnp.einsum(
        "stkgc,skcd->stkgd", weights, cache_values, preferred_element_type=jnp.float32
    )
    return (
        peak.reshape(row_count, step_count, -1),
        weight_sum.reshape(row_count, step_count, -1),
        summed.reshape(row_count, step_count, feature_count),
    )


def fresh_part(queries, new_keys, new_values, head_size):
    row_count, step_count, feature_count = queries.shape
    kv_heads = new_keys.shape[2] // head_size
    group_size = feature_count // (kv_heads * head_size)
    grouped = queries.reshape(row_count, step_count, kv_heads, group_size, head_size)
    fresh_keys = new_keys.reshape(row_count, step_count, kv_heads, head_size)
    fresh_values = new_values.reshape(row_count, step_count, kv_heads, head_size)
    scores = jnp.einsum(
        "stkgd,sukd->stkgu", grouped, fresh_keys, preferred_element_type=jnp.float32
    ) * (1.0 / math.sqrt(head_size))
    causal = jnp.arange(step_count)[None, :] <= jnp.arange(step_count)[:, None]
    scores = jnp.where(causal[None, :, None, None, :], scores, MASKED)
    peak = jnp.max(scores, axis=-1)
    weights = jnp.exp(scores - peak[..., None]).astype(jnp.bfloat16)
    weight_sum = jnp.sum(weights.astype(jnp.float32), axis=-1)
    summed = jnp.einsum(
        "stkgu,sukd->stkgd", weights, fresh_values, preferred_element_type=jnp.float32
    )
    return (
        peak.reshape(row_count, step_count, -1),
        weight_sum.reshape(row_count, step_count, -1),
        summed.reshape(row_count, step_count, feature_count),
    )


def combine_parts(cache_side, fresh_side, head_size):
    peak = jnp.maximum(cache_side[0], fresh_side[0])
    cache_factor = jnp.exp(cache_side[0] - peak)
    fresh_factor = jnp.exp(fresh_side[0] - peak)
    row_count, step_count, head_count = peak.shape
    numerator = (
        cache_side[2].reshape(row_count, step_count, head_count, head_size)
        * cache_factor[..., None]
        + fresh_side[2].reshape(row_count, step_count, head_count, head_size)
        * fresh_factor[..., None]
    )
    denominator = cache_side[1] * cache_factor + fresh_side[1] * fresh_factor
    attended = numerator / denominator[..., None]
    return attended.reshape(row_count, step_count, head_count * head_size).astype(jnp.bfloat16)


def send_layout(dest_replica, replicas, capacity):
    row_count = dest_replica.shape[0]
    row_ids = jnp.arange(row_count)
    same_target = (dest_replica[:, None] == dest_replica[None, :]) & (
        row_ids[None, :] < row_ids[:, None]
    )
    rank_among = jnp.sum(same_target.astype(jnp.int32), axis=1)
    position = dest_replica * capacity + rank_among
    spot_ids = jnp.arange(replicas * capacity)
    placed = position[None, :] == spot_ids[:, None]
    filled = jnp.any(placed, axis=1)
    source = jnp.sum(jnp.where(placed, row_ids[None, :], 0), axis=1)
    return (position, filled, source)


def arrival_index(arrived, row_count):
    spot_ids = jnp.arange(arrived.shape[0])
    matched = arrived[None, :] == jnp.arange(row_count)[:, None] + 1
    where_from = jnp.sum(jnp.where(matched, spot_ids[None, :], 0), axis=1)
    target_slot = jnp.sum(jnp.where(matched, jnp.arange(row_count)[:, None], 0), axis=0)
    return (where_from, target_slot)


def on_device(
    cache_keys,
    cache_values,
    cache_lengths,
    dest_replica,
    dest_slot,
    queries,
    new_keys,
    new_values,
    out_weight,
):
    replicas = lax.axis_size("rep")
    row_count = cache_keys.shape[0]
    step_count = queries.shape[1]
    head_size = cache_keys.shape[3]
    capacity = max(2, 2 * row_count // replicas)
    position, filled, source = send_layout(dest_replica, replicas, capacity)
    labels = jnp.where(filled, jnp.take(dest_slot, source) + 1, 0)
    new_part = fresh_part(queries, new_keys, new_values, head_size)
    key_rows = cache_keys.reshape(row_count, -1)
    value_rows = cache_values.reshape(row_count, -1)
    packed_keys = jnp.where(
        filled[:, None], jnp.take(key_rows, source, axis=0), jnp.zeros((), jnp.bfloat16)
    )
    packed_values = jnp.where(
        filled[:, None], jnp.take(value_rows, source, axis=0), jnp.zeros((), jnp.bfloat16)
    )
    sent_lengths = jnp.where(filled, jnp.take(cache_lengths, source), 0)
    labeled = jnp.stack([labels, sent_lengths], axis=1).reshape(replicas, capacity, 2)
    got_keys, got_values, got_labels = (
        lax.all_to_all(
            packed_keys.reshape(replicas, capacity, -1),
            "rep",
            split_axis=0,
            concat_axis=0,
            tiled=True,
        ),
        lax.all_to_all(
            packed_values.reshape(replicas, capacity, -1),
            "rep",
            split_axis=0,
            concat_axis=0,
            tiled=True,
        ),
        lax.all_to_all(labeled, "rep", split_axis=0, concat_axis=0, tiled=True),
    )
    got_labels = got_labels.reshape(replicas * capacity, 2)
    where_from, target_slot = arrival_index(got_labels[:, 0], row_count)
    moved_keys = jnp.take(got_keys.reshape(replicas * capacity, -1), where_from, axis=0).reshape(
        cache_keys.shape
    )
    moved_values = jnp.take(
        got_values.reshape(replicas * capacity, -1), where_from, axis=0
    ).reshape(cache_values.shape)
    moved_lengths = jnp.take(got_labels[:, 1], where_from)
    cache_side = cached_part(queries, moved_keys, moved_values, moved_lengths)
    attended = combine_parts(cache_side, new_part, head_size)
    pieces = []
    for step_index in range(step_count):
        partial_value = jnp.dot(
            attended[:, step_index], out_weight, preferred_element_type=jnp.float32
        )
        pieces.append(
            lax.psum_scatter(
                partial_value.astype(jnp.bfloat16), "tp", scatter_dimension=1, tiled=True
            ).astype(jnp.float32)
        )
    result = jnp.stack(pieces, axis=1)
    return result.astype(jnp.bfloat16)


def solution(mesh):
    return jax.shard_map(
        on_device,
        mesh=mesh,
        in_specs=(
            P("rep", "tp", None, None),
            P("rep", "tp", None, None),
            P("rep"),
            P("rep"),
            P("rep"),
            P("rep", None, "tp"),
            P("rep", None, "tp"),
            P("rep", None, "tp"),
            P("tp", None),
        ),
        out_specs=P("rep", None, "tp"),
        check_vma=False,
    )
```

profile of v0, /device:TPU:1, one launch (start us, length us, event | category | flops | bytes accessed | tf_op | source)
XLA Modules:
  0.0 354.9 jit_solution(13963977611214334732)
XLA Ops:
  6.5 0.9 convert_reduce_fusion.2
  7.4 0.7 multiply_add_fusion.1
  8.3 1.4 gather_fusion.2
  9.7 1.4 gather_fusion.3
  11.4 0.6 copy.45
  12.1 8.6 %all-to-all-start.1 = ((s32[32,2,2]{1,2,0:T(2,128)}), s32[32,2,2]{1,2,0:T(2,128)S(1)}, u32[]{:S(2)}, u32[]{:S(2)}) async-start(s32[32,2,2]{1,2,0:T(2,128)} %copy.45), calls=%async_computation.1 | async-start | bytes 65536 | tf_op jit(solution)/shard_map/all_to_all | solution.py:144
  20.7 2.9 copy.81
  23.6 5.2 %gather_fusion.5 = bf16[64,32768]{1,0:T(8,128)(2,1)} fusion(bf16[32,32768]{1,0:T(8,128)(2,1)S(1)} %bitcast.133, s32[1024]{0:T(1024)S(1)} %pad_clamp_fusion.2), kind=kCustom, calls=%fused_computation.3.clone | custom fusion | bytes 8388864 | tf_op jit(solution)/shard_map/jit(_take)/gather | solution.py:122
  28.9 2.9 copy.82
  31.8 5.2 %gather_fusion.1 = bf16[64,32768]{1,0:T(8,128)(2,1)} fusion(bf16[32,32768]{1,0:T(8,128)(2,1)S(1)} %bitcast.132, s32[1024]{0:T(1024)S(1)} %pad_clamp_fusion.2), kind=kCustom, calls=%fused_computation.clone | custom fusion | bytes 8388864 | tf_op jit(solution)/shard_map/jit(_take)/gather | solution.py:125
  37.0 6.0 %select_select_fusion.1 = (bf16[64,32768]{1,0:T(8,128)(2,1)}, bf16[64,32768]{1,0:T(8,128)(2,1)}) fusion(bf16[64,32768]{1,0:T(8,128)(2,1)} %gather_fusion.1, pred[64]{0:T(512)(128)(4,1)S(1)} %get-tuple-element.14, pred[64]{0:T(512)(128)(4,1)S(1)} %fusion.30, bf16[64,32768]{1,0:T(8,128)(2,1)} %gather_fusion.5), kind=kLoop, calls=%fused_computation.12 | loop fusion | flops 8388608 | bytes 16777344 | tf_op jit(solution)/shard_map/jit(_where)/select_n | solution.py:124
  43.0 7.7 %reshape.203 = bf16[32,2,32768]{2,1,0:T(2,128)(2,1)} reshape(bf16[64,32768]{1,0:T(8,128)(2,1)} %get-tuple-element.15) | data formatting | bytes 8388608 | tf_op jit(solution)/shard_map/reshape | solution.py:138
  50.7 7.4 %all-to-all-start = ((bf16[32,2,32768]{2,1,0:T(2,128)(2,1)}), bf16[32,2,32768]{2,1,0:T(2,128)(2,1)}, u32[]{:S(2)}, u32[]{:S(2)}) async-start(bf16[32,2,32768]{2,1,0:T(2,128)(2,1)} %reshape.203), calls=%async_computation | async-start | bytes 8388608 | tf_op jit(solution)/shard_map/all_to_all | solution.py:137
  58.1 7.6 %reshape.208 = bf16[32,2,32768]{2,1,0:T(2,128)(2,1)} reshape(bf16[64,32768]{1,0:T(8,128)(2,1)} %get-tuple-element.16) | data formatting | bytes 8388608 | tf_op jit(solution)/shard_map/reshape | solution.py:131
  65.8 44.6 %all-to-all-done = bf16[32,2,32768]{2,1,0:T(2,128)(2,1)} async-done(((bf16[32,2,32768]{2,1,0:T(2,128)(2,1)}), bf16[32,2,32768]{2,1,0:T(2,128)(2,1)}, u32[]{:S(2)}, u32[]{:S(2)}) %all-to-all-start) | async-done | bytes 4194336 | tf_op jit(solution)/shard_map/all_to_all | solution.py:137
  110.3 7.2 %all-to-all-start.2 = ((bf16[32,2,32768]{2,1,0:T(2,128)(2,1)}), bf16[32,2,32768]{2,1,0:T(2,128)(2,1)}, u32[]{:S(2)}, u32[]{:S(2)}) async-start(bf16[32,2,32768]{2,1,0:T(2,128)(2,1)} %reshape.208), calls=%async_computation.2 | async-start | bytes 8388608 | tf_op jit(solution)/shard_map/all_to_all | solution.py:130
  117.5 0.2 reduce-scatter.5.cloned.1.call-start
  117.9 1.3 fusion.36
  119.3 0.3 convert_reduce_fusion.1
  119.6 0.3 convolution_bitcast_fusion
  119.9 1.0 reshape_reshape.7
  121.2 0.7 gather_fusion
  122.0 7.2 %reshape.204 = bf16[64,32768]{1,0:T(8,128)(2,1)} reshape(bf16[32,2,32768]{2,1,0:T(2,128)(2,1)} %all-to-all-done) | data formatting | bytes 8388608 | tf_op jit(solution)/shard_map/reshape | solution.py:152
  129.2 6.4 %gather_fusion.4 = bf16[32,32768]{1,0:T(8,128)(2,1)S(1)} fusion(bf16[64,32768]{1,0:T(8,128)(2,1)} %reshape.204, s32[1024]{0:T(1024)S(1)} %pad_clamp_fusion.1), kind=kCustom, calls=%fused_computation.2.clone | custom fusion | bytes 4194432 | tf_op jit(solution)/shard_map/jit(_take)/gather | solution.py:151
  135.6 34.1 %all-to-all-done.2 = bf16[32,2,32768]{2,1,0:T(2,128)(2,1)} async-done(((bf16[32,2,32768]{2,1,0:T(2,128)(2,1)}), bf16[32,2,32768]{2,1,0:T(2,128)(2,1)}, u32[]{:S(2)}, u32[]{:S(2)}) %all-to-all-start.2) | async-done | bytes 4194336 | tf_op jit(solution)/shard_map/all_to_all | solution.py:130
  169.7 7.2 %reshape.209 = bf16[64,32768]{1,0:T(8,128)(2,1)} reshape(bf16[32,2,32768]{2,1,0:T(2,128)(2,1)} %all-to-all-done.2) | data formatting | bytes 8388608 | tf_op jit(solution)/shard_map/reshape | solution.py:148
  177.0 7.7 %gather_fusion.6 = bf16[32,32768]{1,0:T(8,128)(2,1)} fusion(bf16[64,32768]{1,0:T(8,128)(2,1)} %reshape.209, s32[1024]{0:T(1024)S(1)} %pad_clamp_fusion.1), kind=kCustom, calls=%fused_computation.5.clone | custom fusion | bytes 4194432 | tf_op jit(solution)/shard_map/jit(_take)/gather | solution.py:148
  184.7 2.0 select_bitcast_fusion.1
  186.7 0.5 copy.66
  187.2 0.5 copy.64
  187.7 0.9 fusion.37
  188.7 0.5 convert_reduce_fusion
  189.2 1.3 fusion.16
  190.5 1.3 reshape_reshape.6
  191.9 0.2 div.11
  192.3 0.2 mul.73
  192.7 0.2 mul.76
  193.0 0.7 fusion.24
  193.7 5.6 %convolution_convert_fusion.3 = bf16[32,4096]{1,0:T(8,128)(2,1)} fusion(bf16[1024,4096]{1,0:T(8,128)(2,1)} %param.23, bf16[32,4,1024]{2,0,1:T(8,128)(2,1)S(1)} %fusion.24), kind=kOutput, calls=%fused_computation.10 | convolution fusion | flops 268566528 | bytes 8716288 | tf_op jit(solution)/shard_map/dot_general | solution.py:159
  199.4 5.6 %convolution_convert_fusion.2 = bf16[32,4096]{1,0:T(8,128)(2,1)} fusion(bf16[1024,4096]{1,0:T(8,128)(2,1)} %param.23, bf16[32,4,1024]{2,0,1:T(8,128)(2,1)S(1)} %fusion.24), kind=kOutput, calls=%fused_computation.9 | convolution fusion | flops 268566528 | bytes 8716288 | tf_op jit(solution)/shard_map/dot_general | solution.py:159
  205.1 5.6 %convolution_convert_fusion.1 = bf16[32,4096]{1,0:T(8,128)(2,1)} fusion(bf16[1024,4096]{1,0:T(8,128)(2,1)} %param.23, bf16[32,4,1024]{2,0,1:T(8,128)(2,1)S(1)} %fusion.24), kind=kOutput, calls=%fused_computation.8 | convolution fusion | flops 268566528 | bytes 8716288 | tf_op jit(solution)/shard_map/dot_general | solution.py:159
  210.8 5.7 %convolution_convert_fusion = bf16[32,4096]{1,0:T(8,128)(2,1)} fusion(bf16[1024,4096]{1,0:T(8,128)(2,1)} %param.23, bf16[32,4,1024]{2,0,1:T(8,128)(2,1)S(1)} %fusion.24), kind=kOutput, calls=%fused_computation.7 | convolution fusion | flops 268566528 | bytes 8716288 | tf_op jit(solution)/shard_map/dot_general | solution.py:159
  216.5 16.6 %reduce-scatter.5.cloned.1.call-done = bf16[32,512]{1,0:T(8,128)(2,1)} async-done(((bf16[32,4096]{1,0:T(8,128)(2,1)}), bf16[32,512]{1,0:T(8,128)(2,1)}) %reduce-scatter.5.cloned.1.call-update) | async-done | bytes 32784 | tf_op jit(solution)/shard_map/reduce_scatter | solution.py:163
  233.1 37.9 %reduce-scatter.7.cloned.1.call-done = bf16[32,512]{1,0:T(8,128)(2,1)} async-done(((bf16[32,4096]{1,0:T(8,128)(2,1)}), bf16[32,512]{1,0:T(8,128)(2,1)}) %reduce-scatter.7.cloned.1.call-update) | async-done | bytes 32784 | tf_op jit(solution)/shard_map/reduce_scatter | solution.py:163
  271.0 37.9 %reduce-scatter.9.cloned.1.call-done = bf16[32,512]{1,0:T(8,128)(2,1)} async-done(((bf16[32,4096]{1,0:T(8,128)(2,1)}), bf16[32,512]{1,0:T(8,128)(2,1)}) %reduce-scatter.9.cloned.1.call-update) | async-done | bytes 32784 | tf_op jit(solution)/shard_map/reduce_scatter | solution.py:163
  308.9 37.9 %reduce-scatter.11.cloned.1.call-done = bf16[32,512]{1,0:T(8,128)(2,1)} async-done(((bf16[32,4096]{1,0:T(8,128)(2,1)}), bf16[32,512]{1,0:T(8,128)(2,1)}) %reduce-scatter.11.cloned.1.call-update) | async-done | bytes 32784 | tf_op jit(solution)/shard_map/reduce_scatter | solution.py:163
  346.8 0.8 pad_maximum_fusion
  347.6 0.8 copy.58
  (50 shorter events, 1.9 us)
Async XLA Ops:
  6.5 113.1 %copy-start = (bf16[32,4,128]{2,1,0:T(4,128)(2,1)S(1)}, bf16[32,4,128]{2,1,0:T(4,128)(2,1)}, u32[]{:S(2)}) copy-start(bf16[32,4,128]{2,1,0:T(4,128)(2,1)} %param.22) | copy-start | bytes 98308
  12.1 38.6 %all-to-all-start.1 = ((s32[32,2,2]{1,2,0:T(2,128)}), s32[32,2,2]{1,2,0:T(2,128)S(1)}, u32[]{:S(2)}, u32[]{:S(2)}) async-start(s32[32,2,2]{1,2,0:T(2,128)} %copy.45), calls=%async_computation.1 | async-start | bytes 65536 | tf_op jit(solution)/shard_map/all_to_all | solution.py:144
  50.7 59.7 %all-to-all-start = ((bf16[32,2,32768]{2,1,0:T(2,128)(2,1)}), bf16[32,2,32768]{2,1,0:T(2,128)(2,1)}, u32[]{:S(2)}, u32[]{:S(2)}) async-start(bf16[32,2,32768]{2,1,0:T(2,128)(2,1)} %reshape.203), calls=%async_computation | async-start | bytes 8388608 | tf_op jit(solution)/shard_map/all_to_all | solution.py:137
  65.7 52.0 %copy-start.3 = (bf16[32,4,1024]{2,1,0:T(4,128)(2,1)S(1)}, bf16[32,4,1024]{2,1,0:T(4,128)(2,1)}, u32[]{:S(2)}) copy-start(bf16[32,4,1024]{2,1,0:T(4,128)(2,1)} %param.20) | copy-start | bytes 786436
  65.7 52.1 %copy-start.4 = (bf16[32,4,128]{2,1,0:T(4,128)(2,1)S(1)}, bf16[32,4,128]{2,1,0:T(4,128)(2,1)}, u32[]{:S(2)}) copy-start(bf16[32,4,128]{2,1,0:T(4,128)(2,1)} %param.21) | copy-start | bytes 98308
  110.3 59.4 %all-to-all-start.2 = ((bf16[32,2,32768]{2,1,0:T(2,128)(2,1)}), bf16[32,2,32768]{2,1,0:T(2,128)(2,1)}, u32[]{:S(2)}, u32[]{:S(2)}) async-start(bf16[32,2,32768]{2,1,0:T(2,128)(2,1)} %reshape.208), calls=%async_computation.2 | async-start | bytes 8388608 | tf_op jit(solution)/shard_map/all_to_all | solution.py:130
  117.5 115.6 %reduce-scatter.5.cloned.1.call-start = ((), (), s32[]{:S(2)}) async-start(), calls=%async_computation.7 | async-start | bytes 294912 | tf_op jit(solution)/shard_map/reduce_scatter | solution.py:163
  190.4 2.5 copy-start.2
  199.3 71.7 %reduce-scatter.7.cloned.1.call-start = ((), (), s32[]{:S(2)}) async-start(), calls=%async_computation.8 | async-start | bytes 294912 | tf_op jit(solution)/shard_map/reduce_scatter | solution.py:163
  205.0 103.8 %reduce-scatter.9.cloned.1.call-start = ((), (), s32[]{:S(2)}) async-start(), calls=%async_computation.9 | async-start | bytes 294912 | tf_op jit(solution)/shard_map/reduce_scatter | solution.py:163
  210.7 137.7 %copy-start.1 = (bf16[32,4,128]{2,1,0:T(4,128)(2,1)S(1)}, bf16[32,4,128]{2,1,0:T(4,128)(2,1)}, u32[]{:S(2)}) copy-start(bf16[32,4,128]{2,1,0:T(4,128)(2,1)} %param.22) | copy-start | bytes 98308
  210.7 136.1 %reduce-scatter.11.cloned.1.call-start = ((), (), s32[]{:S(2)}) async-start(), calls=%async_computation.10 | async-start | bytes 294912 | tf_op jit(solution)/shard_map/reduce_scatter | solution.py:163
Sparse Core Ops, SparseCore 0:
  199.4 33.6 reduce-scatter.4
  235.7 35.1 reduce-scatter.6
  273.5 35.3 reduce-scatter.8
  311.4 35.3 reduce-scatter.10
where the time goes:
time: 361 us; the launch traced here: 355 us
  waiting for transfers between devices  209 us (58%)
  local copies, waits for them, and re-layouts  70.2 us (19%)
  matrix products  26.4 us (7%)
  starting transfers between devices  23.5 us (7%)
  between operations  13.4 us (4%)
  other arithmetic  12.3 us (3%)
    reduce_scatter x4, waiting for transfers between devices, on_device(): lax.psum_scatter(partial_value.astype(jnp.bfloat16), 'tp', scatter_dimens...  130 us
    all_to_all x1, waiting for transfers between devices, on_device(): lax.all_to_all(packed_values.reshape(replicas, capacity, -1), 'rep', spli...  44.6 us
    all_to_all x1, waiting for transfers between devices, on_device(): lax.all_to_all(packed_keys.reshape(replicas, capacity, -1), 'rep', split_...  34.1 us
    dot_general x4, matrix products, on_device(): jnp.dot(attended[:, step_index], out_weight, preferred_element_type=jnp.f...  22.6 us
    all_to_all x1, starting transfers between devices, on_device(): lax.all_to_all(labeled, 'rep', split_axis=0, concat_axis=0, tiled=True)  8.59 us
    gather x1, local copies, waits for them, and re-layouts, on_device(): jnp.take(got_keys.reshape(replicas * capacity, -1), where_from, axis=0)  7.71 us
    reshape x1, local copies, waits for them, and re-layouts, on_device(): packed_values.reshape(replicas, capacity, -1)  7.68 us
    reshape x1, local copies, waits for them, and re-layouts, on_device(): packed_keys.reshape(replicas, capacity, -1)  7.62 us
  transfers between devices with their start and end apart: 7, of which 6 were waited for; matrix products, arithmetic and copies ran while one was open for 20% of the time, Pallas kernels for 0%

commit v1 on v0

v1 whole, which is shorter than its diff:
```python
import math

import jax
import jax.numpy as jnp
from jax import lax
from jax.experimental import pallas as pl
from jax.experimental.pallas import tpu as pltpu
from jax.sharding import PartitionSpec as P

MASKED = -1e30
VMEM_BYTES = 48 * 1024 * 1024
PAIR_CHUNK = 4


def vmem_spec():
    return pl.BlockSpec(memory_space=pltpu.VMEM)


def smem_spec():
    return pl.BlockSpec(memory_space=pltpu.SMEM)


def hbm_spec():
    return pl.BlockSpec(memory_space=pl.ANY)


def params():
    return pltpu.CompilerParams(vmem_limit_bytes=VMEM_BYTES)


def spots_matrix(bits, steps):
    replicas, tokens = bits.shape
    shape = (replicas, 2 * steps, tokens)
    spread = jnp.broadcast_to(bits[:, None, :], shape)
    within = lax.broadcasted_iota(jnp.int32, shape, 1)
    token = lax.broadcasted_iota(jnp.int32, shape, 2)
    bit = jnp.where(within < steps, spread & 1, spread >> 1)
    hot = jnp.where((token % steps) == (within % steps), bit, 0)
    return hot.astype(jnp.float32).astype(jnp.bfloat16).reshape(replicas * 2 * steps, tokens)


def route_kernel(steps, target_ref, slot_ref, wire_ref, bits_ref):
    replicas, tokens = wire_ref.shape
    shape = (replicas, tokens)
    replica = lax.broadcasted_iota(jnp.int32, shape, 0)
    token = lax.broadcasted_iota(jnp.int32, shape, 1)
    row = token // steps
    mine = target_ref[...] == replica
    first = jnp.min(jnp.where(mine, row, tokens), axis=1, keepdims=True)
    early = mine & (row == first)
    late = mine & (row != first)
    slots = jnp.broadcast_to(slot_ref[...], shape)
    early_slot = jnp.max(jnp.where(early, slots, -1), axis=1, keepdims=True)
    late_slot = jnp.max(jnp.where(late, slots, -1), axis=1, keepdims=True)
    bits_ref[...] = jnp.where(early, 1, 0) + jnp.where(late, 2, 0)
    wire_ref[...] = jnp.where(row == early_slot, 1, 0) + jnp.where(row == late_slot, 2, 0)


def pack_kernel(steps, bits_ref, rows_ref, out_ref):
    hot = spots_matrix(bits_ref[...], steps)
    out_ref[...] = jnp.dot(hot, rows_ref[...], preferred_element_type=jnp.float32).astype(
        jnp.bfloat16
    )


def take_back(hot, rows):
    return lax.dot_general(
        hot, rows, (((0,), (0,)), ((), ())), preferred_element_type=jnp.float32
    ).astype(jnp.bfloat16)


def attend_kernel(
    steps,
    lengths_ref,
    bits_ref,
    got_ref,
    keys_hbm,
    values_hbm,
    weight_hbm,
    *rest,
):
    groups = weight_hbm.shape[1] // rest[0].shape[1]
    outs = rest[:groups]
    here, keys, values, weight, attended, key_sem, value_sem, weight_sem = rest[groups:]
    rows, context, head_size = keys.shape
    features = attended.shape[1]
    heads = features // head_size
    width = outs[0].shape[1]
    tokens = rows * steps
    me = lax.axis_index("tp")

    chunks = key_sem.shape[0]
    per = rows // chunks
    key_copies, value_copies, weight_copies = [], [], []
    for c in range(chunks):
        part = pl.ds(c * per, per)
        key_copies.append(pltpu.make_async_copy(keys_hbm.at[part], keys.at[part], key_sem.at[c]))
        value_copies.append(
            pltpu.make_async_copy(values_hbm.at[part], values.at[part], value_sem.at[c])
        )
        key_copies[-1].start()
        value_copies[-1].start()
    for k in range(groups):
        start = pl.multiple_of(lax.rem(me + k, groups) * width, width)
        weight_copies.append(
            pltpu.make_async_copy(
                weight_hbm.at[:, pl.ds(start, width)], weight.at[k], weight_sem.at[k]
            )
        )
        weight_copies[-1].start()

    here[...] = take_back(spots_matrix(bits_ref[...], steps), got_ref[...])

    pair = 2 * steps
    lines = heads * pair
    scale = 1.0 / math.sqrt(head_size) * math.log2(math.e)
    line = lax.broadcasted_iota(jnp.int32, (lines, context), 0) % pair
    column = lax.broadcasted_iota(jnp.int32, (lines, context), 1)
    upper = line < steps
    fresh_line = lax.broadcasted_iota(jnp.int32, (lines, pair), 0) % pair
    fresh_column = lax.broadcasted_iota(jnp.int32, (lines, pair), 1)
    fresh_live = (fresh_line // steps == fresh_column // steps) & (fresh_column <= fresh_line)
    out_upper = lax.broadcasted_iota(jnp.int32, (lines, head_size), 0) % pair < steps

    def score(left, right):
        return lax.dot_general(
            left, right, (((1,), (1,)), ((), ())), preferred_element_type=jnp.float32
        )

    for step in range(rows // 2):
        a, b = 2 * step, 2 * step + 1
        if a % per == 0:
            key_copies[a // per].wait()
            value_copies[a // per].wait()
        block = here[a * steps : a * steps + pair, :]
        queries = jnp.concatenate(
            [block[:, h * head_size : (h + 1) * head_size] for h in range(heads)], axis=0
        )
        new_keys = block[:, features : features + head_size]
        new_values = block[:, features + head_size :]
        limit = jnp.where(upper, lengths_ref[a], lengths_ref[b])
        scores = jnp.where(upper, score(queries, keys[a]), score(queries, keys[b]))
        scores = jnp.where(column < limit, scores * scale, MASKED)
        fresh = jnp.where(fresh_live, score(queries, new_keys) * scale, MASKED)
        peak = jnp.maximum(
            jnp.max(scores, axis=1, keepdims=True), jnp.max(fresh, axis=1, keepdims=True)
        )
        weights = jnp.exp2(scores - peak).astype(jnp.bfloat16)
        fresh_weights = jnp.exp2(fresh - peak).astype(jnp.bfloat16)
        total = jnp.sum(weights.astype(jnp.float32), axis=1, keepdims=True) + jnp.sum(
            fresh_weights.astype(jnp.float32), axis=1, keepdims=True
        )
        summed = jnp.where(
            out_upper,
            jnp.dot(weights, values[a], preferred_element_type=jnp.float32),
            jnp.dot(weights, values[b], preferred_element_type=jnp.float32),
        ) + jnp.dot(fresh_weights, new_values, preferred_element_type=jnp.float32)
        result = (summed / total).astype(jnp.bfloat16)
        for h in range(heads):
            attended[a * steps : a * steps + pair, h * head_size : (h + 1) * head_size] = result[
                h * pair : (h + 1) * pair
            ]

    for k in range(groups):
        weight_copies[k].wait()
        outs[k][...] = jnp.dot(
            attended[...], weight[k], preferred_element_type=jnp.float32
        ).astype(jnp.bfloat16)


def merge_kernel(steps, bits_ref, *refs):
    parts, out_ref = refs[:-1], refs[-1]
    total = parts[0][...].astype(jnp.float32)
    for part in parts[1:]:
        total = total + part[...].astype(jnp.float32)
    hot = spots_matrix(bits_ref[...], steps)
    out_ref[...] = jnp.dot(
        hot, total.astype(jnp.bfloat16), preferred_element_type=jnp.float32
    ).astype(jnp.bfloat16)


def unpack_kernel(steps, bits_ref, got_ref, out_ref):
    out_ref[...] = take_back(spots_matrix(bits_ref[...], steps), got_ref[...])


def on_device(
    cache_keys,
    cache_values,
    cache_lengths,
    dest_replica,
    dest_slot,
    queries,
    new_keys,
    new_values,
    out_weight,
):
    replicas = lax.axis_size("rep")
    groups = lax.axis_size("tp")
    rows, _, context, head_size = cache_keys.shape
    steps, features = queries.shape[1:]
    tokens = rows * steps
    width = out_weight.shape[1] // groups
    spots = replicas * 2 * steps
    bf16 = jnp.bfloat16

    def out(shape, dtype=bf16):
        return jax.ShapeDtypeStruct(shape, dtype)

    def kernel(body, out_shape, in_specs, out_specs=None, scratch=(), cost=None):
        return pl.pallas_call(
            lambda *refs: body(steps, *refs),
            out_shape=out_shape,
            in_specs=in_specs,
            out_specs=vmem_spec() if out_specs is None else out_specs,
            scratch_shapes=scratch,
            compiler_params=params(),
            cost_estimate=cost,
        )

    targets = jnp.repeat(dest_replica, steps).reshape(1, tokens)
    slots = jnp.repeat(dest_slot, steps).reshape(1, tokens)
    wire, bits = kernel(
        route_kernel,
        (out((replicas, tokens), jnp.int32), out((replicas, tokens), jnp.int32)),
        [vmem_spec()] * 2,
        (vmem_spec(), vmem_spec()),
    )(targets, slots)
    wire = lax.all_to_all(wire.reshape(replicas, 1, tokens), "rep", 0, 0, tiled=True)
    wire = wire.reshape(replicas, tokens)

    full = features + 2 * head_size
    moving = jnp.concatenate([queries, new_keys, new_values], axis=2).reshape(tokens, full)
    packed = kernel(pack_kernel, out((spots, full)), [vmem_spec()] * 2)(wire, moving)
    got = lax.all_to_all(packed.reshape(replicas, 2 * steps, full), "rep", 0, 0, tiled=True)

    partials = kernel(
        attend_kernel,
        tuple(out((tokens, width)) for _ in range(groups)),
        [smem_spec(), vmem_spec(), vmem_spec(), hbm_spec(), hbm_spec(), hbm_spec()],
        tuple(vmem_spec() for _ in range(groups)),
        [
            pltpu.VMEM((tokens, full), bf16),
            pltpu.VMEM((rows, context, head_size), bf16),
            pltpu.VMEM((rows, context, head_size), bf16),
            pltpu.VMEM((groups, features, width), bf16),
            pltpu.VMEM((tokens, features), bf16),
            pltpu.SemaphoreType.DMA((PAIR_CHUNK,)),
            pltpu.SemaphoreType.DMA((PAIR_CHUNK,)),
            pltpu.SemaphoreType.DMA((groups,)),
        ],
    )(
        cache_lengths,
        bits,
        got.reshape(spots, full),
        cache_keys.reshape(rows, context, head_size),
        cache_values.reshape(rows, context, head_size),
        out_weight,
    )

    order = sorted(range(1, groups), key=lambda k: -min(k, groups - k))
    arrived = [
        lax.ppermute(partials[k], "tp", [(i, (i + k) % groups) for i in range(groups)])
        for k in order
    ]
    back = kernel(merge_kernel, out((spots, width)), [vmem_spec()] * (groups + 1))(
        bits, partials[0], *arrived
    )
    back = lax.all_to_all(back.reshape(replicas, 2 * steps, width), "rep", 0, 0, tiled=True)
    result = kernel(unpack_kernel, out((tokens, width)), [vmem_spec()] * 2)(
        wire, back.reshape(spots, width)
    )
    return result.reshape(rows, steps, width)


def solution(mesh):
    return jax.shard_map(
        on_device,
        mesh=mesh,
        in_specs=(
            P("rep", "tp", None, None),
            P("rep", "tp", None, None),
            P("rep"),
            P("rep"),
            P("rep"),
            P("rep", None, "tp"),
            P("rep", None, "tp"),
            P("rep", None, "tp"),
            P("tp", None),
        ),
        out_specs=P("rep", None, "tp"),
        check_vma=False,
    )
```

time: 361 us -> 91.1 us (0.25); the launches traced: 355 us -> 90.8 us
  waiting for transfers between devices: 209 us -> 21 us
  local copies, waits for them, and re-layouts: 70.2 us -> 4.18 us
  blocking collectives: 0 us -> 29.5 us
  matrix products: 26.4 us -> 0 us
  between operations: 13.4 us -> 0.07 us
  other arithmetic: 12.3 us -> 1.15 us
  Pallas kernels: 0 us -> 10.5 us
    reduce_scatter x4 -> x0, waiting for transfers between devices: 130 us -> none  [on_device(): lax.psum_scatter(partial_value.astype(jnp.bfloat16), 'tp', scatter_dimens...]
    all_to_all x3 -> x1, waiting for transfers between devices: 78.7 us -> 5.64 us  [on_device(): lax.all_to_all(wire.reshape(replicas, 1, tokens), 'rep', 0, 0, tiled=True)]
    all_to_all x0 -> x2, blocking collectives: none -> 29.5 us  [the longest x1 16.7 us: on_device(): lax.all_to_all(packed.reshape(replicas, 2 * steps, full), 'rep', 0, 0, ti...]
    reshape x5 -> x2, local copies, waits for them, and re-layouts: 29.9 us -> 0.77 us  [the longest x1 0.69 us: on_device(): return result.reshape(rows, steps, width)]
    gather x7 -> x0, local copies, waits for them, and re-layouts: 28.1 us -> none  [the longest x1 7.71 us: on_device(): jnp.take(got_keys.reshape(replicas * capacity, -1), where_from, axis=0)]
    dot_general x8 -> x0, matrix products: 26.4 us -> none  [the longest x4 22.6 us: on_device(): jnp.dot(attended[:, step_index], out_weight, preferred_element_type=jnp.f...]
    ppermute x0 -> x7, starting transfers between devices: none -> 15.8 us  [on_device(): lax.ppermute(partials[k], 'tp', [(i, (i + k) % groups) for i in range(gro...]
    ppermute x0 -> x7, waiting for transfers between devices: none -> 15.4 us  [on_device(): lax.ppermute(partials[k], 'tp', [(i, (i + k) % groups) for i in range(gro...]
  transfers between devices with their start and end apart: 7 -> 8, of which waited for: 6 -> 6; matrix products, arithmetic and copies ran while one was open for 20% -> 1% of each run, Pallas kernels for 0% -> 0%
where the time goes in v1:
time: 91.1 us; the launch traced here: 90.8 us
  blocking collectives  29.5 us (32%)
  starting transfers between devices  24.4 us (27%)
  waiting for transfers between devices  21 us (23%)
  Pallas kernels  10.5 us (12%)
  local copies, waits for them, and re-layouts  4.18 us (5%)
  other arithmetic  1.15 us (1%)
    all_to_all x1, blocking collectives, on_device(): lax.all_to_all(packed.reshape(replicas, 2 * steps, full), 'rep', 0, 0, ti...  16.7 us
    ppermute x7, starting transfers between devices, on_device(): lax.ppermute(partials[k], 'tp', [(i, (i + k) % groups) for i in range(gro...  15.8 us
    ppermute x7, waiting for transfers between devices, on_device(): lax.ppermute(partials[k], 'tp', [(i, (i + k) % groups) for i in range(gro...  15.4 us
    all_to_all x1, blocking collectives, on_device(): lax.all_to_all(back.reshape(replicas, 2 * steps, width), 'rep', 0, 0, til...  12.9 us
    pallas_call x1, Pallas kernels, on_device(): kernel(attend_kernel, tuple((out((tokens, width)) for _ in range(groups))...  8.69 us
    all_to_all x1, starting transfers between devices, on_device(): lax.all_to_all(wire.reshape(replicas, 1, tokens), 'rep', 0, 0, tiled=True)  8.59 us
    all_to_all x1, waiting for transfers between devices, on_device(): lax.all_to_all(wire.reshape(replicas, 1, tokens), 'rep', 0, 0, tiled=True)  5.64 us
  transfers between devices with their start and end apart: 8, of which 6 were waited for; matrix products, arithmetic and copies ran while one was open for 1% of the time, Pallas kernels for 0%

profile of v1, /device:TPU:1, one launch (start us, length us, event | category | flops | bytes accessed | tf_op | source)
XLA Modules:
  0.0 90.8 jit_solution(272888563738689966)
XLA Ops:
  0.0 0.0 copy-start.2
  0.0 0.0 copy-start
  0.0 0.9 broadcast_in_dim.6
  0.9 0.1 reshape_reshape.6.refs_0_
  1.0 0.7 broadcast_in_dim.7
  1.7 0.1 reshape_reshape.7.refs_1_
  1.8 0.9 %shard_map.91 = (s32[32,128]{1,0:T(8,128)}, s32[32,128]{1,0:T(8,128)S(1)}) custom-call(s32[1,128]{1,0:T(1,128)S(1)} %reshape_reshape.6.refs_0_, s32[1,128]{1,0:T(1,128)S(1)} %reshape_reshape.7.refs_1_), custom_call_target="tpu_custom_call" | custom-call | tf_op jit(solution)/shard_map/pallas_call | solution.py:222
  2.8 8.6 %all-to-all-start = ((s32[32,1,128]{2,1,0:T(1,128)}), s32[32,1,128]{2,1,0:T(1,128)S(1)}, u32[]{:S(2)}, u32[]{:S(2)}) async-start(s32[32,1,128]{2,1,0:T(1,128)} %bitcast.1), calls=%async_computation | async-start | bytes 32768 | tf_op jit(solution)/shard_map/all_to_all | solution.py:228
  11.4 1.1 %pad_maximum_fusion = bf16[32,4,1280]{2,1,0:T(4,128)(2,1)S(1)} fusion(bf16[32,4,128]{2,1,0:T(4,128)(2,1)} %param.16, bf16[32,4,128]{2,1,0:T(4,128)(2,1)} %param.15, bf16[32,4,1024]{2,1,0:T(4,128)(2,1)} %param.14), kind=kLoop, calls=%fused_computation | loop fusion | flops 983040 | bytes 655360 | tf_op jit(solution)/shard_map/concatenate | solution.py:232
  12.5 0.1 reshape.32.refs_1_
  12.6 5.6 %all-to-all-done = s32[32,1,128]{2,1,0:T(1,128)S(1)} async-done(((s32[32,1,128]{2,1,0:T(1,128)}), s32[32,1,128]{2,1,0:T(1,128)S(1)}, u32[]{:S(2)}, u32[]{:S(2)}) %all-to-all-start) | async-done | bytes 16416 | tf_op jit(solution)/shard_map/all_to_all | solution.py:228
  18.2 0.3 shard_map.92
  18.5 16.7 %all_to_all.15 = bf16[32,8,1280]{2,1,0:T(8,128)(2,1)S(1)} all-to-all(bf16[32,8,1280]{2,1,0:T(8,128)(2,1)S(1)} %bitcast.11), channel_id=1, replica_groups=mesh['rep'=32,'tp'=8] {'rep'}, dimensions={0} | all-to-all | bytes 1310720 | tf_op jit(solution)/shard_map/all_to_all | solution.py:234
  35.2 0.0 copy-done.2
  35.2 0.0 copy-done
  35.2 0.0 copy-start.1
  35.2 1.6 %copy-done.1 = bf16[32,1,256,128]{3,2,1,0:T(8,128)(2,1)S(1)} copy-done((bf16[32,1,256,128]{3,2,1,0:T(8,128)(2,1)S(1)}, bf16[32,1,256,128]{3,2,1,0:T(8,128)(2,1)}, u32[]{:S(2)}) %copy-start.1) | copy-done | bytes 2097176
  36.8 8.7 %shard_map.93 = (bf16[128,512]{1,0:T(8,128)(2,1)S(1)}, bf16[128,512]{1,0:T(8,128)(2,1)S(1)}, bf16[128,512]{1,0:T(8,128)(2,1)S(1)}, bf16[128,512]{1,0:T(8,128)(2,...) custom-call(s32[32]{0:T(128)S(1)} %copy-done.2, ...), custom_call_target="tpu_custom_call" | custom-call | tf_op jit(solution)/shard_map/pallas_call | solution.py:236
  45.5 7.0 %collective-permute-start = (bf16[128,512]{1,0:T(8,128)(2,1)S(1)}, bf16[128,512]{1,0:T(8,128)(2,1)S(1)}, u32[]{:S(2)}, u32[]{:S(2)}) collective-permute-start(bf16[128,512]{1,0:T(8,128)(2,1)S(1)} %get-tuple-element.18), channel_id=1, source_target_pairs={{0,4},{1,5},{2,6},{3,7},{4,0},{5,1},{6,2},{7,3},{8,12},{9,13},{10,... | collective-permute-start | bytes 393224 | tf_op jit(solution)/shard_map/ppermute | solution.py:262
  52.5 1.6 %collective-permute-start.1 = (bf16[128,512]{1,0:T(8,128)(2,1)S(1)}, bf16[128,512]{1,0:T(8,128)(2,1)S(1)}, u32[]{:S(2)}, u32[]{:S(2)}) collective-permute-start(bf16[128,512]{1,0:T(8,128)(2,1)S(1)} %get-tuple-element.19), channel_id=1, source_target_pairs={{0,3},{1,4},{2,5},{3,6},{4,7},{5,0},{6,1},{7,2},{8,11},{9,12},{10,... | collective-permute-start | bytes 393224 | tf_op jit(solution)/shard_map/ppermute | solution.py:262
  54.1 2.9 %collective-permute-start.2 = (bf16[128,512]{1,0:T(8,128)(2,1)S(1)}, bf16[128,512]{1,0:T(8,128)(2,1)S(1)}, u32[]{:S(2)}, u32[]{:S(2)}) collective-permute-start(bf16[128,512]{1,0:T(8,128)(2,1)S(1)} %get-tuple-element.20), channel_id=1, source_target_pairs={{0,5},{1,6},{2,7},{3,0},{4,1},{5,2},{6,3},{7,4},{8,13},{9,14},{10,... | collective-permute-start | bytes 393224 | tf_op jit(solution)/shard_map/ppermute | solution.py:262
  57.0 1.2 %collective-permute-start.3 = (bf16[128,512]{1,0:T(8,128)(2,1)S(1)}, bf16[128,512]{1,0:T(8,128)(2,1)S(1)}, u32[]{:S(2)}, u32[]{:S(2)}) collective-permute-start(bf16[128,512]{1,0:T(8,128)(2,1)S(1)} %get-tuple-element.21), channel_id=1, source_target_pairs={{0,2},{1,3},{2,4},{3,5},{4,6},{5,7},{6,0},{7,1},{8,10},{9,11},{10,... | collective-permute-start | bytes 393224 | tf_op jit(solution)/shard_map/ppermute | solution.py:262
  58.2 2.4 %collective-permute-start.4 = (bf16[128,512]{1,0:T(8,128)(2,1)S(1)}, bf16[128,512]{1,0:T(8,128)(2,1)S(1)}, u32[]{:S(2)}, u32[]{:S(2)}) collective-permute-start(bf16[128,512]{1,0:T(8,128)(2,1)S(1)} %get-tuple-element.22), channel_id=1, source_target_pairs={{0,6},{1,7},{2,0},{3,1},{4,2},{5,3},{6,4},{7,5},{8,14},{9,15},{10,... | collective-permute-start | bytes 393224 | tf_op jit(solution)/shard_map/ppermute | solution.py:262
  60.6 0.0 collective-permute-done.refs_2_
  60.6 0.7 collective-permute-start.5
  61.3 7.5 %collective-permute-done.1.refs_3_ = bf16[128,512]{1,0:T(8,128)(2,1)S(1)} collective-permute-done((bf16[128,512]{1,0:T(8,128)(2,1)S(1)}, bf16[128,512]{1,0:T(8,128)(2,1)S(1)}, u32[]{:S(2)}, u32[]{:S(2)}) %collective-permute-start.1) | collective-permute-done | bytes 131104 | tf_op jit(solution)/shard_map/ppermute | solution.py:262
  68.8 0.0 collective-permute-start.6
  68.8 0.0 collective-permute-done.2.refs_4_
  68.8 1.4 %collective-permute-done.3.refs_5_ = bf16[128,512]{1,0:T(8,128)(2,1)S(1)} collective-permute-done((bf16[128,512]{1,0:T(8,128)(2,1)S(1)}, bf16[128,512]{1,0:T(8,128)(2,1)S(1)}, u32[]{:S(2)}, u32[]{:S(2)}) %collective-permute-start.3) | collective-permute-done | bytes 131104 | tf_op jit(solution)/shard_map/ppermute | solution.py:262
  70.3 3.5 %collective-permute-done.4.refs_6_ = bf16[128,512]{1,0:T(8,128)(2,1)S(1)} collective-permute-done((bf16[128,512]{1,0:T(8,128)(2,1)S(1)}, bf16[128,512]{1,0:T(8,128)(2,1)S(1)}, u32[]{:S(2)}, u32[]{:S(2)}) %collective-permute-start.4) | collective-permute-done | bytes 131104 | tf_op jit(solution)/shard_map/ppermute | solution.py:262
  73.7 2.2 %collective-permute-done.5.refs_7_ = bf16[128,512]{1,0:T(8,128)(2,1)S(1)} collective-permute-done((bf16[128,512]{1,0:T(8,128)(2,1)S(1)}, bf16[128,512]{1,0:T(8,128)(2,1)S(1)}, u32[]{:S(2)}, u32[]{:S(2)}) %collective-permute-start.5) | collective-permute-done | bytes 131104 | tf_op jit(solution)/shard_map/ppermute | solution.py:262
  75.9 0.8 collective-permute-done.6.refs_8_
  76.7 0.3 shard_map.94
  77.1 12.9 %all_to_all.16 = bf16[32,8,512]{2,1,0:T(8,128)(2,1)S(1)} all-to-all(bf16[32,8,512]{2,1,0:T(8,128)(2,1)S(1)} %bitcast.15), channel_id=1, replica_groups=mesh['rep'=32,'tp'=8] {'rep'}, dimensions={0} | all-to-all | bytes 524288 | tf_op jit(solution)/shard_map/all_to_all | solution.py:268
  89.9 0.2 shard_map.95
  90.2 0.7 reshape.39
Async XLA Ops:
  0.0 35.2 %copy-start.2 = (s32[32]{0:T(128)S(1)}, s32[32]{0:T(128)}, u32[]{:S(2)}) copy-start(s32[32]{0:T(128)} %refs_0_.1) | copy-start | bytes 388
  0.0 35.2 %copy-start = (bf16[32,1,256,128]{3,2,1,0:T(8,128)(2,1)S(1)}, bf16[32,1,256,128]{3,2,1,0:T(8,128)(2,1)}, u32[]{:S(2)}) copy-start(bf16[32,1,256,128]{3,2,1,0:T(8,128)(2,1)} %param.9) | copy-start | bytes 6291460
  2.8 15.5 %all-to-all-start = ((s32[32,1,128]{2,1,0:T(1,128)}), s32[32,1,128]{2,1,0:T(1,128)S(1)}, u32[]{:S(2)}, u32[]{:S(2)}) async-start(s32[32,1,128]{2,1,0:T(1,128)} %bitcast.1), calls=%async_computation | async-start | bytes 32768 | tf_op jit(solution)/shard_map/all_to_all | solution.py:228
  35.2 1.6 %copy-start.1 = (bf16[32,1,256,128]{3,2,1,0:T(8,128)(2,1)S(1)}, bf16[32,1,256,128]{3,2,1,0:T(8,128)(2,1)}, u32[]{:S(2)}) copy-start(bf16[32,1,256,128]{3,2,1,0:T(8,128)(2,1)} %param.10) | copy-start | bytes 6291460
  45.5 15.1 %collective-permute-start = (bf16[128,512]{1,0:T(8,128)(2,1)S(1)}, bf16[128,512]{1,0:T(8,128)(2,1)S(1)}, u32[]{:S(2)}, u32[]{:S(2)}) collective-permute-start(bf16[128,512]{1,0:T(8,128)(2,1)S(1)} %get-tuple-element.18), channel_id=1, source_target_pairs={{0,4},{1,5},{2,6},{3,7},{4,0},{5,1},{6,2},{7,3},{8,12},{9,13},{10,... | collective-permute-start | bytes 393224 | tf_op jit(solution)/shard_map/ppermute | solution.py:262
  52.5 16.3 %collective-permute-start.1 = (bf16[128,512]{1,0:T(8,128)(2,1)S(1)}, bf16[128,512]{1,0:T(8,128)(2,1)S(1)}, u32[]{:S(2)}, u32[]{:S(2)}) collective-permute-start(bf16[128,512]{1,0:T(8,128)(2,1)S(1)} %get-tuple-element.19), channel_id=1, source_target_pairs={{0,3},{1,4},{2,5},{3,6},{4,7},{5,0},{6,1},{7,2},{8,11},{9,12},{10,... | collective-permute-start | bytes 393224 | tf_op jit(solution)/shard_map/ppermute | solution.py:262
  54.1 14.7 %collective-permute-start.2 = (bf16[128,512]{1,0:T(8,128)(2,1)S(1)}, bf16[128,512]{1,0:T(8,128)(2,1)S(1)}, u32[]{:S(2)}, u32[]{:S(2)}) collective-permute-start(bf16[128,512]{1,0:T(8,128)(2,1)S(1)} %get-tuple-element.20), channel_id=1, source_target_pairs={{0,5},{1,6},{2,7},{3,0},{4,1},{5,2},{6,3},{7,4},{8,13},{9,14},{10,... | collective-permute-start | bytes 393224 | tf_op jit(solution)/shard_map/ppermute | solution.py:262
  57.0 13.3 %collective-permute-start.3 = (bf16[128,512]{1,0:T(8,128)(2,1)S(1)}, bf16[128,512]{1,0:T(8,128)(2,1)S(1)}, u32[]{:S(2)}, u32[]{:S(2)}) collective-permute-start(bf16[128,512]{1,0:T(8,128)(2,1)S(1)} %get-tuple-element.21), channel_id=1, source_target_pairs={{0,2},{1,3},{2,4},{3,5},{4,6},{5,7},{6,0},{7,1},{8,10},{9,11},{10,... | collective-permute-start | bytes 393224 | tf_op jit(solution)/shard_map/ppermute | solution.py:262
  58.2 15.5 %collective-permute-start.4 = (bf16[128,512]{1,0:T(8,128)(2,1)S(1)}, bf16[128,512]{1,0:T(8,128)(2,1)S(1)}, u32[]{:S(2)}, u32[]{:S(2)}) collective-permute-start(bf16[128,512]{1,0:T(8,128)(2,1)S(1)} %get-tuple-element.22), channel_id=1, source_target_pairs={{0,6},{1,7},{2,0},{3,1},{4,2},{5,3},{6,4},{7,5},{8,14},{9,15},{10,... | collective-permute-start | bytes 393224 | tf_op jit(solution)/shard_map/ppermute | solution.py:262
  60.6 15.3 %collective-permute-start.5 = (bf16[128,512]{1,0:T(8,128)(2,1)S(1)}, bf16[128,512]{1,0:T(8,128)(2,1)S(1)}, u32[]{:S(2)}, u32[]{:S(2)}) collective-permute-start(bf16[128,512]{1,0:T(8,128)(2,1)S(1)} %get-tuple-element.23), channel_id=1, source_target_pairs={{0,1},{1,2},{2,3},{3,4},{4,5},{5,6},{6,7},{7,0},{8,9},{9,10},{10,1... | collective-permute-start | bytes 393224 | tf_op jit(solution)/shard_map/ppermute | solution.py:262
  68.8 7.9 %collective-permute-start.6 = (bf16[128,512]{1,0:T(8,128)(2,1)S(1)}, bf16[128,512]{1,0:T(8,128)(2,1)S(1)}, u32[]{:S(2)}, u32[]{:S(2)}) collective-permute-start(bf16[128,512]{1,0:T(8,128)(2,1)S(1)} %get-tuple-element.24), channel_id=1, source_target_pairs={{0,7},{1,0},{2,1},{3,2},{4,3},{5,4},{6,5},{7,6},{8,15},{9,8},{10,9... | collective-permute-start | bytes 393224 | tf_op jit(solution)/shard_map/ppermute | solution.py:262

commit v2 on v1

v2 whole, which is shorter than its diff:
```python
import math

import jax
import jax.numpy as jnp
from jax import lax
from jax.experimental import pallas as pl
from jax.experimental.pallas import tpu as pltpu
from jax.sharding import PartitionSpec as P

MASKED = -1e30
FIRST = (4, 3, 5)
SECOND = (2, 6, 1, 7)
LAST = (0,)
VMEM_BYTES = 24 * 1024 * 1024


def vmem_spec():
    return pl.BlockSpec(memory_space=pltpu.VMEM)


def smem_spec():
    return pl.BlockSpec(memory_space=pltpu.SMEM)


def hbm_spec():
    return pl.BlockSpec(memory_space=pltpu.HBM)


def in_hbm(array):
    return pltpu.with_memory_space_constraint(array, pltpu.HBM)


def params():
    return pltpu.CompilerParams(vmem_limit_bytes=VMEM_BYTES)


def spots_matrix(bits, steps):
    replicas, tokens = bits.shape
    shape = (replicas, 2 * steps, tokens)
    spread = jnp.broadcast_to(bits[:, None, :], shape)
    within = lax.broadcasted_iota(jnp.int32, shape, 1)
    token = lax.broadcasted_iota(jnp.int32, shape, 2)
    bit = jnp.where(within < steps, spread & 1, spread >> 1)
    hot = jnp.where((token % steps) == (within % steps), bit, 0)
    return hot.astype(jnp.float32).astype(jnp.bfloat16).reshape(replicas * 2 * steps, tokens)


def route_kernel(steps, target_hbm, slot_hbm, wire_ref, bits_ref, target_ref, slot_ref, sems):
    replicas, tokens = wire_ref.shape
    copies = [
        pltpu.make_async_copy(target_hbm, target_ref, sems.at[0]),
        pltpu.make_async_copy(slot_hbm, slot_ref, sems.at[1]),
    ]
    for copy in copies:
        copy.start()
    rows = tokens // steps
    shape = (replicas, tokens)
    spread = lax.broadcasted_iota(jnp.int32, (rows, tokens), 1) // steps
    spread = spread == lax.broadcasted_iota(jnp.int32, (rows, tokens), 0)
    spread = spread.astype(jnp.float32).astype(jnp.bfloat16)
    for copy in copies:
        copy.wait()
    both = jnp.where(
        lax.broadcasted_iota(jnp.int32, (8, rows), 0) == 0, target_ref[...], slot_ref[...]
    )
    both = jnp.dot(
        both.astype(jnp.float32).astype(jnp.bfloat16), spread, preferred_element_type=jnp.float32
    ).astype(jnp.int32)
    replica = lax.broadcasted_iota(jnp.int32, shape, 0)
    row = lax.broadcasted_iota(jnp.int32, shape, 1) // steps
    mine = both[0:1] == replica
    first = jnp.min(jnp.where(mine, row, tokens), axis=1, keepdims=True)
    early = mine & (row == first)
    late = mine & (row != first)
    slots = jnp.broadcast_to(both[1:2], shape)
    early_slot = jnp.max(jnp.where(early, slots, -1), axis=1, keepdims=True)
    late_slot = jnp.max(jnp.where(late, slots, -1), axis=1, keepdims=True)
    bits_ref[...] = jnp.where(early, 1, 0) + jnp.where(late, 2, 0)
    wire_ref[...] = jnp.where(row == early_slot, 1, 0) + jnp.where(row == late_slot, 2, 0)


def pack_kernel(steps, bits_ref, rows_ref, out_ref):
    hot = spots_matrix(bits_ref[...], steps)
    out_ref[...] = jnp.dot(hot, rows_ref[...], preferred_element_type=jnp.float32).astype(
        jnp.bfloat16
    )


def take_back(hot, rows):
    return lax.dot_general(
        hot, rows, (((0,), (0,)), ((), ())), preferred_element_type=jnp.float32
    ).astype(jnp.bfloat16)


def column_copies(offsets, weight_hbm, weight, sems):
    me = lax.axis_index("tp")
    width = weight.shape[2]
    groups = weight_hbm.shape[1] // width
    copies = []
    for i, offset in enumerate(offsets):
        start = pl.multiple_of(lax.rem(me + offset, groups) * width, width)
        copies.append(
            pltpu.make_async_copy(
                weight_hbm.at[:, pl.ds(start, width)], weight.at[i], sems.at[i]
            )
        )
    return copies


def project(attended, copies, weight, outs):
    for i, (copy, out_ref) in enumerate(zip(copies, outs)):
        copy.wait()
        out_ref[...] = jnp.dot(attended, weight[i], preferred_element_type=jnp.float32).astype(
            jnp.bfloat16
        )


def attend_kernel(
    steps,
    lengths_ref,
    bits_ref,
    got_ref,
    keys,
    values_hbm,
    weight_hbm,
    out_ref,
    far_ref,
    right_ref,
    left_ref,
    values,
    weight,
    here,
    cache_scores,
    fresh_scores,
    cache_weights,
    fresh_weights,
    inverse,
    value_sem,
    weight_sems,
):
    value_copy = pltpu.make_async_copy(values_hbm, values, value_sem)
    value_copy.start()
    copies = column_copies(FIRST, weight_hbm, weight, weight_sems)
    for copy in copies:
        copy.start()
    rows, context, head_size = keys.shape
    features = out_ref.shape[1]
    heads = features // head_size
    pair = 2 * steps
    lines = heads * pair
    scale = 1.0 / math.sqrt(head_size) * math.log2(math.e)
    here[...] = take_back(spots_matrix(bits_ref[...], steps), got_ref[...])

    upper = lax.broadcasted_iota(jnp.int32, (lines, context), 0) % pair < steps
    column = lax.broadcasted_iota(jnp.int32, (lines, context), 1)
    fresh_line = lax.broadcasted_iota(jnp.int32, (lines, pair), 0) % pair
    fresh_column = lax.broadcasted_iota(jnp.int32, (lines, pair), 1)
    fresh_live = (fresh_line // steps == fresh_column // steps) & (fresh_column <= fresh_line)
    out_upper = lax.broadcasted_iota(jnp.int32, (lines, head_size), 0) % pair < steps

    def score(left, right):
        return lax.dot_general(
            left, right, (((1,), (1,)), ((), ())), preferred_element_type=jnp.float32
        )

    def mix(weights, block):
        return jnp.dot(weights, block, preferred_element_type=jnp.float32)

    for i in range(rows // 2):
        a, b = 2 * i, 2 * i + 1
        block = here[i * pair : (i + 1) * pair, :]
        queries = jnp.concatenate(
            [block[:, h * head_size : (h + 1) * head_size] for h in range(heads)], axis=0
        )
        limit = jnp.where(upper, lengths_ref[a], lengths_ref[b])
        scores = jnp.where(upper, score(queries, keys[a]), score(queries, keys[b]))
        cache_scores[i] = jnp.where(column < limit, scores * scale, MASKED)
        fresh = score(queries, block[:, features : features + head_size])
        fresh_scores[i] = jnp.where(fresh_live, fresh * scale, MASKED)

    for i in range(rows // 2):
        scores, fresh = cache_scores[i], fresh_scores[i]
        peak = jnp.maximum(
            jnp.max(scores, axis=1, keepdims=True), jnp.max(fresh, axis=1, keepdims=True)
        )
        weights = jnp.exp2(scores - peak).astype(jnp.bfloat16)
        weights_new = jnp.exp2(fresh - peak).astype(jnp.bfloat16)
        cache_weights[i] = weights
        fresh_weights[i] = weights_new
        total = jnp.sum(weights.astype(jnp.float32), axis=1, keepdims=True) + jnp.sum(
            weights_new.astype(jnp.float32), axis=1, keepdims=True
        )
        inverse[i] = jnp.broadcast_to(1.0 / total, (lines, head_size))

    value_copy.wait()
    for i in range(rows // 2):
        lot = slice(i * pair, (i + 1) * pair)
        weights = cache_weights[i]
        summed = jnp.where(out_upper, mix(weights, values[2 * i]), mix(weights, values[2 * i + 1]))
        summed = summed + mix(fresh_weights[i], here[lot, features + head_size :])
        result = (summed * inverse[i]).astype(jnp.bfloat16)
        for h in range(heads):
            out_ref[lot, h * head_size : (h + 1) * head_size] = result[h * pair : (h + 1) * pair]

    project(out_ref[...], copies, weight, (far_ref, right_ref, left_ref))


def project_kernel(offsets, steps, attended_ref, weight_hbm, *refs):
    outs, (weight, sems) = refs[:-2], refs[-2:]
    copies = column_copies(offsets, weight_hbm, weight, sems)
    for copy in copies:
        copy.start()
    project(attended_ref[...], copies, weight, outs)


def wide(ref):
    return ref[...].astype(jnp.float32)


def relay_kernel(steps, right_ref, left_ref, from_left, from_right, far_ref, right_out, left_out):
    even = lax.rem(lax.axis_index("tp"), 2) == 0
    far = wide(far_ref)
    none = jnp.zeros_like(far)
    right = wide(right_ref) + wide(from_left) + jnp.where(even, far, none)
    left = wide(left_ref) + wide(from_right) + jnp.where(even, none, far)
    right_out[...] = right.astype(jnp.bfloat16)
    left_out[...] = left.astype(jnp.bfloat16)


def merge_kernel(steps, bits_ref, *refs):
    parts, out_ref = refs[:-1], refs[-1]
    total = wide(parts[0])
    for part in parts[1:]:
        total = total + wide(part)
    hot = spots_matrix(bits_ref[...], steps)
    out_ref[...] = jnp.dot(
        hot, total.astype(jnp.bfloat16), preferred_element_type=jnp.float32
    ).astype(jnp.bfloat16)


def unpack_kernel(steps, bits_ref, got_ref, out_ref):
    out_ref[...] = take_back(spots_matrix(bits_ref[...], steps), got_ref[...]).reshape(
        out_ref.shape
    )


def on_device(
    cache_keys,
    cache_values,
    cache_lengths,
    dest_replica,
    dest_slot,
    queries,
    new_keys,
    new_values,
    out_weight,
):
    replicas = lax.axis_size("rep")
    groups = lax.axis_size("tp")
    rows, _, context, head_size = cache_keys.shape
    steps, features = queries.shape[1:]
    tokens = rows * steps
    width = out_weight.shape[1] // groups
    spots = replicas * 2 * steps
    bf16 = jnp.bfloat16

    def out(shape, dtype=bf16):
        return jax.ShapeDtypeStruct(shape, dtype)

    def kernel(body, out_shape, in_specs, out_specs=None, scratch=(), cost=None):
        return pl.pallas_call(
            lambda *refs: body(steps, *refs),
            out_shape=out_shape,
            in_specs=in_specs,
            out_specs=vmem_spec() if out_specs is None else out_specs,
            scratch_shapes=scratch,
            compiler_params=params(),
            cost_estimate=cost,
        )

    wire, bits = kernel(
        route_kernel,
        (out((replicas, tokens), jnp.int32), out((replicas, tokens), jnp.int32)),
        [hbm_spec()] * 2,
        (vmem_spec(), vmem_spec()),
        [
            pltpu.VMEM((1, rows), jnp.int32),
            pltpu.VMEM((1, rows), jnp.int32),
            pltpu.SemaphoreType.DMA((2,)),
        ],
    )(in_hbm(dest_replica.reshape(1, rows)), in_hbm(dest_slot.reshape(1, rows)))
    wire = lax.all_to_all(wire.reshape(replicas, 1, tokens), "rep", 0, 0, tiled=True)
    wire = wire.reshape(replicas, tokens)

    full = features + 2 * head_size
    moving = jnp.concatenate([queries, new_keys, new_values], axis=2).reshape(tokens, full)
    packed = kernel(pack_kernel, out((spots, full)), [vmem_spec()] * 2)(wire, moving)
    got = lax.all_to_all(packed.reshape(replicas, 2 * steps, full), "rep", 0, 0, tiled=True)

    lines = features // head_size * 2 * steps
    chunk = out((tokens, width))
    attended, far, to_right, to_left = kernel(
        attend_kernel,
        (out((tokens, features)), chunk, chunk, chunk),
        [smem_spec()] + [vmem_spec()] * 3 + [hbm_spec()] * 2,
        (vmem_spec(),) * 4,
        [
            pltpu.VMEM((rows, context, head_size), bf16),
            pltpu.VMEM((len(FIRST), features, width), bf16),
            pltpu.VMEM((tokens, full), bf16),
            pltpu.VMEM((rows // 2, lines, context), jnp.float32),
            pltpu.VMEM((rows // 2, lines, 2 * steps), jnp.float32),
            pltpu.VMEM((rows // 2, lines, context), bf16),
            pltpu.VMEM((rows // 2, lines, 2 * steps), bf16),
            pltpu.VMEM((rows // 2, lines, head_size), jnp.float32),
            pltpu.SemaphoreType.DMA(()),
            pltpu.SemaphoreType.DMA((len(FIRST),)),
        ],
    )(
        cache_lengths,
        bits,
        got.reshape(spots, full),
        cache_keys.reshape(rows, context, head_size),
        in_hbm(cache_values.reshape(rows, context, head_size)),
        in_hbm(out_weight),
    )

    def shift(block, by):
        return lax.ppermute(block, "tp", [(i, (i + by) % groups) for i in range(groups)])

    far = lax.ppermute(
        far, "tp", [(i, (i + (-2 if i % 2 else 2)) % groups) for i in range(groups)]
    )
    from_left, from_right = shift(to_right, 1), shift(to_left, -1)
    def projected(offsets):
        count = len(offsets)
        return kernel(
            lambda steps, *refs: project_kernel(offsets, steps, *refs),
            (chunk,) * count,
            [vmem_spec(), hbm_spec()],
            (vmem_spec(),) * count,
            [
                pltpu.VMEM((count, features, width), bf16),
                pltpu.SemaphoreType.DMA((count,)),
            ],
            pl.CostEstimate(
                flops=2 * count * tokens * features * width,
                bytes_accessed=2 * count * features * width,
                transcendentals=0,
            ),
        )(attended, in_hbm(out_weight))

    next_right, next_left, near_right, near_left = projected(SECOND)
    (own,) = projected(LAST)
    near_from_left, near_from_right = shift(near_right, 1), shift(near_left, -1)
    relay_right, relay_left = kernel(
        relay_kernel, (chunk, chunk), [vmem_spec()] * 5, (vmem_spec(),) * 2
    )(next_right, next_left, from_left, from_right, far)
    sum_from_left, sum_from_right = shift(relay_right, 2), shift(relay_left, -2)
    back = kernel(merge_kernel, out((spots, width)), [vmem_spec()] * 6)(
        bits, own, near_from_left, near_from_right, sum_from_left, sum_from_right
    )
    back = lax.all_to_all(back.reshape(replicas, 2 * steps, width), "rep", 0, 0, tiled=True)
    return kernel(unpack_kernel, out((rows, steps, width)), [vmem_spec()] * 2)(
        wire, back.reshape(spots, width)
    )


def solution(mesh):
    return jax.shard_map(
        on_device,
        mesh=mesh,
        in_specs=(
            P("rep", "tp", None, None),
            P("rep", "tp", None, None),
            P("rep"),
            P("rep"),
            P("rep"),
            P("rep", None, "tp"),
            P("rep", None, "tp"),
            P("rep", None, "tp"),
            P("tp", None),
        ),
        out_specs=P("rep", None, "tp"),
        check_vma=False,
    )
```

time: 91.1 us -> 77.3 us (0.85)
  waiting for transfers between devices: 21 us -> 9.16 us
  local copies, waits for them, and re-layouts: 4.18 us -> 0.09 us
  blocking collectives: 29.5 us -> 33.5 us
  starting transfers between devices: 24.4 us -> 20.8 us
  Pallas kernels: 10.5 us -> 12.3 us
    ppermute x7, waiting for transfers between devices: 15.4 us -> 3.52 us  [the longest x1 2.32 us: on_device(): lax.ppermute(far, 'tp', [(i, (i + (-2 if i % 2 else 2)) % groups) for i i...]
    all_to_all x1, blocking collectives: 12.9 us -> 16.8 us  [on_device(): lax.all_to_all(back.reshape(replicas, 2 * steps, width), 'rep', 0, 0, til...]
    ppermute x7, starting transfers between devices: 15.8 us -> 12.2 us  [the longest x6 12.2 us: shift(): lax.ppermute(block, 'tp', [(i, (i + by) % groups) for i in range(groups)])]
    broadcast_in_dim x2 -> x0, local copies, waits for them, and re-layouts: 1.6 us -> none  [the longest x1 0.87 us: on_device(): targets = jnp.repeat(dest_replica, steps).reshape(1, tokens)]
    unnamed x6 -> x4, local copies, waits for them, and re-layouts: 1.6 us -> 0.01 us
    pallas_call x1, Pallas kernels: 0.94 us -> 1.89 us  [on_device(): kernel(route_kernel, (out((replicas, tokens), jnp.int32), out((replicas,...]
    pallas_call x3 -> x6, Pallas kernels: 9.26 us -> 10.1 us  [the longest x1 4.67 us: on_device(): kernel(attend_kernel, (out((tokens, features)), chunk, chunk, chunk), [sm...]
  transfers between devices with their start and end apart: 8 -> 8, of which waited for: 6 -> 3; matrix products, arithmetic and copies ran while one was open for 1% -> 2% of each run, Pallas kernels for 0% -> 5%
where the time goes in v2:
time: 77.3 us; the launch traced here: 77 us
  blocking collectives  33.5 us (43%)
  starting transfers between devices  20.8 us (27%)
  Pallas kernels  12.3 us (16%)
  waiting for transfers between devices  9.16 us (12%)
  other arithmetic  1.15 us (1%)
    all_to_all x1, blocking collectives, on_device(): lax.all_to_all(back.reshape(replicas, 2 * steps, width), 'rep', 0, 0, til...  16.8 us
    all_to_all x1, blocking collectives, on_device(): lax.all_to_all(packed.reshape(replicas, 2 * steps, full), 'rep', 0, 0, ti...  16.6 us
    ppermute x6, starting transfers between devices, shift(): lax.ppermute(block, 'tp', [(i, (i + by) % groups) for i in range(groups)])  12.2 us
    all_to_all x1, starting transfers between devices, on_device(): lax.all_to_all(wire.reshape(replicas, 1, tokens), 'rep', 0, 0, tiled=True)  8.6 us
    all_to_all x1, waiting for transfers between devices, on_device(): lax.all_to_all(wire.reshape(replicas, 1, tokens), 'rep', 0, 0, tiled=True)  5.64 us
    pallas_call x1, Pallas kernels, on_device(): kernel(attend_kernel, (out((tokens, features)), chunk, chunk, chunk), [sm...  4.67 us
    pallas_call x2, Pallas kernels, projected(): kernel(lambda steps, *refs: project_kernel(offsets, steps, *refs), (chunk...  4.11 us
    ppermute x1, waiting for transfers between devices, on_device(): lax.ppermute(far, 'tp', [(i, (i + (-2 if i % 2 else 2)) % groups) for i i...  2.32 us
  transfers between devices with their start and end apart: 8, of which 3 were waited for; matrix products, arithmetic and copies ran while one was open for 2% of the time, Pallas kernels for 5%

profile of v2, /device:TPU:1, one launch (start us, length us, event | category | flops | bytes accessed | tf_op | source)
XLA Modules:
  0.0 77.0 jit_solution(8259874722714602687)
XLA Ops:
  0.0 0.0 copy-start.1
  0.0 0.0 copy-start
  0.0 1.9 %shard_map.91 = (s32[32,128]{1,0:T(8,128)}, s32[32,128]{1,0:T(8,128)S(1)}) custom-call(s32[1,32]{1,0:T(1,128)} %bitcast.20, s32[1,32]{1,0:T(1,128)} %bitcast.21), custom_call_target="tpu_custom_call" | custom-call | tf_op jit(solution)/shard_map/pallas_call | solution.py:281
  1.9 8.6 %all-to-all-start = ((s32[32,1,128]{2,1,0:T(1,128)}), s32[32,1,128]{2,1,0:T(1,128)S(1)}, u32[]{:S(2)}, u32[]{:S(2)}) async-start(s32[32,1,128]{2,1,0:T(1,128)} %bitcast.3), calls=%async_computation | async-start | bytes 32768 | tf_op jit(solution)/shard_map/all_to_all | solution.py:292
  10.5 1.1 %pad_maximum_fusion = bf16[32,4,1280]{2,1,0:T(4,128)(2,1)S(1)} fusion(bf16[32,4,128]{2,1,0:T(4,128)(2,1)} %param.16, bf16[32,4,128]{2,1,0:T(4,128)(2,1)} %param.15, bf16[32,4,1024]{2,1,0:T(4,128)(2,1)} %param.14), kind=kLoop, calls=%fused_computation | loop fusion | flops 983040 | bytes 655360 | tf_op jit(solution)/shard_map/concatenate | solution.py:296
  11.7 0.1 reshape.37.refs_1_
  11.7 5.6 %all-to-all-done = s32[32,1,128]{2,1,0:T(1,128)S(1)} async-done(((s32[32,1,128]{2,1,0:T(1,128)}), s32[32,1,128]{2,1,0:T(1,128)S(1)}, u32[]{:S(2)}, u32[]{:S(2)}) %all-to-all-start) | async-done | bytes 16416 | tf_op jit(solution)/shard_map/all_to_all | solution.py:292
  17.4 0.3 shard_map.92
  17.7 16.6 %all_to_all.15 = bf16[32,8,1280]{2,1,0:T(8,128)(2,1)S(1)} all-to-all(bf16[32,8,1280]{2,1,0:T(8,128)(2,1)S(1)} %bitcast.13), channel_id=1, replica_groups=mesh['rep'=32,'tp'=8] {'rep'}, dimensions={0} | all-to-all | bytes 1310720 | tf_op jit(solution)/shard_map/all_to_all | solution.py:298
  34.3 0.0 copy-done.1
  34.4 0.0 copy-done
  34.4 4.7 %shard_map.93 = (bf16[128,1024]{1,0:T(8,128)(2,1)S(1)}, bf16[128,512]{1,0:T(8,128)(2,1)S(1)}, bf16[128,512]{1,0:T(8,128)(2,1)S(1)}, bf16[128,512]{1,0:T(8,128)(2,1)S(1)}) custom-call(s32[32]{0:T(128)S(1)} %copy-done.1, s32[32,128]{1,0:T(8,128)S(1)} %get-tuple-element.18.refs_1_.refs_0_, bf16[256,1280]{1,0:T(8,128)(2,1)S(1)} %bitcast.12, ...), custom_call_target="tpu_custom_call" | custom-call | tf_op jit(solution)/shard_map/pallas_call | solution.py:302
  39.0 1.7 %collective-permute-start.2 = (bf16[128,512]{1,0:T(8,128)(2,1)S(1)}, bf16[128,512]{1,0:T(8,128)(2,1)S(1)}, u32[]{:S(2)}, u32[]{:S(2)}) collective-permute-start(bf16[128,512]{1,0:T(8,128)(2,1)S(1)} %get-tuple-element.24), channel_id=1, source_target_pairs={{0,1},{1,2},{2,3},{3,4},{4,5},{5,6},{6,7},{7,0},{8,9},{9,10},{10,1... | collective-permute-start | bytes 393224 | tf_op jit(solution)/shard_map/ppermute | solution.py:329
  40.8 4.0 %collective-permute-start.3 = (bf16[128,512]{1,0:T(8,128)(2,1)S(1)}, bf16[128,512]{1,0:T(8,128)(2,1)S(1)}, u32[]{:S(2)}, u32[]{:S(2)}) collective-permute-start(bf16[128,512]{1,0:T(8,128)(2,1)S(1)} %get-tuple-element.25), channel_id=1, source_target_pairs={{0,7},{1,0},{2,1},{3,2},{4,3},{5,4},{6,5},{7,6},{8,15},{9,8},{10,9... | collective-permute-start | bytes 393224 | tf_op jit(solution)/shard_map/ppermute | solution.py:329
  44.8 0.0 collective-permute-start.4
  44.8 2.5 %shard_map.95 = (bf16[128,512]{1,0:T(8,128)(2,1)S(1)}, bf16[128,512]{1,0:T(8,128)(2,1)S(1)}, bf16[128,512]{1,0:T(8,128)(2,1)S(1)}, bf16[128,512]{1,0:T(8,128)(2,1)S(1)}) custom-call(bf16[128,1024]{1,0:T(8,128)(2,1)S(1)} %get-tuple-element.19.refs_0_, bf16[1024,4096]{1,0:T(8,128)(2,1)} %refs_1_.3), custom_call_target="tpu_custom_call" | custom-call | flops 536870912 | bytes 4194304 | tf_op jit(solution)/shard_map/pallas_call | solution.py:337
  47.3 2.7 %collective-permute-start = (bf16[128,512]{1,0:T(8,128)(2,1)S(1)}, bf16[128,512]{1,0:T(8,128)(2,1)S(1)}, u32[]{:S(2)}, u32[]{:S(2)}) collective-permute-start(bf16[128,512]{1,0:T(8,128)(2,1)S(1)} %get-tuple-element.20), channel_id=1, source_target_pairs={{0,1},{1,2},{2,3},{3,4},{4,5},{5,6},{6,7},{7,0},{8,9},{9,10},{10,1... | collective-permute-start | bytes 393224 | tf_op jit(solution)/shard_map/ppermute | solution.py:329
  50.0 0.1 collective-permute-start.1
  50.1 0.0 collective-permute-done.2.refs_2_
  50.1 0.0 collective-permute-done.3.refs_3_
  50.1 2.3 %collective-permute-done.4.refs_4_ = bf16[128,512]{1,0:T(8,128)(2,1)S(1)} collective-permute-done((bf16[128,512]{1,0:T(8,128)(2,1)S(1)}, bf16[128,512]{1,0:T(8,128)(2,1)S(1)}, u32[]{:S(2)}, u32[]{:S(2)}) %collective-permute-start.4) | collective-permute-done | bytes 131104 | tf_op jit(solution)/shard_map/ppermute | solution.py:331
  52.5 0.1 shard_map.96
  52.6 0.8 collective-permute-start.5
  53.3 2.9 %collective-permute-start.6 = (bf16[128,512]{1,0:T(8,128)(2,1)S(1)}, bf16[128,512]{1,0:T(8,128)(2,1)S(1)}, u32[]{:S(2)}, u32[]{:S(2)}) collective-permute-start(bf16[128,512]{1,0:T(8,128)(2,1)S(1)} %get-tuple-element.28), channel_id=1, source_target_pairs={{0,6},{1,7},{2,0},{3,1},{4,2},{5,3},{6,4},{7,5},{8,14},{9,15},{10,... | collective-permute-start | bytes 393224 | tf_op jit(solution)/shard_map/ppermute | solution.py:329
  56.2 1.6 %shard_map.94.refs_1_ = bf16[128,512]{1,0:T(8,128)(2,1)S(1)} custom-call(bf16[128,1024]{1,0:T(8,128)(2,1)S(1)} %get-tuple-element.19.refs_0_, bf16[1024,4096]{1,0:T(8,128)(2,1)} %refs_1_.3), custom_call_target="tpu_custom_call" | custom-call | flops 134217728 | bytes 1048576 | tf_op jit(solution)/shard_map/pallas_call | solution.py:337
  57.8 0.0 collective-permute-done.refs_2_
  57.8 0.0 collective-permute-done.1.refs_3_
  57.8 1.2 %collective-permute-done.5.refs_4_ = bf16[128,512]{1,0:T(8,128)(2,1)S(1)} collective-permute-done((bf16[128,512]{1,0:T(8,128)(2,1)S(1)}, bf16[128,512]{1,0:T(8,128)(2,1)S(1)}, u32[]{:S(2)}, u32[]{:S(2)}) %collective-permute-start.5) | collective-permute-done | bytes 131104 | tf_op jit(solution)/shard_map/ppermute | solution.py:329
  59.0 0.0 collective-permute-done.6.refs_5_
  59.0 0.3 shard_map.97
  59.3 16.8 %all_to_all.16 = bf16[32,8,512]{2,1,0:T(8,128)(2,1)S(1)} all-to-all(bf16[32,8,512]{2,1,0:T(8,128)(2,1)S(1)} %bitcast.15), channel_id=1, replica_groups=mesh['rep'=32,'tp'=8] {'rep'}, dimensions={0} | all-to-all | bytes 524288 | tf_op jit(solution)/shard_map/all_to_all | solution.py:363
  76.1 0.9 %shard_map.98 = bf16[32,4,512]{2,1,0:T(4,128)(2,1)} custom-call(s32[32,128]{1,0:T(8,128)S(1)} %bitcast.18, bf16[256,512]{1,0:T(8,128)(2,1)S(1)} %bitcast.16), custom_call_target="tpu_custom_call" | custom-call | tf_op jit(solution)/shard_map/pallas_call | solution.py:364
Async XLA Ops:
  0.0 34.4 %copy-start.1 = (s32[32]{0:T(128)S(1)}, s32[32]{0:T(128)}, u32[]{:S(2)}) copy-start(s32[32]{0:T(128)} %refs_0_.1) | copy-start | bytes 388
  0.0 34.4 %copy-start = (bf16[32,1,256,128]{3,2,1,0:T(8,128)(2,1)S(1)}, bf16[32,1,256,128]{3,2,1,0:T(8,128)(2,1)}, u32[]{:S(2)}) copy-start(bf16[32,1,256,128]{3,2,1,0:T(8,128)(2,1)} %param.9) | copy-start | bytes 6291460
  1.9 15.5 %all-to-all-start = ((s32[32,1,128]{2,1,0:T(1,128)}), s32[32,1,128]{2,1,0:T(1,128)S(1)}, u32[]{:S(2)}, u32[]{:S(2)}) async-start(s32[32,1,128]{2,1,0:T(1,128)} %bitcast.3), calls=%async_computation | async-start | bytes 32768 | tf_op jit(solution)/shard_map/all_to_all | solution.py:292
  39.0 11.1 %collective-permute-start.2 = (bf16[128,512]{1,0:T(8,128)(2,1)S(1)}, bf16[128,512]{1,0:T(8,128)(2,1)S(1)}, u32[]{:S(2)}, u32[]{:S(2)}) collective-permute-start(bf16[128,512]{1,0:T(8,128)(2,1)S(1)} %get-tuple-element.24), channel_id=1, source_target_pairs={{0,1},{1,2},{2,3},{3,4},{4,5},{5,6},{6,7},{7,0},{8,9},{9,10},{10,1... | collective-permute-start | bytes 393224 | tf_op jit(solution)/shard_map/ppermute | solution.py:329
  40.8 9.4 %collective-permute-start.3 = (bf16[128,512]{1,0:T(8,128)(2,1)S(1)}, bf16[128,512]{1,0:T(8,128)(2,1)S(1)}, u32[]{:S(2)}, u32[]{:S(2)}) collective-permute-start(bf16[128,512]{1,0:T(8,128)(2,1)S(1)} %get-tuple-element.25), channel_id=1, source_target_pairs={{0,7},{1,0},{2,1},{3,2},{4,3},{5,4},{6,5},{7,6},{8,15},{9,8},{10,9... | collective-permute-start | bytes 393224 | tf_op jit(solution)/shard_map/ppermute | solution.py:329
  44.8 7.7 %collective-permute-start.4 = (bf16[128,512]{1,0:T(8,128)(2,1)S(1)}, bf16[128,512]{1,0:T(8,128)(2,1)S(1)}, u32[]{:S(2)}, u32[]{:S(2)}) collective-permute-start(bf16[128,512]{1,0:T(8,128)(2,1)S(1)} %get-tuple-element.26), channel_id=1, source_target_pairs={{0,2},{1,7},{2,4},{3,1},{4,6},{5,3},{6,0},{7,5},{8,10},{9,15},{10,... | collective-permute-start | bytes 393224 | tf_op jit(solution)/shard_map/ppermute | solution.py:331
  47.3 10.4 %collective-permute-start = (bf16[128,512]{1,0:T(8,128)(2,1)S(1)}, bf16[128,512]{1,0:T(8,128)(2,1)S(1)}, u32[]{:S(2)}, u32[]{:S(2)}) collective-permute-start(bf16[128,512]{1,0:T(8,128)(2,1)S(1)} %get-tuple-element.20), channel_id=1, source_target_pairs={{0,1},{1,2},{2,3},{3,4},{4,5},{5,6},{6,7},{7,0},{8,9},{9,10},{10,1... | collective-permute-start | bytes 393224 | tf_op jit(solution)/shard_map/ppermute | solution.py:329
  50.0 7.8 %collective-permute-start.1 = (bf16[128,512]{1,0:T(8,128)(2,1)S(1)}, bf16[128,512]{1,0:T(8,128)(2,1)S(1)}, u32[]{:S(2)}, u32[]{:S(2)}) collective-permute-start(bf16[128,512]{1,0:T(8,128)(2,1)S(1)} %get-tuple-element.21), channel_id=1, source_target_pairs={{0,7},{1,0},{2,1},{3,2},{4,3},{5,4},{6,5},{7,6},{8,15},{9,8},{10,9... | collective-permute-start | bytes 393224 | tf_op jit(solution)/shard_map/ppermute | solution.py:329
  52.6 6.4 %collective-permute-start.5 = (bf16[128,512]{1,0:T(8,128)(2,1)S(1)}, bf16[128,512]{1,0:T(8,128)(2,1)S(1)}, u32[]{:S(2)}, u32[]{:S(2)}) collective-permute-start(bf16[128,512]{1,0:T(8,128)(2,1)S(1)} %get-tuple-element.27), channel_id=1, source_target_pairs={{0,2},{1,3},{2,4},{3,5},{4,6},{5,7},{6,0},{7,1},{8,10},{9,11},{10,... | collective-permute-start | bytes 393224 | tf_op jit(solution)/shard_map/ppermute | solution.py:329
  53.3 5.7 %collective-permute-start.6 = (bf16[128,512]{1,0:T(8,128)(2,1)S(1)}, bf16[128,512]{1,0:T(8,128)(2,1)S(1)}, u32[]{:S(2)}, u32[]{:S(2)}) collective-permute-start(bf16[128,512]{1,0:T(8,128)(2,1)S(1)} %get-tuple-element.28), channel_id=1, source_target_pairs={{0,6},{1,7},{2,0},{3,1},{4,2},{5,3},{6,4},{7,5},{8,14},{9,15},{10,... | collective-permute-start | bytes 393224 | tf_op jit(solution)/shard_map/ppermute | solution.py:329

commit v3 on v2

--- a/solution.py
+++ b/solution.py
@@ -8,8 +8,9 @@
 from jax.sharding import PartitionSpec as P
 
 MASKED = -1e30
-FIRST = (4, 3, 5)
-SECOND = (2, 6, 1, 7)
+FIRST = (3, 5)
+SECOND = (4, 2, 6)
+THIRD = (1, 7)
 LAST = (0,)
 VMEM_BYTES = 24 * 1024 * 1024
 
@@ -45,20 +46,23 @@
     return hot.astype(jnp.float32).astype(jnp.bfloat16).reshape(replicas * 2 * steps, tokens)
 
 
-def route_kernel(steps, target_hbm, slot_hbm, wire_ref, bits_ref, target_ref, slot_ref, sems):
-    replicas, tokens = wire_ref.shape
+def route_kernel(steps, *refs):
+    sources, (wire_ref, bits_ref, moving_ref) = refs[:5], refs[5:8]
+    locals_, sems = refs[8:13], refs[13]
+    target_ref, slot_ref, *blocks = locals_
     copies = [
-        pltpu.make_async_copy(target_hbm, target_ref, sems.at[0]),
-        pltpu.make_async_copy(slot_hbm, slot_ref, sems.at[1]),
+        pltpu.make_async_copy(source, local, sems.at[i])
+        for i, (source, local) in enumerate(zip(sources, locals_))
     ]
     for copy in copies:
         copy.start()
+    replicas, tokens = wire_ref.shape
     rows = tokens // steps
     shape = (replicas, tokens)
     spread = lax.broadcasted_iota(jnp.int32, (rows, tokens), 1) // steps
     spread = spread == lax.broadcasted_iota(jnp.int32, (rows, tokens), 0)
     spread = spread.astype(jnp.float32).astype(jnp.bfloat16)
-    for copy in copies:
+    for copy in copies[:2]:
         copy.wait()
     both = jnp.where(
         lax.broadcasted_iota(jnp.int32, (8, rows), 0) == 0, target_ref[...], slot_ref[...]
@@ -77,6 +81,12 @@
     late_slot = jnp.max(jnp.where(late, slots, -1), axis=1, keepdims=True)
     bits_ref[...] = jnp.where(early, 1, 0) + jnp.where(late, 2, 0)
     wire_ref[...] = jnp.where(row == early_slot, 1, 0) + jnp.where(row == late_slot, 2, 0)
+    at = 0
+    for copy, block in zip(copies[2:], blocks):
+        copy.wait()
+        features = block.shape[2]
+        moving_ref[:, at : at + features] = block[...].reshape(tokens, features)
+        at += features
 
 
 def pack_kernel(steps, bits_ref, rows_ref, out_ref):
@@ -124,7 +134,6 @@
     values_hbm,
     weight_hbm,
     out_ref,
-    far_ref,
     right_ref,
     left_ref,
     values,
@@ -202,29 +211,36 @@
         for h in range(heads):
             out_ref[lot, h * head_size : (h + 1) * head_size] = result[h * pair : (h + 1) * pair]
 
-    project(out_ref[...], copies, weight, (far_ref, right_ref, left_ref))
-
-
-def project_kernel(offsets, steps, attended_ref, weight_hbm, *refs):
-    outs, (weight, sems) = refs[:-2], refs[-2:]
-    copies = column_copies(offsets, weight_hbm, weight, sems)
-    for copy in copies:
-        copy.start()
-    project(attended_ref[...], copies, weight, outs)
+    project(out_ref[...], copies, weight, (right_ref, left_ref))
+
+
+def project_kernel(offsets, steps, attended_ref, weight_ref, *outs):
+    me = lax.axis_index("tp")
+    width = outs[0].shape[1]
+    groups = weight_ref.shape[1] // width
+    for offset, out_ref in zip(offsets, outs):
+        start = pl.multiple_of(lax.rem(me + offset, groups) * width, width)
+        out_ref[...] = jnp.dot(
+            attended_ref[...],
+            weight_ref[:, pl.ds(start, width)],
+            preferred_element_type=jnp.float32,
+        ).astype(jnp.bfloat16)
 
 
 def wide(ref):
     return ref[...].astype(jnp.float32)
 
 
-def relay_kernel(steps, right_ref, left_ref, from_left, from_right, far_ref, right_out, left_out):
+def relay_kernel(steps, right_ref, left_ref, from_left, from_right, *refs):
+    far, out_ref = refs[:-1], refs[-1]
     even = lax.rem(lax.axis_index("tp"), 2) == 0
-    far = wide(far_ref)
-    none = jnp.zeros_like(far)
-    right = wide(right_ref) + wide(from_left) + jnp.where(even, far, none)
-    left = wide(left_ref) + wide(from_right) + jnp.where(even, none, far)
-    right_out[...] = right.astype(jnp.bfloat16)
-    left_out[...] = left.astype(jnp.bfloat16)
+    right = wide(right_ref) + wide(from_left)
+    left = wide(left_ref) + wide(from_right)
+    if far:
+        total = jnp.where(even, right, left) + wide(far[0])
+    else:
+        total = jnp.where(even, left, right)
+    out_ref[...] = total.astype(jnp.bfloat16)
 
 
 def merge_kernel(steps, bits_ref, *refs):
@@ -278,32 +294,39 @@
             cost_estimate=cost,
         )
 
-    wire, bits = kernel(
+    full = features + 2 * head_size
+    sources = (
+        dest_replica.reshape(1, rows),
+        dest_slot.reshape(1, rows),
+        queries,
+        new_keys,
+        new_values,
+    )
+    wire, bits, moving = kernel(
         route_kernel,
-        (out((replicas, tokens), jnp.int32), out((replicas, tokens), jnp.int32)),
-        [hbm_spec()] * 2,
-        (vmem_spec(), vmem_spec()),
-        [
-            pltpu.VMEM((1, rows), jnp.int32),
-            pltpu.VMEM((1, rows), jnp.int32),
-            pltpu.SemaphoreType.DMA((2,)),
-        ],
-    )(in_hbm(dest_replica.reshape(1, rows)), in_hbm(dest_slot.reshape(1, rows)))
+        (
+            out((replicas, tokens), jnp.int32),
+            out((replicas, tokens), jnp.int32),
+            out((tokens, full)),
+        ),
+        [hbm_spec()] * 5,
+        (vmem_spec(),) * 3,
+        [pltpu.VMEM(source.shape, source.dtype) for source in sources]
+        + [pltpu.SemaphoreType.DMA((5,))],
+    )(*(in_hbm(source) for source in sources))
     wire = lax.all_to_all(wire.reshape(replicas, 1, tokens), "rep", 0, 0, tiled=True)
     wire = wire.reshape(replicas, tokens)
 
-    full = features + 2 * head_size
-    moving = jnp.concatenate([queries, new_keys, new_values], axis=2).reshape(tokens, full)
     packed = kernel(pack_kernel, out((spots, full)), [vmem_spec()] * 2)(wire, moving)
     got = lax.all_to_all(packed.reshape(replicas, 2 * steps, full), "rep", 0, 0, tiled=True)
 
     lines = features // head_size * 2 * steps
     chunk = out((tokens, width))
-    attended, far, to_right, to_left = kernel(
+    attended, to_right, to_left = kernel(
         attend_kernel,
-        (out((tokens, features)), chunk, chunk, chunk),
+        (out((tokens, features)), chunk, chunk),
         [smem_spec()] + [vmem_spec()] * 3 + [hbm_spec()] * 2,
-        (vmem_spec(),) * 4,
+        (vmem_spec(),) * 3,
         [
             pltpu.VMEM((rows, context, head_size), bf16),
             pltpu.VMEM((len(FIRST), features, width), bf16),
@@ -328,37 +351,41 @@
     def shift(block, by):
         return lax.ppermute(block, "tp", [(i, (i + by) % groups) for i in range(groups)])
 
-    far = lax.ppermute(
-        far, "tp", [(i, (i + (-2 if i % 2 else 2)) % groups) for i in range(groups)]
-    )
+    def cross(block, by):
+        return lax.ppermute(
+            block, "tp", [(i, (i + (-by if i % 2 else by)) % groups) for i in range(groups)]
+        )
+
     from_left, from_right = shift(to_right, 1), shift(to_left, -1)
     def projected(offsets):
         count = len(offsets)
         return kernel(
             lambda steps, *refs: project_kernel(offsets, steps, *refs),
             (chunk,) * count,
-            [vmem_spec(), hbm_spec()],
+            [vmem_spec()] * 2,
             (vmem_spec(),) * count,
-            [
-                pltpu.VMEM((count, features, width), bf16),
-                pltpu.SemaphoreType.DMA((count,)),
-            ],
+            (),
             pl.CostEstimate(
                 flops=2 * count * tokens * features * width,
                 bytes_accessed=2 * count * features * width,
                 transcendentals=0,
             ),
-        )(attended, in_hbm(out_weight))
-
-    next_right, next_left, near_right, near_left = projected(SECOND)
+        )(attended, out_weight)
+
+    far, next_right, next_left = projected(SECOND)
+    far = cross(far, 2)
+    near_right, near_left = projected(THIRD)
     (own,) = projected(LAST)
+    inner = (next_right, next_left, from_left, from_right)
+    relay = [
+        kernel(relay_kernel, chunk, [vmem_spec()] * len(blocks))(*blocks)
+        for blocks in (inner, (*inner, far))
+    ]
+    first = cross(relay[0], -2)
     near_from_left, near_from_right = shift(near_right, 1), shift(near_left, -1)
-    relay_right, relay_left = kernel(
-        relay_kernel, (chunk, chunk), [vmem_spec()] * 5, (vmem_spec(),) * 2
-    )(next_right, next_left, from_left, from_right, far)
-    sum_from_left, sum_from_right = shift(relay_right, 2), shift(relay_left, -2)
+    second = cross(relay[1], 2)
     back = kernel(merge_kernel, out((spots, width)), [vmem_spec()] * 6)(
-        bits, own, near_from_left, near_from_right, sum_from_left, sum_from_right
+        bits, own, near_from_left, near_from_right, first, second
     )
     back = lax.all_to_all(back.reshape(replicas, 2 * steps, width), "rep", 0, 0, tiled=True)
     return kernel(unpack_kernel, out((rows, steps, width)), [vmem_spec()] * 2)(

time: 77.3 us -> 74.8 us (0.968)
  blocking collectives: 33.5 us -> 47.7 us
  starting transfers between devices: 20.8 us -> 11.1 us
  Pallas kernels: 12.3 us -> 8.26 us
  waiting for transfers between devices: 9.16 us -> 7.47 us
  other arithmetic: 1.15 us -> 0.01 us
    all_to_all x0 -> x1, blocking collectives: none -> 15.3 us  [on_device(): lax.all_to_all(wire.reshape(replicas, 1, tokens), 'rep', 0, 0, tiled=True)]
    all_to_all x1 -> x0, starting transfers between devices: 8.6 us -> none  [on_device(): lax.all_to_all(wire.reshape(replicas, 1, tokens), 'rep', 0, 0, tiled=True)]
    all_to_all x1 -> x0, waiting for transfers between devices: 5.64 us -> none  [on_device(): lax.all_to_all(wire.reshape(replicas, 1, tokens), 'rep', 0, 0, tiled=True)]
    ppermute x6 -> x4, starting transfers between devices: 12.2 us -> 8.52 us  [shift(): lax.ppermute(block, 'tp', [(i, (i + by) % groups) for i in range(groups)])]
    ppermute x1 -> x3, waiting for transfers between devices: 2.32 us -> 5.45 us  [cross(): lax.ppermute(block, 'tp', [(i, (i + (-by if i % 2 else by)) % groups) for...]
    pallas_call x2 -> x3, Pallas kernels: 4.11 us -> 1.41 us  [projected(): kernel(lambda steps, *refs: project_kernel(offsets, steps, *refs), (chunk...]
    ppermute x1 -> x3, starting transfers between devices: 0.01 us -> 2.58 us  [cross(): lax.ppermute(block, 'tp', [(i, (i + (-by if i % 2 else by)) % groups) for...]
    all_to_all x1, blocking collectives: 16.8 us -> 15.5 us  [on_device(): lax.all_to_all(back.reshape(replicas, 2 * steps, width), 'rep', 0, 0, til...]
  transfers between devices with their start and end apart: 8 -> 7, of which waited for: 3 -> 4; matrix products, arithmetic and copies ran while one was open for 2% -> 0% of each run, Pallas kernels for 5% -> 2%
where the time goes in v3:
time: 74.8 us; the launch traced here: 74.6 us
  blocking collectives  47.7 us (64%)
  starting transfers between devices  11.1 us (15%)
  Pallas kernels  8.26 us (11%)
  waiting for transfers between devices  7.47 us (10%)
    all_to_all x1, blocking collectives, on_device(): lax.all_to_all(packed.reshape(replicas, 2 * steps, full), 'rep', 0, 0, ti...  16.9 us
    all_to_all x1, blocking collectives, on_device(): lax.all_to_all(back.reshape(replicas, 2 * steps, width), 'rep', 0, 0, til...  15.5 us
    all_to_all x1, blocking collectives, on_device(): lax.all_to_all(wire.reshape(replicas, 1, tokens), 'rep', 0, 0, tiled=True)  15.3 us
    ppermute x4, starting transfers between devices, shift(): lax.ppermute(block, 'tp', [(i, (i + by) % groups) for i in range(groups)])  8.52 us
    ppermute x3, waiting for transfers between devices, cross(): lax.ppermute(block, 'tp', [(i, (i + (-by if i % 2 else by)) % groups) for...  5.45 us
    pallas_call x1, Pallas kernels, on_device(): kernel(attend_kernel, (out((tokens, features)), chunk, chunk), [smem_spec...  3.84 us
    ppermute x3, starting transfers between devices, cross(): lax.ppermute(block, 'tp', [(i, (i + (-by if i % 2 else by)) % groups) for...  2.58 us
    ppermute x4, waiting for transfers between devices, shift(): lax.ppermute(block, 'tp', [(i, (i + by) % groups) for i in range(groups)])  2.02 us
  transfers between devices with their start and end apart: 7, of which 4 were waited for; matrix products, arithmetic and copies ran while one was open for 0% of the time, Pallas kernels for 2%

profile of v3, /device:TPU:1, one launch (start us, length us, event | category | flops | bytes accessed | tf_op | source)
XLA Modules:
  0.0 74.6 jit_solution(17704446592835207570)
XLA Ops:
  0.0 0.0 copy-start.1
  0.0 0.0 copy-start
  0.0 1.4 %shard_map.91 = (s32[32,128]{1,0:T(8,128)S(1)}, s32[32,128]{1,0:T(8,128)S(1)}, bf16[128,1280]{1,0:T(8,128)(2,1)S(1)}) custom-call(s32[1,32]{1,0:T(1,128)} %bitcast.23, s32[1,32]{1,0:T(1,128)} %bitcast.24, bf16[32,4,1024]{2,1,0:T(4,128)(2,1)} %refs_2_.1, bf16[32,4,128]{2,1,0:T(4,128)(2,1)} %refs_3_.1, bf16[32,4,128]{2,1,0:T(4,128)(2,1)} %refs_4_.1), custom_call_target="tpu_custom_call" | custom-call | tf_op jit(solution)/shard_map/pallas_call | solution.py:305
  1.4 15.3 %all_to_all.15 = s32[32,1,128]{2,1,0:T(1,128)S(1)} all-to-all(s32[32,1,128]{2,1,0:T(1,128)S(1)} %bitcast.21), channel_id=1, replica_groups=mesh['rep'=32,'tp'=8] {'rep'}, dimensions={0} | all-to-all | bytes 32768 | tf_op jit(solution)/shard_map/all_to_all | solution.py:317
  16.7 0.0 slice-start
  16.7 0.3 shard_map.92
  17.0 16.9 %all_to_all.16 = bf16[32,8,1280]{2,1,0:T(8,128)(2,1)S(1)} all-to-all(bf16[32,8,1280]{2,1,0:T(8,128)(2,1)S(1)} %bitcast.15), channel_id=1, replica_groups=mesh['rep'=32,'tp'=8] {'rep'}, dimensions={0} | all-to-all | bytes 1310720 | tf_op jit(solution)/shard_map/all_to_all | solution.py:321
  34.0 0.0 copy-done.1
  34.0 0.0 copy-done
  34.0 0.0 slice-start.1
  34.0 3.8 %shard_map.93 = (bf16[128,1024]{1,0:T(8,128)(2,1)S(1)}, bf16[128,512]{1,0:T(8,128)(2,1)S(1)}, bf16[128,512]{1,0:T(8,128)(2,1)S(1)}) custom-call(s32[32]{0:T(128)S(1)} %copy-done.1, s32[32,128]{1,0:T(8,128)S(1)} %get-tuple-element.17.refs_1_.refs_0_, bf16[256,1280]{1,0:T(8,128)(2,1)S(1)} %bitcast.14, bf16[32,256,128]{2,1,0:T(8,128)(2,1)S(1)} %bitcast.16, ...), custom_call_target="tpu_custom_call" | custom-call | tf_op jit(solution)/shard_map/pallas_call | solution.py:325
  37.8 1.7 %collective-permute-start.2 = (bf16[128,512]{1,0:T(8,128)(2,1)S(1)}, bf16[128,512]{1,0:T(8,128)(2,1)S(1)}, u32[]{:S(2)}, u32[]{:S(2)}) collective-permute-start(bf16[128,512]{1,0:T(8,128)(2,1)S(1)} %get-tuple-element.24), channel_id=1, source_target_pairs={{0,1},{1,2},{2,3},{3,4},{4,5},{5,6},{6,7},{7,0},{8,9},{9,10},{10,1... | collective-permute-start | bytes 393224 | tf_op jit(solution)/shard_map/ppermute | solution.py:352
  39.5 4.0 %collective-permute-start.3 = (bf16[128,512]{1,0:T(8,128)(2,1)S(1)}, bf16[128,512]{1,0:T(8,128)(2,1)S(1)}, u32[]{:S(2)}, u32[]{:S(2)}) collective-permute-start(bf16[128,512]{1,0:T(8,128)(2,1)S(1)} %get-tuple-element.25), channel_id=1, source_target_pairs={{0,7},{1,0},{2,1},{3,2},{4,3},{5,4},{6,5},{7,6},{8,15},{9,8},{10,9... | collective-permute-start | bytes 393224 | tf_op jit(solution)/shard_map/ppermute | solution.py:352
  43.6 0.0 slice-done
  43.6 0.0 slice-done.1
  43.6 0.6 shard_map.96
  44.2 0.1 collective-permute-start.5
  44.3 0.5 shard_map.95
  44.7 2.6 %collective-permute-start = (bf16[128,512]{1,0:T(8,128)(2,1)S(1)}, bf16[128,512]{1,0:T(8,128)(2,1)S(1)}, u32[]{:S(2)}, u32[]{:S(2)}) collective-permute-start(bf16[128,512]{1,0:T(8,128)(2,1)S(1)} %get-tuple-element.20), channel_id=1, source_target_pairs={{0,1},{1,2},{2,3},{3,4},{4,5},{5,6},{6,7},{7,0},{8,9},{9,10},{10,1... | collective-permute-start | bytes 393224 | tf_op jit(solution)/shard_map/ppermute | solution.py:352
  47.4 0.1 collective-permute-start.1
  47.5 0.0 collective-permute-done.2.refs_2_
  47.5 0.0 collective-permute-done.3.refs_3_
  47.5 0.1 shard_map.97
  47.6 2.4 %collective-permute-start.4 = (bf16[128,512]{1,0:T(8,128)(2,1)S(1)}, bf16[128,512]{1,0:T(8,128)(2,1)S(1)}, u32[]{:S(2)}, u32[]{:S(2)}) collective-permute-start(bf16[128,512]{1,0:T(8,128)(2,1)S(1)} %shard_map.97), channel_id=1, source_target_pairs={{0,6},{1,3},{2,0},{3,5},{4,2},{5,7},{6,4},{7,1},{8,14},{9,11},{10,... | collective-permute-start | bytes 393224 | tf_op jit(solution)/shard_map/ppermute | solution.py:355
  50.0 1.5 %collective-permute-done.5.refs_4_ = bf16[128,512]{1,0:T(8,128)(2,1)S(1)} collective-permute-done((bf16[128,512]{1,0:T(8,128)(2,1)S(1)}, bf16[128,512]{1,0:T(8,128)(2,1)S(1)}, u32[]{:S(2)}, u32[]{:S(2)}) %collective-permute-start.5) | collective-permute-done | bytes 131104 | tf_op jit(solution)/shard_map/ppermute | solution.py:355
  51.5 0.1 shard_map.98
  51.6 0.1 collective-permute-start.6
  51.7 0.3 shard_map.94.refs_1_
  52.0 2.0 %collective-permute-done.refs_2_ = bf16[128,512]{1,0:T(8,128)(2,1)S(1)} collective-permute-done((bf16[128,512]{1,0:T(8,128)(2,1)S(1)}, bf16[128,512]{1,0:T(8,128)(2,1)S(1)}, u32[]{:S(2)}, u32[]{:S(2)}) %collective-permute-start) | collective-permute-done | bytes 131104 | tf_op jit(solution)/shard_map/ppermute | solution.py:352
  54.0 0.0 collective-permute-done.1.refs_3_
  54.0 2.4 %collective-permute-done.4.refs_4_ = bf16[128,512]{1,0:T(8,128)(2,1)S(1)} collective-permute-done((bf16[128,512]{1,0:T(8,128)(2,1)S(1)}, bf16[128,512]{1,0:T(8,128)(2,1)S(1)}, u32[]{:S(2)}, u32[]{:S(2)}) %collective-permute-start.4) | collective-permute-done | bytes 131104 | tf_op jit(solution)/shard_map/ppermute | solution.py:355
  56.4 1.6 %collective-permute-done.6.refs_5_ = bf16[128,512]{1,0:T(8,128)(2,1)S(1)} collective-permute-done((bf16[128,512]{1,0:T(8,128)(2,1)S(1)}, bf16[128,512]{1,0:T(8,128)(2,1)S(1)}, u32[]{:S(2)}, u32[]{:S(2)}) %collective-permute-start.6) | collective-permute-done | bytes 131104 | tf_op jit(solution)/shard_map/ppermute | solution.py:355
  58.0 0.3 shard_map.99
  58.3 15.5 %all_to_all.17 = bf16[32,8,512]{2,1,0:T(8,128)(2,1)S(1)} all-to-all(bf16[32,8,512]{2,1,0:T(8,128)(2,1)S(1)} %bitcast.17), channel_id=1, replica_groups=mesh['rep'=32,'tp'=8] {'rep'}, dimensions={0} | all-to-all | bytes 524288 | tf_op jit(solution)/shard_map/all_to_all | solution.py:390
  73.7 0.9 %shard_map.100 = bf16[32,4,512]{2,1,0:T(4,128)(2,1)} custom-call(s32[32,128]{1,0:T(8,128)S(1)} %bitcast.20, bf16[256,512]{1,0:T(8,128)(2,1)S(1)} %bitcast.18), custom_call_target="tpu_custom_call" | custom-call | tf_op jit(solution)/shard_map/pallas_call | solution.py:391
  (1 shorter events, 0.0 us)
Async XLA Ops:
  0.0 34.0 %copy-start.1 = (s32[32]{0:T(128)S(1)}, s32[32]{0:T(128)}, u32[]{:S(2)}) copy-start(s32[32]{0:T(128)} %refs_0_.1) | copy-start | bytes 388
  0.0 34.0 %copy-start = (bf16[32,1,256,128]{3,2,1,0:T(8,128)(2,1)S(1)}, bf16[32,1,256,128]{3,2,1,0:T(8,128)(2,1)}, u32[]{:S(2)}) copy-start(bf16[32,1,256,128]{3,2,1,0:T(8,128)(2,1)} %param.9) | copy-start | bytes 6291460
  16.7 26.8 %slice-start = ((s8[8388608]{0:T(1024)(128)(4,1)}), s8[4194304]{0:T(1024)(128)(4,1)S(1)}, s32[]{:S(2)}) async-start(s8[8388608]{0:T(1024)(128)(4,1)} %bitcast.12), calls=%async_computation.3 | async-start | bytes 8388608
  34.0 9.6 %slice-start.1 = ((s8[8388608]{0:T(1024)(128)(4,1)}), s8[4194304]{0:T(1024)(128)(4,1)S(1)}, s32[]{:S(2)}) async-start(s8[8388608]{0:T(1024)(128)(4,1)} %bitcast.12), calls=%async_computation.4 | async-start | bytes 8388608
  37.8 9.7 %collective-permute-start.2 = (bf16[128,512]{1,0:T(8,128)(2,1)S(1)}, bf16[128,512]{1,0:T(8,128)(2,1)S(1)}, u32[]{:S(2)}, u32[]{:S(2)}) collective-permute-start(bf16[128,512]{1,0:T(8,128)(2,1)S(1)} %get-tuple-element.24), channel_id=1, source_target_pairs={{0,1},{1,2},{2,3},{3,4},{4,5},{5,6},{6,7},{7,0},{8,9},{9,10},{10,1... | collective-permute-start | bytes 393224 | tf_op jit(solution)/shard_map/ppermute | solution.py:352
  39.5 8.0 %collective-permute-start.3 = (bf16[128,512]{1,0:T(8,128)(2,1)S(1)}, bf16[128,512]{1,0:T(8,128)(2,1)S(1)}, u32[]{:S(2)}, u32[]{:S(2)}) collective-permute-start(bf16[128,512]{1,0:T(8,128)(2,1)S(1)} %get-tuple-element.25), channel_id=1, source_target_pairs={{0,7},{1,0},{2,1},{3,2},{4,3},{5,4},{6,5},{7,6},{8,15},{9,8},{10,9... | collective-permute-start | bytes 393224 | tf_op jit(solution)/shard_map/ppermute | solution.py:352
  44.2 7.3 %collective-permute-start.5 = (bf16[128,512]{1,0:T(8,128)(2,1)S(1)}, bf16[128,512]{1,0:T(8,128)(2,1)S(1)}, u32[]{:S(2)}, u32[]{:S(2)}) collective-permute-start(bf16[128,512]{1,0:T(8,128)(2,1)S(1)} %get-tuple-element.26), channel_id=1, source_target_pairs={{0,2},{1,7},{2,4},{3,1},{4,6},{5,3},{6,0},{7,5},{8,10},{9,15},{10,... | collective-permute-start | bytes 393224 | tf_op jit(solution)/shard_map/ppermute | solution.py:355
  44.7 9.3 %collective-permute-start = (bf16[128,512]{1,0:T(8,128)(2,1)S(1)}, bf16[128,512]{1,0:T(8,128)(2,1)S(1)}, u32[]{:S(2)}, u32[]{:S(2)}) collective-permute-start(bf16[128,512]{1,0:T(8,128)(2,1)S(1)} %get-tuple-element.20), channel_id=1, source_target_pairs={{0,1},{1,2},{2,3},{3,4},{4,5},{5,6},{6,7},{7,0},{8,9},{9,10},{10,1... | collective-permute-start | bytes 393224 | tf_op jit(solution)/shard_map/ppermute | solution.py:352
  47.4 6.6 %collective-permute-start.1 = (bf16[128,512]{1,0:T(8,128)(2,1)S(1)}, bf16[128,512]{1,0:T(8,128)(2,1)S(1)}, u32[]{:S(2)}, u32[]{:S(2)}) collective-permute-start(bf16[128,512]{1,0:T(8,128)(2,1)S(1)} %get-tuple-element.21), channel_id=1, source_target_pairs={{0,7},{1,0},{2,1},{3,2},{4,3},{5,4},{6,5},{7,6},{8,15},{9,8},{10,9... | collective-permute-start | bytes 393224 | tf_op jit(solution)/shard_map/ppermute | solution.py:352
  47.6 8.8 %collective-permute-start.4 = (bf16[128,512]{1,0:T(8,128)(2,1)S(1)}, bf16[128,512]{1,0:T(8,128)(2,1)S(1)}, u32[]{:S(2)}, u32[]{:S(2)}) collective-permute-start(bf16[128,512]{1,0:T(8,128)(2,1)S(1)} %shard_map.97), channel_id=1, source_target_pairs={{0,6},{1,3},{2,0},{3,5},{4,2},{5,7},{6,4},{7,1},{8,14},{9,11},{10,... | collective-permute-start | bytes 393224 | tf_op jit(solution)/shard_map/ppermute | solution.py:355
  51.6 6.4 %collective-permute-start.6 = (bf16[128,512]{1,0:T(8,128)(2,1)S(1)}, bf16[128,512]{1,0:T(8,128)(2,1)S(1)}, u32[]{:S(2)}, u32[]{:S(2)}) collective-permute-start(bf16[128,512]{1,0:T(8,128)(2,1)S(1)} %shard_map.98), channel_id=1, source_target_pairs={{0,2},{1,7},{2,4},{3,1},{4,6},{5,3},{6,0},{7,5},{8,10},{9,15},{10,... | collective-permute-start | bytes 393224 | tf_op jit(solution)/shard_map/ppermute | solution.py:355

commit v4 on v3

--- a/solution.py
+++ b/solution.py
@@ -8,9 +8,9 @@
 from jax.sharding import PartitionSpec as P
 
 MASKED = -1e30
-FIRST = (3, 5)
-SECOND = (4, 2, 6)
-THIRD = (1, 7)
+FIRST = ((3, 5),)
+SECOND = (4, (6, 2))
+THIRD = ((1, 7),)
 LAST = (0,)
 VMEM_BYTES = 24 * 1024 * 1024
 
@@ -102,27 +102,28 @@
     ).astype(jnp.bfloat16)
 
 
-def column_copies(offsets, weight_hbm, weight, sems):
-    me = lax.axis_index("tp")
-    width = weight.shape[2]
-    groups = weight_hbm.shape[1] // width
-    copies = []
-    for i, offset in enumerate(offsets):
-        start = pl.multiple_of(lax.rem(me + offset, groups) * width, width)
-        copies.append(
-            pltpu.make_async_copy(
-                weight_hbm.at[:, pl.ds(start, width)], weight.at[i], sems.at[i]
-            )
-        )
-    return copies
-
-
-def project(attended, copies, weight, outs):
-    for i, (copy, out_ref) in enumerate(zip(copies, outs)):
-        copy.wait()
-        out_ref[...] = jnp.dot(attended, weight[i], preferred_element_type=jnp.float32).astype(
-            jnp.bfloat16
-        )
+def column_start(offset, groups, width):
+    return pl.multiple_of(lax.rem(lax.axis_index("tp") + offset, groups) * width, width)
+
+
+def flat(chunks):
+    return [offset for chunk in chunks for offset in (chunk if isinstance(chunk, tuple) else [chunk])]
+
+
+def give_out(chunks, products, outs):
+    odd = (lax.axis_index("tp") & 1) == 1
+    products, outs = iter(products), iter(outs)
+    for chunk in chunks:
+        if isinstance(chunk, tuple):
+            one, other = next(products), next(products)
+            next(outs)[...] = jnp.where(odd, one, other)
+            next(outs)[...] = jnp.where(odd, other, one)
+        else:
+            next(outs)[...] = next(products)
+
+
+def project(attended, columns):
+    return jnp.dot(attended, columns, preferred_element_type=jnp.float32).astype(jnp.bfloat16)
 
 
 def attend_kernel(
@@ -134,8 +135,8 @@
     values_hbm,
     weight_hbm,
     out_ref,
-    right_ref,
-    left_ref,
+    outer_ref,
+    inner_ref,
     values,
     weight,
     here,
@@ -149,7 +150,16 @@
 ):
     value_copy = pltpu.make_async_copy(values_hbm, values, value_sem)
     value_copy.start()
-    copies = column_copies(FIRST, weight_hbm, weight, weight_sems)
+    width = outer_ref.shape[1]
+    groups = weight_hbm.shape[1] // width
+    copies = [
+        pltpu.make_async_copy(
+            weight_hbm.at[:, pl.ds(column_start(offset, groups, width), width)],
+            weight.at[i],
+            weight_sems.at[i],
+        )
+        for i, offset in enumerate(flat(FIRST))
+    ]
     for copy in copies:
         copy.start()
     rows, context, head_size = keys.shape
@@ -211,36 +221,32 @@
         for h in range(heads):
             out_ref[lot, h * head_size : (h + 1) * head_size] = result[h * pair : (h + 1) * pair]
 
-    project(out_ref[...], copies, weight, (right_ref, left_ref))
-
-
-def project_kernel(offsets, steps, attended_ref, weight_ref, *outs):
-    me = lax.axis_index("tp")
+    products = []
+    for i, copy in enumerate(copies):
+        copy.wait()
+        products.append(project(out_ref[...], weight[i]))
+    give_out(FIRST, products, (outer_ref, inner_ref))
+
+
+def project_kernel(chunks, steps, attended_ref, weight_ref, *outs):
     width = outs[0].shape[1]
     groups = weight_ref.shape[1] // width
-    for offset, out_ref in zip(offsets, outs):
-        start = pl.multiple_of(lax.rem(me + offset, groups) * width, width)
-        out_ref[...] = jnp.dot(
-            attended_ref[...],
-            weight_ref[:, pl.ds(start, width)],
-            preferred_element_type=jnp.float32,
-        ).astype(jnp.bfloat16)
+    products = [
+        project(attended_ref[...], weight_ref[:, pl.ds(column_start(offset, groups, width), width)])
+        for offset in flat(chunks)
+    ]
+    give_out(chunks, products, outs)
 
 
 def wide(ref):
     return ref[...].astype(jnp.float32)
 
 
-def relay_kernel(steps, right_ref, left_ref, from_left, from_right, *refs):
-    far, out_ref = refs[:-1], refs[-1]
-    even = lax.rem(lax.axis_index("tp"), 2) == 0
-    right = wide(right_ref) + wide(from_left)
-    left = wide(left_ref) + wide(from_right)
-    if far:
-        total = jnp.where(even, right, left) + wide(far[0])
-    else:
-        total = jnp.where(even, left, right)
-    out_ref[...] = total.astype(jnp.bfloat16)
+def relay_kernel(steps, *refs):
+    total = wide(refs[0])
+    for ref in refs[1:-1]:
+        total = total + wide(ref)
+    refs[-1][...] = total.astype(jnp.bfloat16)
 
 
 def merge_kernel(steps, bits_ref, *refs):
@@ -322,14 +328,14 @@
 
     lines = features // head_size * 2 * steps
     chunk = out((tokens, width))
-    attended, to_right, to_left = kernel(
+    attended, outer, inner = kernel(
         attend_kernel,
         (out((tokens, features)), chunk, chunk),
         [smem_spec()] + [vmem_spec()] * 3 + [hbm_spec()] * 2,
         (vmem_spec(),) * 3,
         [
             pltpu.VMEM((rows, context, head_size), bf16),
-            pltpu.VMEM((len(FIRST), features, width), bf16),
+            pltpu.VMEM((len(flat(FIRST)), features, width), bf16),
             pltpu.VMEM((tokens, full), bf16),
             pltpu.VMEM((rows // 2, lines, context), jnp.float32),
             pltpu.VMEM((rows // 2, lines, 2 * steps), jnp.float32),
@@ -337,7 +343,7 @@
             pltpu.VMEM((rows // 2, lines, 2 * steps), bf16),
             pltpu.VMEM((rows // 2, lines, head_size), jnp.float32),
             pltpu.SemaphoreType.DMA(()),
-            pltpu.SemaphoreType.DMA((len(FIRST),)),
+            pltpu.SemaphoreType.DMA((len(flat(FIRST)),)),
         ],
     )(
         cache_lengths,
@@ -348,19 +354,17 @@
         in_hbm(out_weight),
     )
 
-    def shift(block, by):
-        return lax.ppermute(block, "tp", [(i, (i + by) % groups) for i in range(groups)])
-
     def cross(block, by):
         return lax.ppermute(
-            block, "tp", [(i, (i + (-by if i % 2 else by)) % groups) for i in range(groups)]
-        )
-
-    from_left, from_right = shift(to_right, 1), shift(to_left, -1)
-    def projected(offsets):
-        count = len(offsets)
+            block, "tp", [(i, (i + (by if i % 2 else -by)) % groups) for i in range(groups)]
+        )
+
+    outer, inner = cross(outer, 1), cross(inner, -1)
+
+    def projected(chunks):
+        count = len(flat(chunks))
         return kernel(
-            lambda steps, *refs: project_kernel(offsets, steps, *refs),
+            lambda steps, *refs: project_kernel(chunks, steps, *refs),
             (chunk,) * count,
             [vmem_spec()] * 2,
             (vmem_spec(),) * count,
@@ -372,20 +376,18 @@
             ),
         )(attended, out_weight)
 
-    far, next_right, next_left = projected(SECOND)
+    far, first, second = projected(SECOND)
     far = cross(far, 2)
-    near_right, near_left = projected(THIRD)
+    near = [cross(block, by) for block, by in zip(projected(THIRD), (1, -1))]
     (own,) = projected(LAST)
-    inner = (next_right, next_left, from_left, from_right)
-    relay = [
-        kernel(relay_kernel, chunk, [vmem_spec()] * len(blocks))(*blocks)
-        for blocks in (inner, (*inner, far))
-    ]
-    first = cross(relay[0], -2)
-    near_from_left, near_from_right = shift(near_right, 1), shift(near_left, -1)
-    second = cross(relay[1], 2)
+
+    def relay(*blocks):
+        return kernel(relay_kernel, chunk, [vmem_spec()] * len(blocks))(*blocks)
+
+    first = cross(relay(first, outer), -2)
+    second = cross(relay(second, inner, far), 2)
     back = kernel(merge_kernel, out((spots, width)), [vmem_spec()] * 6)(
-        bits, own, near_from_left, near_from_right, first, second
+        bits, own, *near, first, second
     )
     back = lax.all_to_all(back.reshape(replicas, 2 * steps, width), "rep", 0, 0, tiled=True)
     return kernel(unpack_kernel, out((rows, steps, width)), [vmem_spec()] * 2)(

time: 74.8 us -> 74.4 us (level)
  starting transfers between devices: 11.1 us -> 14 us
  waiting for transfers between devices: 7.47 us -> 5.15 us
  blocking collectives: 47.7 us -> 46.7 us
    ppermute x7, starting transfers between devices: 11.1 us -> 14 us  [cross(): lax.ppermute(block, 'tp', [(i, (i + (by if i % 2 else -by)) % groups) for...]
    ppermute x7, waiting for transfers between devices: 7.47 us -> 5.15 us  [cross(): lax.ppermute(block, 'tp', [(i, (i + (by if i % 2 else -by)) % groups) for...]
    all_to_all x1, blocking collectives: 15.5 us -> 14.5 us  [on_device(): lax.all_to_all(back.reshape(replicas, 2 * steps, width), 'rep', 0, 0, til...]
  transfers between devices with their start and end apart: 7 -> 7, of which waited for: 4 -> 2; matrix products, arithmetic and copies ran while one was open for 0% -> 0% of each run, Pallas kernels for 2% -> 2%
where the time goes in v4:
time: 74.4 us; the launch traced here: 74.2 us
  blocking collectives  46.7 us (63%)
  starting transfers between devices  14 us (19%)
  Pallas kernels  8.19 us (11%)
  waiting for transfers between devices  5.15 us (7%)
    all_to_all x1, blocking collectives, on_device(): lax.all_to_all(packed.reshape(replicas, 2 * steps, full), 'rep', 0, 0, ti...  16.9 us
    all_to_all x1, blocking collectives, on_device(): lax.all_to_all(wire.reshape(replicas, 1, tokens), 'rep', 0, 0, tiled=True)  15.3 us
    all_to_all x1, blocking collectives, on_device(): lax.all_to_all(back.reshape(replicas, 2 * steps, width), 'rep', 0, 0, til...  14.5 us
    ppermute x7, starting transfers between devices, cross(): lax.ppermute(block, 'tp', [(i, (i + (by if i % 2 else -by)) % groups) for...  14 us
    ppermute x7, waiting for transfers between devices, cross(): lax.ppermute(block, 'tp', [(i, (i + (by if i % 2 else -by)) % groups) for...  5.15 us
    pallas_call x1, Pallas kernels, on_device(): kernel(attend_kernel, (out((tokens, features)), chunk, chunk), [smem_spec...  3.86 us
  transfers between devices with their start and end apart: 7, of which 2 were waited for; matrix products, arithmetic and copies ran while one was open for 0% of the time, Pallas kernels for 2%

profile of v4, /device:TPU:1, one launch (start us, length us, event | category | flops | bytes accessed | tf_op | source)
XLA Modules:
  0.0 74.2 jit_solution(17334366346706717071)
XLA Ops:
  0.0 0.0 copy-start.1
  0.0 0.0 copy-start
  0.0 1.4 %shard_map.91 = (s32[32,128]{1,0:T(8,128)S(1)}, s32[32,128]{1,0:T(8,128)S(1)}, bf16[128,1280]{1,0:T(8,128)(2,1)S(1)}) custom-call(s32[1,32]{1,0:T(1,128)} %bitcast.23, s32[1,32]{1,0:T(1,128)} %bitcast.24, bf16[32,4,1024]{2,1,0:T(4,128)(2,1)} %refs_2_.1, bf16[32,4,128]{2,1,0:T(4,128)(2,1)} %refs_3_.1, bf16[32,4,128]{2,1,0:T(4,128)(2,1)} %refs_4_.1), custom_call_target="tpu_custom_call" | custom-call | tf_op jit(solution)/shard_map/pallas_call | solution.py:311
  1.4 15.3 %all_to_all.15 = s32[32,1,128]{2,1,0:T(1,128)S(1)} all-to-all(s32[32,1,128]{2,1,0:T(1,128)S(1)} %bitcast.21), channel_id=1, replica_groups=mesh['rep'=32,'tp'=8] {'rep'}, dimensions={0} | all-to-all | bytes 32768 | tf_op jit(solution)/shard_map/all_to_all | solution.py:323
  16.7 0.0 slice-start
  16.7 0.3 shard_map.92
  17.0 16.9 %all_to_all.16 = bf16[32,8,1280]{2,1,0:T(8,128)(2,1)S(1)} all-to-all(bf16[32,8,1280]{2,1,0:T(8,128)(2,1)S(1)} %bitcast.15), channel_id=1, replica_groups=mesh['rep'=32,'tp'=8] {'rep'}, dimensions={0} | all-to-all | bytes 1310720 | tf_op jit(solution)/shard_map/all_to_all | solution.py:327
  34.0 0.0 copy-done.1
  34.0 0.0 copy-done
  34.0 0.0 slice-start.1
  34.0 3.9 %shard_map.93 = (bf16[128,1024]{1,0:T(8,128)(2,1)S(1)}, bf16[128,512]{1,0:T(8,128)(2,1)S(1)}, bf16[128,512]{1,0:T(8,128)(2,1)S(1)}) custom-call(s32[32]{0:T(128)S(1)} %copy-done.1, s32[32,128]{1,0:T(8,128)S(1)} %get-tuple-element.17.refs_1_.refs_0_, bf16[256,1280]{1,0:T(8,128)(2,1)S(1)} %bitcast.14, bf16[32,256,128]{2,1,0:T(8,128)(2,1)S(1)} %bitcast.16, ...), custom_call_target="tpu_custom_call" | custom-call | tf_op jit(solution)/shard_map/pallas_call | solution.py:331
  37.8 5.7 %collective-permute-start.2 = (bf16[128,512]{1,0:T(8,128)(2,1)S(1)}, bf16[128,512]{1,0:T(8,128)(2,1)S(1)}, u32[]{:S(2)}, u32[]{:S(2)}) collective-permute-start(bf16[128,512]{1,0:T(8,128)(2,1)S(1)} %get-tuple-element.23), channel_id=1, source_target_pairs={{0,7},{1,2},{2,1},{3,4},{4,3},{5,6},{6,5},{7,0},{8,15},{9,10},{10,... | collective-permute-start | bytes 393224 | tf_op jit(solution)/shard_map/ppermute | solution.py:358
  43.5 0.0 collective-permute-start.4
  43.5 0.0 slice-done
  43.5 0.0 slice-done.1
  43.5 0.6 shard_map.96
  44.1 1.4 %collective-permute-start.5 = (bf16[128,512]{1,0:T(8,128)(2,1)S(1)}, bf16[128,512]{1,0:T(8,128)(2,1)S(1)}, u32[]{:S(2)}, u32[]{:S(2)}) collective-permute-start(bf16[128,512]{1,0:T(8,128)(2,1)S(1)} %get-tuple-element.26), channel_id=1, source_target_pairs={{0,6},{1,3},{2,0},{3,5},{4,2},{5,7},{6,4},{7,1},{8,14},{9,11},{10,... | collective-permute-start | bytes 393224 | tf_op jit(solution)/shard_map/ppermute | solution.py:358
  45.5 0.5 shard_map.95
  46.0 2.7 %collective-permute-start = (bf16[128,512]{1,0:T(8,128)(2,1)S(1)}, bf16[128,512]{1,0:T(8,128)(2,1)S(1)}, u32[]{:S(2)}, u32[]{:S(2)}) collective-permute-start(bf16[128,512]{1,0:T(8,128)(2,1)S(1)} %get-tuple-element.20), channel_id=1, source_target_pairs={{0,7},{1,2},{2,1},{3,4},{4,3},{5,6},{6,5},{7,0},{8,15},{9,10},{10,... | collective-permute-start | bytes 393224 | tf_op jit(solution)/shard_map/ppermute | solution.py:358
  48.6 0.0 collective-permute-start.1
  48.6 0.0 collective-permute-done.2.refs_1_
  48.7 2.0 %collective-permute-start.3 = (bf16[128,512]{1,0:T(8,128)(2,1)S(1)}, bf16[128,512]{1,0:T(8,128)(2,1)S(1)}, u32[]{:S(2)}, u32[]{:S(2)}) collective-permute-start(bf16[128,512]{1,0:T(8,128)(2,1)S(1)} %shard_map.97), channel_id=1, source_target_pairs={{0,2},{1,7},{2,4},{3,1},{4,6},{5,3},{6,0},{7,5},{8,10},{9,15},{10,... | collective-permute-start | bytes 393224 | tf_op jit(solution)/shard_map/ppermute | solution.py:358
  50.6 0.7 collective-permute-done.4.refs_1_
  51.4 0.0 collective-permute-done.5.refs_2_
  51.4 0.1 shard_map.98
  51.4 2.4 %collective-permute-start.6 = (bf16[128,512]{1,0:T(8,128)(2,1)S(1)}, bf16[128,512]{1,0:T(8,128)(2,1)S(1)}, u32[]{:S(2)}, u32[]{:S(2)}) collective-permute-start(bf16[128,512]{1,0:T(8,128)(2,1)S(1)} %shard_map.98), channel_id=1, source_target_pairs={{0,6},{1,3},{2,0},{3,5},{4,2},{5,7},{6,4},{7,1},{8,14},{9,11},{10,... | collective-permute-start | bytes 393224 | tf_op jit(solution)/shard_map/ppermute | solution.py:358
  53.8 0.3 shard_map.94.refs_1_
  54.1 0.0 collective-permute-done.refs_2_
  54.2 0.0 collective-permute-done.1.refs_3_
  54.2 4.4 %collective-permute-done.3.refs_4_ = bf16[128,512]{1,0:T(8,128)(2,1)S(1)} collective-permute-done((bf16[128,512]{1,0:T(8,128)(2,1)S(1)}, bf16[128,512]{1,0:T(8,128)(2,1)S(1)}, u32[]{:S(2)}, u32[]{:S(2)}) %collective-permute-start.3) | collective-permute-done | bytes 131104 | tf_op jit(solution)/shard_map/ppermute | solution.py:358
  58.5 0.0 collective-permute-done.6.refs_5_
  58.5 0.3 shard_map.99
  58.8 14.5 %all_to_all.17 = bf16[32,8,512]{2,1,0:T(8,128)(2,1)S(1)} all-to-all(bf16[32,8,512]{2,1,0:T(8,128)(2,1)S(1)} %bitcast.17), channel_id=1, replica_groups=mesh['rep'=32,'tp'=8] {'rep'}, dimensions={0} | all-to-all | bytes 524288 | tf_op jit(solution)/shard_map/all_to_all | solution.py:392
  73.3 0.9 %shard_map.100 = bf16[32,4,512]{2,1,0:T(4,128)(2,1)} custom-call(s32[32,128]{1,0:T(8,128)S(1)} %bitcast.20, bf16[256,512]{1,0:T(8,128)(2,1)S(1)} %bitcast.18), custom_call_target="tpu_custom_call" | custom-call | tf_op jit(solution)/shard_map/pallas_call | solution.py:393
  (2 shorter events, 0.0 us)
Async XLA Ops:
  0.0 34.0 %copy-start.1 = (s32[32]{0:T(128)S(1)}, s32[32]{0:T(128)}, u32[]{:S(2)}) copy-start(s32[32]{0:T(128)} %refs_0_.1) | copy-start | bytes 388
  0.0 34.0 %copy-start = (bf16[32,1,256,128]{3,2,1,0:T(8,128)(2,1)S(1)}, bf16[32,1,256,128]{3,2,1,0:T(8,128)(2,1)}, u32[]{:S(2)}) copy-start(bf16[32,1,256,128]{3,2,1,0:T(8,128)(2,1)} %param.9) | copy-start | bytes 6291460
  16.7 26.8 %slice-start = ((s8[8388608]{0:T(1024)(128)(4,1)}), s8[4194304]{0:T(1024)(128)(4,1)S(1)}, s32[]{:S(2)}) async-start(s8[8388608]{0:T(1024)(128)(4,1)} %bitcast.12), calls=%async_computation.3 | async-start | bytes 8388608
  34.0 9.5 %slice-start.1 = ((s8[8388608]{0:T(1024)(128)(4,1)}), s8[4194304]{0:T(1024)(128)(4,1)S(1)}, s32[]{:S(2)}) async-start(s8[8388608]{0:T(1024)(128)(4,1)} %bitcast.12), calls=%async_computation.4 | async-start | bytes 8388608
  37.8 10.8 %collective-permute-start.2 = (bf16[128,512]{1,0:T(8,128)(2,1)S(1)}, bf16[128,512]{1,0:T(8,128)(2,1)S(1)}, u32[]{:S(2)}, u32[]{:S(2)}) collective-permute-start(bf16[128,512]{1,0:T(8,128)(2,1)S(1)} %get-tuple-element.23), channel_id=1, source_target_pairs={{0,7},{1,2},{2,1},{3,4},{4,3},{5,6},{6,5},{7,0},{8,15},{9,10},{10,... | collective-permute-start | bytes 393224 | tf_op jit(solution)/shard_map/ppermute | solution.py:358
  43.5 7.9 %collective-permute-start.4 = (bf16[128,512]{1,0:T(8,128)(2,1)S(1)}, bf16[128,512]{1,0:T(8,128)(2,1)S(1)}, u32[]{:S(2)}, u32[]{:S(2)}) collective-permute-start(bf16[128,512]{1,0:T(8,128)(2,1)S(1)} %get-tuple-element.25), channel_id=1, source_target_pairs={{0,1},{1,0},{2,3},{3,2},{4,5},{5,4},{6,7},{7,6},{8,9},{9,8},{10,11... | collective-permute-start | bytes 393224 | tf_op jit(solution)/shard_map/ppermute | solution.py:358
  44.1 7.2 %collective-permute-start.5 = (bf16[128,512]{1,0:T(8,128)(2,1)S(1)}, bf16[128,512]{1,0:T(8,128)(2,1)S(1)}, u32[]{:S(2)}, u32[]{:S(2)}) collective-permute-start(bf16[128,512]{1,0:T(8,128)(2,1)S(1)} %get-tuple-element.26), channel_id=1, source_target_pairs={{0,6},{1,3},{2,0},{3,5},{4,2},{5,7},{6,4},{7,1},{8,14},{9,11},{10,... | collective-permute-start | bytes 393224 | tf_op jit(solution)/shard_map/ppermute | solution.py:358
  46.0 8.2 %collective-permute-start = (bf16[128,512]{1,0:T(8,128)(2,1)S(1)}, bf16[128,512]{1,0:T(8,128)(2,1)S(1)}, u32[]{:S(2)}, u32[]{:S(2)}) collective-permute-start(bf16[128,512]{1,0:T(8,128)(2,1)S(1)} %get-tuple-element.20), channel_id=1, source_target_pairs={{0,7},{1,2},{2,1},{3,4},{4,3},{5,6},{6,5},{7,0},{8,15},{9,10},{10,... | collective-permute-start | bytes 393224 | tf_op jit(solution)/shard_map/ppermute | solution.py:358
  48.6 5.5 %collective-permute-start.1 = (bf16[128,512]{1,0:T(8,128)(2,1)S(1)}, bf16[128,512]{1,0:T(8,128)(2,1)S(1)}, u32[]{:S(2)}, u32[]{:S(2)}) collective-permute-start(bf16[128,512]{1,0:T(8,128)(2,1)S(1)} %get-tuple-element.21), channel_id=1, source_target_pairs={{0,1},{1,0},{2,3},{3,2},{4,5},{5,4},{6,7},{7,6},{8,9},{9,8},{10,11... | collective-permute-start | bytes 393224 | tf_op jit(solution)/shard_map/ppermute | solution.py:358
  48.7 9.9 %collective-permute-start.3 = (bf16[128,512]{1,0:T(8,128)(2,1)S(1)}, bf16[128,512]{1,0:T(8,128)(2,1)S(1)}, u32[]{:S(2)}, u32[]{:S(2)}) collective-permute-start(bf16[128,512]{1,0:T(8,128)(2,1)S(1)} %shard_map.97), channel_id=1, source_target_pairs={{0,2},{1,7},{2,4},{3,1},{4,6},{5,3},{6,0},{7,5},{8,10},{9,15},{10,... | collective-permute-start | bytes 393224 | tf_op jit(solution)/shard_map/ppermute | solution.py:358
  51.4 7.1 %collective-permute-start.6 = (bf16[128,512]{1,0:T(8,128)(2,1)S(1)}, bf16[128,512]{1,0:T(8,128)(2,1)S(1)}, u32[]{:S(2)}, u32[]{:S(2)}) collective-permute-start(bf16[128,512]{1,0:T(8,128)(2,1)S(1)} %shard_map.98), channel_id=1, source_target_pairs={{0,6},{1,3},{2,0},{3,5},{4,2},{5,7},{6,4},{7,1},{8,14},{9,11},{10,... | collective-permute-start | bytes 393224 | tf_op jit(solution)/shard_map/ppermute | solution.py:358

commit v5 on v4

--- a/solution.py
+++ b/solution.py
@@ -58,29 +58,19 @@
         copy.start()
     replicas, tokens = wire_ref.shape
     rows = tokens // steps
-    shape = (replicas, tokens)
-    spread = lax.broadcasted_iota(jnp.int32, (rows, tokens), 1) // steps
-    spread = spread == lax.broadcasted_iota(jnp.int32, (rows, tokens), 0)
-    spread = spread.astype(jnp.float32).astype(jnp.bfloat16)
+    shift = rows.bit_length()
+    replica = lax.broadcasted_iota(jnp.int32, (replicas, rows), 0)
+    order = lax.broadcasted_iota(jnp.int32, (replicas, rows), 1) << shift
+    row = lax.broadcasted_iota(jnp.int32, (replicas, tokens), 1) // steps
     for copy in copies[:2]:
         copy.wait()
-    both = jnp.where(
-        lax.broadcasted_iota(jnp.int32, (8, rows), 0) == 0, target_ref[...], slot_ref[...]
-    )
-    both = jnp.dot(
-        both.astype(jnp.float32).astype(jnp.bfloat16), spread, preferred_element_type=jnp.float32
-    ).astype(jnp.int32)
-    replica = lax.broadcasted_iota(jnp.int32, shape, 0)
-    row = lax.broadcasted_iota(jnp.int32, shape, 1) // steps
-    mine = both[0:1] == replica
-    first = jnp.min(jnp.where(mine, row, tokens), axis=1, keepdims=True)
-    early = mine & (row == first)
-    late = mine & (row != first)
-    slots = jnp.broadcast_to(both[1:2], shape)
-    early_slot = jnp.max(jnp.where(early, slots, -1), axis=1, keepdims=True)
-    late_slot = jnp.max(jnp.where(late, slots, -1), axis=1, keepdims=True)
-    bits_ref[...] = jnp.where(early, 1, 0) + jnp.where(late, 2, 0)
-    wire_ref[...] = jnp.where(row == early_slot, 1, 0) + jnp.where(row == late_slot, 2, 0)
+    mine = target_ref[...] == replica
+    key = order + slot_ref[...]
+    early = jnp.min(jnp.where(mine, key, (1 << 24) - 1), axis=1, keepdims=True)
+    late = jnp.max(jnp.where(mine, key, -1), axis=1, keepdims=True)
+    low = (1 << shift) - 1
+    wire_ref[...] = jnp.where(row == (early & low), 1, 0) + jnp.where(row == (late & low), 2, 0)
+    bits_ref[...] = jnp.where(row == (early >> shift), 1, 0) + jnp.where(row == (late >> shift), 2, 0)
     at = 0
     for copy, block in zip(copies[2:], blocks):
         copy.wait()

time: 74.4 us -> 74.3 us (level)
  no operation moved by 1% of the time
where the time goes in v5:
time: 74.3 us; the launch traced here: 74.1 us
  blocking collectives  46.7 us (63%)
  starting transfers between devices  14 us (19%)
  Pallas kernels  8.06 us (11%)
  waiting for transfers between devices  5.13 us (7%)
    all_to_all x1, blocking collectives, on_device(): lax.all_to_all(packed.reshape(replicas, 2 * steps, full), 'rep', 0, 0, ti...  16.9 us
    all_to_all x1, blocking collectives, on_device(): lax.all_to_all(wire.reshape(replicas, 1, tokens), 'rep', 0, 0, tiled=True)  15.3 us
    all_to_all x1, blocking collectives, on_device(): lax.all_to_all(back.reshape(replicas, 2 * steps, width), 'rep', 0, 0, til...  14.5 us
    ppermute x7, starting transfers between devices, cross(): lax.ppermute(block, 'tp', [(i, (i + (by if i % 2 else -by)) % groups) for...  14 us
    ppermute x7, waiting for transfers between devices, cross(): lax.ppermute(block, 'tp', [(i, (i + (by if i % 2 else -by)) % groups) for...  5.13 us
    pallas_call x1, Pallas kernels, on_device(): kernel(attend_kernel, (out((tokens, features)), chunk, chunk), [smem_spec...  3.86 us
  transfers between devices with their start and end apart: 7, of which 2 were waited for; matrix products, arithmetic and copies ran while one was open for 0% of the time, Pallas kernels for 2%

profile of v5, /device:TPU:1, one launch (start us, length us, event | category | flops | bytes accessed | tf_op | source)
XLA Modules:
  0.0 74.1 jit_solution(16168889034335111003)
XLA Ops:
  0.0 0.0 copy-start.1
  0.0 0.0 copy-start
  0.0 1.2 %shard_map.91 = (s32[32,128]{1,0:T(8,128)S(1)}, s32[32,128]{1,0:T(8,128)S(1)}, bf16[128,1280]{1,0:T(8,128)(2,1)S(1)}) custom-call(s32[1,32]{1,0:T(1,128)} %bitcast.23, s32[1,32]{1,0:T(1,128)} %bitcast.24, bf16[32,4,1024]{2,1,0:T(4,128)(2,1)} %refs_2_.1, bf16[32,4,128]{2,1,0:T(4,128)(2,1)} %refs_3_.1, bf16[32,4,128]{2,1,0:T(4,128)(2,1)} %refs_4_.1), custom_call_target="tpu_custom_call" | custom-call | tf_op jit(solution)/shard_map/pallas_call | solution.py:301
  1.2 15.3 %all_to_all.15 = s32[32,1,128]{2,1,0:T(1,128)S(1)} all-to-all(s32[32,1,128]{2,1,0:T(1,128)S(1)} %bitcast.21), channel_id=1, replica_groups=mesh['rep'=32,'tp'=8] {'rep'}, dimensions={0} | all-to-all | bytes 32768 | tf_op jit(solution)/shard_map/all_to_all | solution.py:313
  16.6 0.0 slice-start
  16.6 0.3 shard_map.92
  16.9 16.9 %all_to_all.16 = bf16[32,8,1280]{2,1,0:T(8,128)(2,1)S(1)} all-to-all(bf16[32,8,1280]{2,1,0:T(8,128)(2,1)S(1)} %bitcast.15), channel_id=1, replica_groups=mesh['rep'=32,'tp'=8] {'rep'}, dimensions={0} | all-to-all | bytes 1310720 | tf_op jit(solution)/shard_map/all_to_all | solution.py:317
  33.8 0.0 copy-done.1
  33.8 0.0 copy-done
  33.8 0.0 slice-start.1
  33.8 3.9 %shard_map.93 = (bf16[128,1024]{1,0:T(8,128)(2,1)S(1)}, bf16[128,512]{1,0:T(8,128)(2,1)S(1)}, bf16[128,512]{1,0:T(8,128)(2,1)S(1)}) custom-call(s32[32]{0:T(128)S(1)} %copy-done.1, s32[32,128]{1,0:T(8,128)S(1)} %get-tuple-element.17.refs_1_.refs_0_, bf16[256,1280]{1,0:T(8,128)(2,1)S(1)} %bitcast.14, bf16[32,256,128]{2,1,0:T(8,128)(2,1)S(1)} %bitcast.16, ...), custom_call_target="tpu_custom_call" | custom-call | tf_op jit(solution)/shard_map/pallas_call | solution.py:321
  37.7 5.7 %collective-permute-start.2 = (bf16[128,512]{1,0:T(8,128)(2,1)S(1)}, bf16[128,512]{1,0:T(8,128)(2,1)S(1)}, u32[]{:S(2)}, u32[]{:S(2)}) collective-permute-start(bf16[128,512]{1,0:T(8,128)(2,1)S(1)} %get-tuple-element.23), channel_id=1, source_target_pairs={{0,7},{1,2},{2,1},{3,4},{4,3},{5,6},{6,5},{7,0},{8,15},{9,10},{10,... | collective-permute-start | bytes 393224 | tf_op jit(solution)/shard_map/ppermute | solution.py:348
  43.3 0.0 collective-permute-start.4
  43.4 0.0 slice-done
  43.4 0.0 slice-done.1
  43.4 0.6 shard_map.96
  44.0 1.4 %collective-permute-start.5 = (bf16[128,512]{1,0:T(8,128)(2,1)S(1)}, bf16[128,512]{1,0:T(8,128)(2,1)S(1)}, u32[]{:S(2)}, u32[]{:S(2)}) collective-permute-start(bf16[128,512]{1,0:T(8,128)(2,1)S(1)} %get-tuple-element.26), channel_id=1, source_target_pairs={{0,6},{1,3},{2,0},{3,5},{4,2},{5,7},{6,4},{7,1},{8,14},{9,11},{10,... | collective-permute-start | bytes 393224 | tf_op jit(solution)/shard_map/ppermute | solution.py:348
  45.3 0.5 shard_map.95
  45.8 2.7 %collective-permute-start = (bf16[128,512]{1,0:T(8,128)(2,1)S(1)}, bf16[128,512]{1,0:T(8,128)(2,1)S(1)}, u32[]{:S(2)}, u32[]{:S(2)}) collective-permute-start(bf16[128,512]{1,0:T(8,128)(2,1)S(1)} %get-tuple-element.20), channel_id=1, source_target_pairs={{0,7},{1,2},{2,1},{3,4},{4,3},{5,6},{6,5},{7,0},{8,15},{9,10},{10,... | collective-permute-start | bytes 393224 | tf_op jit(solution)/shard_map/ppermute | solution.py:348
  48.5 0.0 collective-permute-start.1
  48.5 0.0 collective-permute-done.2.refs_1_
  48.5 2.0 %collective-permute-start.3 = (bf16[128,512]{1,0:T(8,128)(2,1)S(1)}, bf16[128,512]{1,0:T(8,128)(2,1)S(1)}, u32[]{:S(2)}, u32[]{:S(2)}) collective-permute-start(bf16[128,512]{1,0:T(8,128)(2,1)S(1)} %shard_map.97), channel_id=1, source_target_pairs={{0,2},{1,7},{2,4},{3,1},{4,6},{5,3},{6,0},{7,5},{8,10},{9,15},{10,... | collective-permute-start | bytes 393224 | tf_op jit(solution)/shard_map/ppermute | solution.py:348
  50.5 0.7 collective-permute-done.4.refs_1_
  51.2 0.0 collective-permute-done.5.refs_2_
  51.2 0.1 shard_map.98
  51.3 2.4 %collective-permute-start.6 = (bf16[128,512]{1,0:T(8,128)(2,1)S(1)}, bf16[128,512]{1,0:T(8,128)(2,1)S(1)}, u32[]{:S(2)}, u32[]{:S(2)}) collective-permute-start(bf16[128,512]{1,0:T(8,128)(2,1)S(1)} %shard_map.98), channel_id=1, source_target_pairs={{0,6},{1,3},{2,0},{3,5},{4,2},{5,7},{6,4},{7,1},{8,14},{9,11},{10,... | collective-permute-start | bytes 393224 | tf_op jit(solution)/shard_map/ppermute | solution.py:348
  53.7 0.3 shard_map.94.refs_1_
  54.0 0.0 collective-permute-done.refs_2_
  54.0 0.0 collective-permute-done.1.refs_3_
  54.0 4.4 %collective-permute-done.3.refs_4_ = bf16[128,512]{1,0:T(8,128)(2,1)S(1)} collective-permute-done((bf16[128,512]{1,0:T(8,128)(2,1)S(1)}, bf16[128,512]{1,0:T(8,128)(2,1)S(1)}, u32[]{:S(2)}, u32[]{:S(2)}) %collective-permute-start.3) | collective-permute-done | bytes 131104 | tf_op jit(solution)/shard_map/ppermute | solution.py:348
  58.4 0.0 collective-permute-done.6.refs_5_
  58.4 0.3 shard_map.99
  58.7 14.5 %all_to_all.17 = bf16[32,8,512]{2,1,0:T(8,128)(2,1)S(1)} all-to-all(bf16[32,8,512]{2,1,0:T(8,128)(2,1)S(1)} %bitcast.17), channel_id=1, replica_groups=mesh['rep'=32,'tp'=8] {'rep'}, dimensions={0} | all-to-all | bytes 524288 | tf_op jit(solution)/shard_map/all_to_all | solution.py:382
  73.2 0.9 %shard_map.100 = bf16[32,4,512]{2,1,0:T(4,128)(2,1)} custom-call(s32[32,128]{1,0:T(8,128)S(1)} %bitcast.20, bf16[256,512]{1,0:T(8,128)(2,1)S(1)} %bitcast.18), custom_call_target="tpu_custom_call" | custom-call | tf_op jit(solution)/shard_map/pallas_call | solution.py:383
  (2 shorter events, 0.0 us)
Async XLA Ops:
  0.0 33.8 %copy-start.1 = (s32[32]{0:T(128)S(1)}, s32[32]{0:T(128)}, u32[]{:S(2)}) copy-start(s32[32]{0:T(128)} %refs_0_.1) | copy-start | bytes 388
  0.0 33.8 %copy-start = (bf16[32,1,256,128]{3,2,1,0:T(8,128)(2,1)S(1)}, bf16[32,1,256,128]{3,2,1,0:T(8,128)(2,1)}, u32[]{:S(2)}) copy-start(bf16[32,1,256,128]{3,2,1,0:T(8,128)(2,1)} %param.9) | copy-start | bytes 6291460
  16.6 26.8 %slice-start = ((s8[8388608]{0:T(1024)(128)(4,1)}), s8[4194304]{0:T(1024)(128)(4,1)S(1)}, s32[]{:S(2)}) async-start(s8[8388608]{0:T(1024)(128)(4,1)} %bitcast.12), calls=%async_computation.3 | async-start | bytes 8388608
  33.8 9.5 %slice-start.1 = ((s8[8388608]{0:T(1024)(128)(4,1)}), s8[4194304]{0:T(1024)(128)(4,1)S(1)}, s32[]{:S(2)}) async-start(s8[8388608]{0:T(1024)(128)(4,1)} %bitcast.12), calls=%async_computation.4 | async-start | bytes 8388608
  37.7 10.8 %collective-permute-start.2 = (bf16[128,512]{1,0:T(8,128)(2,1)S(1)}, bf16[128,512]{1,0:T(8,128)(2,1)S(1)}, u32[]{:S(2)}, u32[]{:S(2)}) collective-permute-start(bf16[128,512]{1,0:T(8,128)(2,1)S(1)} %get-tuple-element.23), channel_id=1, source_target_pairs={{0,7},{1,2},{2,1},{3,4},{4,3},{5,6},{6,5},{7,0},{8,15},{9,10},{10,... | collective-permute-start | bytes 393224 | tf_op jit(solution)/shard_map/ppermute | solution.py:348
  43.3 7.9 %collective-permute-start.4 = (bf16[128,512]{1,0:T(8,128)(2,1)S(1)}, bf16[128,512]{1,0:T(8,128)(2,1)S(1)}, u32[]{:S(2)}, u32[]{:S(2)}) collective-permute-start(bf16[128,512]{1,0:T(8,128)(2,1)S(1)} %get-tuple-element.25), channel_id=1, source_target_pairs={{0,1},{1,0},{2,3},{3,2},{4,5},{5,4},{6,7},{7,6},{8,9},{9,8},{10,11... | collective-permute-start | bytes 393224 | tf_op jit(solution)/shard_map/ppermute | solution.py:348
  44.0 7.2 %collective-permute-start.5 = (bf16[128,512]{1,0:T(8,128)(2,1)S(1)}, bf16[128,512]{1,0:T(8,128)(2,1)S(1)}, u32[]{:S(2)}, u32[]{:S(2)}) collective-permute-start(bf16[128,512]{1,0:T(8,128)(2,1)S(1)} %get-tuple-element.26), channel_id=1, source_target_pairs={{0,6},{1,3},{2,0},{3,5},{4,2},{5,7},{6,4},{7,1},{8,14},{9,11},{10,... | collective-permute-start | bytes 393224 | tf_op jit(solution)/shard_map/ppermute | solution.py:348
  45.8 8.2 %collective-permute-start = (bf16[128,512]{1,0:T(8,128)(2,1)S(1)}, bf16[128,512]{1,0:T(8,128)(2,1)S(1)}, u32[]{:S(2)}, u32[]{:S(2)}) collective-permute-start(bf16[128,512]{1,0:T(8,128)(2,1)S(1)} %get-tuple-element.20), channel_id=1, source_target_pairs={{0,7},{1,2},{2,1},{3,4},{4,3},{5,6},{6,5},{7,0},{8,15},{9,10},{10,... | collective-permute-start | bytes 393224 | tf_op jit(solution)/shard_map/ppermute | solution.py:348
  48.5 5.5 %collective-permute-start.1 = (bf16[128,512]{1,0:T(8,128)(2,1)S(1)}, bf16[128,512]{1,0:T(8,128)(2,1)S(1)}, u32[]{:S(2)}, u32[]{:S(2)}) collective-permute-start(bf16[128,512]{1,0:T(8,128)(2,1)S(1)} %get-tuple-element.21), channel_id=1, source_target_pairs={{0,1},{1,0},{2,3},{3,2},{4,5},{5,4},{6,7},{7,6},{8,9},{9,8},{10,11... | collective-permute-start | bytes 393224 | tf_op jit(solution)/shard_map/ppermute | solution.py:348
  48.5 9.9 %collective-permute-start.3 = (bf16[128,512]{1,0:T(8,128)(2,1)S(1)}, bf16[128,512]{1,0:T(8,128)(2,1)S(1)}, u32[]{:S(2)}, u32[]{:S(2)}) collective-permute-start(bf16[128,512]{1,0:T(8,128)(2,1)S(1)} %shard_map.97), channel_id=1, source_target_pairs={{0,2},{1,7},{2,4},{3,1},{4,6},{5,3},{6,0},{7,5},{8,10},{9,15},{10,... | collective-permute-start | bytes 393224 | tf_op jit(solution)/shard_map/ppermute | solution.py:348
  51.3 7.1 %collective-permute-start.6 = (bf16[128,512]{1,0:T(8,128)(2,1)S(1)}, bf16[128,512]{1,0:T(8,128)(2,1)S(1)}, u32[]{:S(2)}, u32[]{:S(2)}) collective-permute-start(bf16[128,512]{1,0:T(8,128)(2,1)S(1)} %shard_map.98), channel_id=1, source_target_pairs={{0,6},{1,3},{2,0},{3,5},{4,2},{5,7},{6,4},{7,1},{8,14},{9,11},{10,... | collective-permute-start | bytes 393224 | tf_op jit(solution)/shard_map/ppermute | solution.py:348

commit v6 on v5

--- a/solution.py
+++ b/solution.py
@@ -9,8 +9,7 @@
 
 MASKED = -1e30
 FIRST = ((3, 5),)
-SECOND = (4, (6, 2))
-THIRD = ((1, 7),)
+SECOND = (4, (6, 2), (1, 7))
 LAST = (0,)
 VMEM_BYTES = 24 * 1024 * 1024
 
@@ -366,9 +365,9 @@
             ),
         )(attended, out_weight)
 
-    far, first, second = projected(SECOND)
+    far, first, second, *near = projected(SECOND)
     far = cross(far, 2)
-    near = [cross(block, by) for block, by in zip(projected(THIRD), (1, -1))]
+    near = [cross(block, by) for block, by in zip(near, (1, -1))]
     (own,) = projected(LAST)
 
     def relay(*blocks):

time: 74.3 us -> 74.6 us (level)
  transfers between devices with their start and end apart: 7 -> 7, of which waited for: 2 -> 3; matrix products, arithmetic and copies ran while one was open for 0% -> 0% of each run, Pallas kernels for 2% -> 2%
where the time goes in v6:
time: 74.6 us; the launch traced here: 74.4 us
  blocking collectives  47 us (63%)
  starting transfers between devices  14.1 us (19%)
  Pallas kernels  7.88 us (11%)
  waiting for transfers between devices  5.33 us (7%)
    all_to_all x1, blocking collectives, on_device(): lax.all_to_all(packed.reshape(replicas, 2 * steps, full), 'rep', 0, 0, ti...  16.9 us
    all_to_all x1, blocking collectives, on_device(): lax.all_to_all(wire.reshape(replicas, 1, tokens), 'rep', 0, 0, tiled=True)  15.3 us
    all_to_all x1, blocking collectives, on_device(): lax.all_to_all(back.reshape(replicas, 2 * steps, width), 'rep', 0, 0, til...  14.8 us
    ppermute x7, starting transfers between devices, cross(): lax.ppermute(block, 'tp', [(i, (i + (by if i % 2 else -by)) % groups) for...  14.1 us
    ppermute x7, waiting for transfers between devices, cross(): lax.ppermute(block, 'tp', [(i, (i + (by if i % 2 else -by)) % groups) for...  5.33 us
    pallas_call x1, Pallas kernels, on_device(): kernel(attend_kernel, (out((tokens, features)), chunk, chunk), [smem_spec...  3.86 us
  transfers between devices with their start and end apart: 7, of which 3 were waited for; matrix products, arithmetic and copies ran while one was open for 0% of the time, Pallas kernels for 2%

profile of v6, /device:TPU:1, one launch (start us, length us, event | category | flops | bytes accessed | tf_op | source)
XLA Modules:
  0.0 74.4 jit_solution(1336159369431438810)
XLA Ops:
  0.0 0.0 copy-start.1
  0.0 0.0 copy-start
  0.0 1.2 %shard_map.91 = (s32[32,128]{1,0:T(8,128)S(1)}, s32[32,128]{1,0:T(8,128)S(1)}, bf16[128,1280]{1,0:T(8,128)(2,1)S(1)}) custom-call(s32[1,32]{1,0:T(1,128)} %bitcast.23, s32[1,32]{1,0:T(1,128)} %bitcast.24, bf16[32,4,1024]{2,1,0:T(4,128)(2,1)} %refs_2_.1, bf16[32,4,128]{2,1,0:T(4,128)(2,1)} %refs_3_.1, bf16[32,4,128]{2,1,0:T(4,128)(2,1)} %refs_4_.1), custom_call_target="tpu_custom_call" | custom-call | tf_op jit(solution)/shard_map/pallas_call | solution.py:300
  1.2 15.3 %all_to_all.15 = s32[32,1,128]{2,1,0:T(1,128)S(1)} all-to-all(s32[32,1,128]{2,1,0:T(1,128)S(1)} %bitcast.21), channel_id=1, replica_groups=mesh['rep'=32,'tp'=8] {'rep'}, dimensions={0} | all-to-all | bytes 32768 | tf_op jit(solution)/shard_map/all_to_all | solution.py:312
  16.6 0.0 slice-start
  16.6 0.3 shard_map.92
  16.9 16.9 %all_to_all.16 = bf16[32,8,1280]{2,1,0:T(8,128)(2,1)S(1)} all-to-all(bf16[32,8,1280]{2,1,0:T(8,128)(2,1)S(1)} %bitcast.15), channel_id=1, replica_groups=mesh['rep'=32,'tp'=8] {'rep'}, dimensions={0} | all-to-all | bytes 1310720 | tf_op jit(solution)/shard_map/all_to_all | solution.py:316
  33.8 0.0 copy-done.1
  33.8 0.0 copy-done
  33.8 0.0 slice-start.1
  33.8 3.9 %shard_map.93 = (bf16[128,1024]{1,0:T(8,128)(2,1)S(1)}, bf16[128,512]{1,0:T(8,128)(2,1)S(1)}, bf16[128,512]{1,0:T(8,128)(2,1)S(1)}) custom-call(s32[32]{0:T(128)S(1)} %copy-done.1, s32[32,128]{1,0:T(8,128)S(1)} %get-tuple-element.17.refs_1_.refs_0_, bf16[256,1280]{1,0:T(8,128)(2,1)S(1)} %bitcast.14, bf16[32,256,128]{2,1,0:T(8,128)(2,1)S(1)} %bitcast.16, ...), custom_call_target="tpu_custom_call" | custom-call | tf_op jit(solution)/shard_map/pallas_call | solution.py:320
  37.7 5.7 %collective-permute-start.2 = (bf16[128,512]{1,0:T(8,128)(2,1)S(1)}, bf16[128,512]{1,0:T(8,128)(2,1)S(1)}, u32[]{:S(2)}, u32[]{:S(2)}) collective-permute-start(bf16[128,512]{1,0:T(8,128)(2,1)S(1)} %get-tuple-element.23), channel_id=1, source_target_pairs={{0,7},{1,2},{2,1},{3,4},{4,3},{5,6},{6,5},{7,0},{8,15},{9,10},{10,... | collective-permute-start | bytes 393224 | tf_op jit(solution)/shard_map/ppermute | solution.py:347
  43.3 0.0 collective-permute-start.4
  43.4 0.0 slice-done
  43.4 0.0 slice-done.1
  43.4 0.9 %shard_map.95 = (bf16[128,512]{1,0:T(8,128)(2,1)S(1)}, bf16[128,512]{1,0:T(8,128)(2,1)S(1)}, bf16[128,512]{1,0:T(8,128)(2,1)S(1)}, bf16[128,512]{1,0:T(8,128)(2,1)S(1)}, bf16[128,512]{1,0:T(8,128)(2,1)S(1)}) custom-call(bf16[128,1024]{1,0:T(8,128)(2,1)S(1)} %get-tuple-element.19.refs_0_, bf16[1024,4096]{1,0:T(8,128)(2,1)S(1)} %bitcast.13), custom_call_target="tpu_custom_call" | custom-call | flops 671088640 | bytes 5242880 | tf_op jit(solution)/shard_map/pallas_call | solution.py:355
  44.3 1.4 %collective-permute-start.5 = (bf16[128,512]{1,0:T(8,128)(2,1)S(1)}, bf16[128,512]{1,0:T(8,128)(2,1)S(1)}, u32[]{:S(2)}, u32[]{:S(2)}) collective-permute-start(bf16[128,512]{1,0:T(8,128)(2,1)S(1)} %get-tuple-element.26), channel_id=1, source_target_pairs={{0,6},{1,3},{2,0},{3,5},{4,2},{5,7},{6,4},{7,1},{8,14},{9,11},{10,... | collective-permute-start | bytes 393224 | tf_op jit(solution)/shard_map/ppermute | solution.py:347
  45.6 2.6 %collective-permute-start = (bf16[128,512]{1,0:T(8,128)(2,1)S(1)}, bf16[128,512]{1,0:T(8,128)(2,1)S(1)}, u32[]{:S(2)}, u32[]{:S(2)}) collective-permute-start(bf16[128,512]{1,0:T(8,128)(2,1)S(1)} %get-tuple-element.20), channel_id=1, source_target_pairs={{0,7},{1,2},{2,1},{3,4},{4,3},{5,6},{6,5},{7,0},{8,15},{9,10},{10,... | collective-permute-start | bytes 393224 | tf_op jit(solution)/shard_map/ppermute | solution.py:347
  48.2 0.0 collective-permute-start.1
  48.2 0.0 collective-permute-done.2.refs_1_
  48.3 2.0 %collective-permute-start.3 = (bf16[128,512]{1,0:T(8,128)(2,1)S(1)}, bf16[128,512]{1,0:T(8,128)(2,1)S(1)}, u32[]{:S(2)}, u32[]{:S(2)}) collective-permute-start(bf16[128,512]{1,0:T(8,128)(2,1)S(1)} %shard_map.96), channel_id=1, source_target_pairs={{0,2},{1,7},{2,4},{3,1},{4,6},{5,3},{6,0},{7,5},{8,10},{9,15},{10,... | collective-permute-start | bytes 393224 | tf_op jit(solution)/shard_map/ppermute | solution.py:347
  50.2 0.9 %collective-permute-done.4.refs_1_ = bf16[128,512]{1,0:T(8,128)(2,1)S(1)} collective-permute-done((bf16[128,512]{1,0:T(8,128)(2,1)S(1)}, bf16[128,512]{1,0:T(8,128)(2,1)S(1)}, u32[]{:S(2)}, u32[]{:S(2)}) %collective-permute-start.4) | collective-permute-done | bytes 131104 | tf_op jit(solution)/shard_map/ppermute | solution.py:347
  51.1 0.0 collective-permute-done.5.refs_2_
  51.1 0.1 shard_map.97
  51.2 2.5 %collective-permute-start.6 = (bf16[128,512]{1,0:T(8,128)(2,1)S(1)}, bf16[128,512]{1,0:T(8,128)(2,1)S(1)}, u32[]{:S(2)}, u32[]{:S(2)}) collective-permute-start(bf16[128,512]{1,0:T(8,128)(2,1)S(1)} %shard_map.97), channel_id=1, source_target_pairs={{0,6},{1,3},{2,0},{3,5},{4,2},{5,7},{6,4},{7,1},{8,14},{9,11},{10,... | collective-permute-start | bytes 393224 | tf_op jit(solution)/shard_map/ppermute | solution.py:347
  53.7 0.3 shard_map.94.refs_1_
  54.0 0.3 collective-permute-done.refs_2_
  54.3 0.0 collective-permute-done.1.refs_3_
  54.3 4.1 %collective-permute-done.3.refs_4_ = bf16[128,512]{1,0:T(8,128)(2,1)S(1)} collective-permute-done((bf16[128,512]{1,0:T(8,128)(2,1)S(1)}, bf16[128,512]{1,0:T(8,128)(2,1)S(1)}, u32[]{:S(2)}, u32[]{:S(2)}) %collective-permute-start.3) | collective-permute-done | bytes 131104 | tf_op jit(solution)/shard_map/ppermute | solution.py:347
  58.4 0.0 collective-permute-done.6.refs_5_
  58.4 0.3 shard_map.98
  58.7 14.8 %all_to_all.17 = bf16[32,8,512]{2,1,0:T(8,128)(2,1)S(1)} all-to-all(bf16[32,8,512]{2,1,0:T(8,128)(2,1)S(1)} %bitcast.17), channel_id=1, replica_groups=mesh['rep'=32,'tp'=8] {'rep'}, dimensions={0} | all-to-all | bytes 524288 | tf_op jit(solution)/shard_map/all_to_all | solution.py:381
  73.5 0.9 %shard_map.99 = bf16[32,4,512]{2,1,0:T(4,128)(2,1)} custom-call(s32[32,128]{1,0:T(8,128)S(1)} %bitcast.20, bf16[256,512]{1,0:T(8,128)(2,1)S(1)} %bitcast.18), custom_call_target="tpu_custom_call" | custom-call | tf_op jit(solution)/shard_map/pallas_call | solution.py:382
  (2 shorter events, 0.0 us)
Async XLA Ops:
  0.0 33.8 %copy-start.1 = (s32[32]{0:T(128)S(1)}, s32[32]{0:T(128)}, u32[]{:S(2)}) copy-start(s32[32]{0:T(128)} %refs_0_.1) | copy-start | bytes 388
  0.0 33.8 %copy-start = (bf16[32,1,256,128]{3,2,1,0:T(8,128)(2,1)S(1)}, bf16[32,1,256,128]{3,2,1,0:T(8,128)(2,1)}, u32[]{:S(2)}) copy-start(bf16[32,1,256,128]{3,2,1,0:T(8,128)(2,1)} %param.9) | copy-start | bytes 6291460
  16.6 26.8 %slice-start = ((s8[8388608]{0:T(1024)(128)(4,1)}), s8[4194304]{0:T(1024)(128)(4,1)S(1)}, s32[]{:S(2)}) async-start(s8[8388608]{0:T(1024)(128)(4,1)} %bitcast.12), calls=%async_computation.3 | async-start | bytes 8388608
  33.8 9.5 %slice-start.1 = ((s8[8388608]{0:T(1024)(128)(4,1)}), s8[4194304]{0:T(1024)(128)(4,1)S(1)}, s32[]{:S(2)}) async-start(s8[8388608]{0:T(1024)(128)(4,1)} %bitcast.12), calls=%async_computation.4 | async-start | bytes 8388608
  37.7 10.5 %collective-permute-start.2 = (bf16[128,512]{1,0:T(8,128)(2,1)S(1)}, bf16[128,512]{1,0:T(8,128)(2,1)S(1)}, u32[]{:S(2)}, u32[]{:S(2)}) collective-permute-start(bf16[128,512]{1,0:T(8,128)(2,1)S(1)} %get-tuple-element.23), channel_id=1, source_target_pairs={{0,7},{1,2},{2,1},{3,4},{4,3},{5,6},{6,5},{7,0},{8,15},{9,10},{10,... | collective-permute-start | bytes 393224 | tf_op jit(solution)/shard_map/ppermute | solution.py:347
  43.3 7.8 %collective-permute-start.4 = (bf16[128,512]{1,0:T(8,128)(2,1)S(1)}, bf16[128,512]{1,0:T(8,128)(2,1)S(1)}, u32[]{:S(2)}, u32[]{:S(2)}) collective-permute-start(bf16[128,512]{1,0:T(8,128)(2,1)S(1)} %get-tuple-element.25), channel_id=1, source_target_pairs={{0,1},{1,0},{2,3},{3,2},{4,5},{5,4},{6,7},{7,6},{8,9},{9,8},{10,11... | collective-permute-start | bytes 393224 | tf_op jit(solution)/shard_map/ppermute | solution.py:347
  44.3 6.9 %collective-permute-start.5 = (bf16[128,512]{1,0:T(8,128)(2,1)S(1)}, bf16[128,512]{1,0:T(8,128)(2,1)S(1)}, u32[]{:S(2)}, u32[]{:S(2)}) collective-permute-start(bf16[128,512]{1,0:T(8,128)(2,1)S(1)} %get-tuple-element.26), channel_id=1, source_target_pairs={{0,6},{1,3},{2,0},{3,5},{4,2},{5,7},{6,4},{7,1},{8,14},{9,11},{10,... | collective-permute-start | bytes 393224 | tf_op jit(solution)/shard_map/ppermute | solution.py:347
  45.6 8.7 %collective-permute-start = (bf16[128,512]{1,0:T(8,128)(2,1)S(1)}, bf16[128,512]{1,0:T(8,128)(2,1)S(1)}, u32[]{:S(2)}, u32[]{:S(2)}) collective-permute-start(bf16[128,512]{1,0:T(8,128)(2,1)S(1)} %get-tuple-element.20), channel_id=1, source_target_pairs={{0,7},{1,2},{2,1},{3,4},{4,3},{5,6},{6,5},{7,0},{8,15},{9,10},{10,... | collective-permute-start | bytes 393224 | tf_op jit(solution)/shard_map/ppermute | solution.py:347
  48.2 6.1 %collective-permute-start.1 = (bf16[128,512]{1,0:T(8,128)(2,1)S(1)}, bf16[128,512]{1,0:T(8,128)(2,1)S(1)}, u32[]{:S(2)}, u32[]{:S(2)}) collective-permute-start(bf16[128,512]{1,0:T(8,128)(2,1)S(1)} %get-tuple-element.21), channel_id=1, source_target_pairs={{0,1},{1,0},{2,3},{3,2},{4,5},{5,4},{6,7},{7,6},{8,9},{9,8},{10,11... | collective-permute-start | bytes 393224 | tf_op jit(solution)/shard_map/ppermute | solution.py:347
  48.3 10.2 %collective-permute-start.3 = (bf16[128,512]{1,0:T(8,128)(2,1)S(1)}, bf16[128,512]{1,0:T(8,128)(2,1)S(1)}, u32[]{:S(2)}, u32[]{:S(2)}) collective-permute-start(bf16[128,512]{1,0:T(8,128)(2,1)S(1)} %shard_map.96), channel_id=1, source_target_pairs={{0,2},{1,7},{2,4},{3,1},{4,6},{5,3},{6,0},{7,5},{8,10},{9,15},{10,... | collective-permute-start | bytes 393224 | tf_op jit(solution)/shard_map/ppermute | solution.py:347
  51.2 7.2 %collective-permute-start.6 = (bf16[128,512]{1,0:T(8,128)(2,1)S(1)}, bf16[128,512]{1,0:T(8,128)(2,1)S(1)}, u32[]{:S(2)}, u32[]{:S(2)}) collective-permute-start(bf16[128,512]{1,0:T(8,128)(2,1)S(1)} %shard_map.97), channel_id=1, source_target_pairs={{0,6},{1,3},{2,0},{3,5},{4,2},{5,7},{6,4},{7,1},{8,14},{9,11},{10,... | collective-permute-start | bytes 393224 | tf_op jit(solution)/shard_map/ppermute | solution.py:347

commit v7 on v5

--- a/solution.py
+++ b/solution.py
@@ -228,6 +228,12 @@
     give_out(chunks, products, outs)
 
 
+def last_kernel(steps, attended_ref, weight_ref, bits_ref, wire_ref, own_ref, spots_ref, places_ref):
+    project_kernel(LAST, steps, attended_ref, weight_ref, own_ref)
+    spots_ref[...] = spots_matrix(bits_ref[...], steps)
+    places_ref[...] = spots_matrix(wire_ref[...], steps).astype(jnp.float32).T.astype(jnp.bfloat16)
+
+
 def wide(ref):
     return ref[...].astype(jnp.float32)
 
@@ -239,21 +245,19 @@
     refs[-1][...] = total.astype(jnp.bfloat16)
 
 
-def merge_kernel(steps, bits_ref, *refs):
+def merge_kernel(steps, spots_ref, *refs):
     parts, out_ref = refs[:-1], refs[-1]
     total = wide(parts[0])
     for part in parts[1:]:
         total = total + wide(part)
-    hot = spots_matrix(bits_ref[...], steps)
     out_ref[...] = jnp.dot(
-        hot, total.astype(jnp.bfloat16), preferred_element_type=jnp.float32
+        spots_ref[...], total.astype(jnp.bfloat16), preferred_element_type=jnp.float32
     ).astype(jnp.bfloat16)
 
 
-def unpack_kernel(steps, bits_ref, got_ref, out_ref):
-    out_ref[...] = take_back(spots_matrix(bits_ref[...], steps), got_ref[...]).reshape(
-        out_ref.shape
-    )
+def unpack_kernel(steps, places_ref, got_ref, out_ref):
+    rows = jnp.dot(places_ref[...], got_ref[...], preferred_element_type=jnp.float32)
+    out_ref[...] = rows.astype(jnp.bfloat16).reshape(out_ref.shape)
 
 
 def on_device(
@@ -369,7 +373,12 @@
     far, first, second = projected(SECOND)
     far = cross(far, 2)
     near = [cross(block, by) for block, by in zip(projected(THIRD), (1, -1))]
-    (own,) = projected(LAST)
+    own, spots_hot, places_hot = kernel(
+        last_kernel,
+        (chunk, out((spots, tokens)), out((tokens, spots))),
+        [vmem_spec()] * 4,
+        (vmem_spec(),) * 3,
+    )(attended, out_weight, bits, wire)
 
     def relay(*blocks):
         return kernel(relay_kernel, chunk, [vmem_spec()] * len(blocks))(*blocks)
@@ -377,11 +386,11 @@
     first = cross(relay(first, outer), -2)
     second = cross(relay(second, inner, far), 2)
     back = kernel(merge_kernel, out((spots, width)), [vmem_spec()] * 6)(
-        bits, own, *near, first, second
+        spots_hot, own, *near, first, second
     )
     back = lax.all_to_all(back.reshape(replicas, 2 * steps, width), "rep", 0, 0, tiled=True)
     return kernel(unpack_kernel, out((rows, steps, width)), [vmem_spec()] * 2)(
-        wire, back.reshape(spots, width)
+        places_hot, back.reshape(spots, width)
     )
 
 

time: 74.3 us -> 76.2 us (1.026)
  waiting for transfers between devices: 5.13 us -> 8.84 us
  starting transfers between devices: 14 us -> 13 us
    ppermute x7, waiting for transfers between devices: 5.13 us -> 8.84 us  [cross(): lax.ppermute(block, 'tp', [(i, (i + (by if i % 2 else -by)) % groups) for...]
    ppermute x7, starting transfers between devices: 14 us -> 13 us  [cross(): lax.ppermute(block, 'tp', [(i, (i + (by if i % 2 else -by)) % groups) for...]
  transfers between devices with their start and end apart: 7 -> 7, of which waited for: 2 -> 3; matrix products, arithmetic and copies ran while one was open for 0% -> 0% of each run, Pallas kernels for 2% -> 1%
where the time goes in v7:
time: 76.2 us; the launch traced here: 76 us
  blocking collectives  46 us (60%)
  starting transfers between devices  13 us (17%)
  waiting for transfers between devices  8.84 us (12%)
  Pallas kernels  8.03 us (11%)
    all_to_all x1, blocking collectives, on_device(): lax.all_to_all(packed.reshape(replicas, 2 * steps, full), 'rep', 0, 0, ti...  16.9 us
    all_to_all x1, blocking collectives, on_device(): lax.all_to_all(wire.reshape(replicas, 1, tokens), 'rep', 0, 0, tiled=True)  15.3 us
    all_to_all x1, blocking collectives, on_device(): lax.all_to_all(back.reshape(replicas, 2 * steps, width), 'rep', 0, 0, til...  13.8 us
    ppermute x7, starting transfers between devices, cross(): lax.ppermute(block, 'tp', [(i, (i + (by if i % 2 else -by)) % groups) for...  13 us
    ppermute x7, waiting for transfers between devices, cross(): lax.ppermute(block, 'tp', [(i, (i + (by if i % 2 else -by)) % groups) for...  8.84 us
    pallas_call x1, Pallas kernels, on_device(): kernel(attend_kernel, (out((tokens, features)), chunk, chunk), [smem_spec...  3.86 us
  transfers between devices with their start and end apart: 7, of which 3 were waited for; matrix products, arithmetic and copies ran while one was open for 0% of the time, Pallas kernels for 1%

profile of v7, /device:TPU:1, one launch (start us, length us, event | category | flops | bytes accessed | tf_op | source)
XLA Modules:
  0.0 76.0 jit_solution(14549206979193704819)
XLA Ops:
  0.0 0.0 copy-start
  0.0 0.0 copy-start.1
  0.0 1.2 %shard_map.91 = (s32[32,128]{1,0:T(8,128)S(1)}, s32[32,128]{1,0:T(8,128)S(1)}, bf16[128,1280]{1,0:T(8,128)(2,1)S(1)}) custom-call(s32[1,32]{1,0:T(1,128)} %bitcast.23, s32[1,32]{1,0:T(1,128)} %bitcast.24, bf16[32,4,1024]{2,1,0:T(4,128)(2,1)} %refs_2_.1, bf16[32,4,128]{2,1,0:T(4,128)(2,1)} %refs_3_.1, bf16[32,4,128]{2,1,0:T(4,128)(2,1)} %refs_4_.1), custom_call_target="tpu_custom_call" | custom-call | tf_op jit(solution)/shard_map/pallas_call | solution.py:305
  1.2 15.3 %all_to_all.15 = s32[32,1,128]{2,1,0:T(1,128)S(1)} all-to-all(s32[32,1,128]{2,1,0:T(1,128)S(1)} %bitcast.21), channel_id=1, replica_groups=mesh['rep'=32,'tp'=8] {'rep'}, dimensions={0} | all-to-all | bytes 32768 | tf_op jit(solution)/shard_map/all_to_all | solution.py:317
  16.6 0.0 slice-start
  16.6 0.3 shard_map.92
  16.9 16.9 %all_to_all.16 = bf16[32,8,1280]{2,1,0:T(8,128)(2,1)S(1)} all-to-all(bf16[32,8,1280]{2,1,0:T(8,128)(2,1)S(1)} %bitcast.15), channel_id=1, replica_groups=mesh['rep'=32,'tp'=8] {'rep'}, dimensions={0} | all-to-all | bytes 1310720 | tf_op jit(solution)/shard_map/all_to_all | solution.py:321
  33.8 0.0 copy-done
  33.8 0.0 copy-done.1
  33.8 0.0 slice-start.1
  33.8 3.9 %shard_map.93 = (bf16[128,1024]{1,0:T(8,128)(2,1)S(1)}, bf16[128,512]{1,0:T(8,128)(2,1)S(1)}, bf16[128,512]{1,0:T(8,128)(2,1)S(1)}) custom-call(s32[32]{0:T(128)S(1)} %copy-done.1, s32[32,128]{1,0:T(8,128)S(1)} %get-tuple-element.19.refs_1_.refs_2_, bf16[256,1280]{1,0:T(8,128)(2,1)S(1)} %bitcast.14, bf16[32,256,128]{2,1,0:T(8,128)(2,1)S(1)} %bitcast.16, ...), custom_call_target="tpu_custom_call" | custom-call | tf_op jit(solution)/shard_map/pallas_call | solution.py:325
  37.7 0.0 slice-done
  37.7 0.0 slice-done.1
  37.7 0.6 shard_map.96
  38.3 6.1 %collective-permute-start.5 = (bf16[128,512]{1,0:T(8,128)(2,1)S(1)}, bf16[128,512]{1,0:T(8,128)(2,1)S(1)}, u32[]{:S(2)}, u32[]{:S(2)}) collective-permute-start(bf16[128,512]{1,0:T(8,128)(2,1)S(1)} %get-tuple-element.32), channel_id=1, source_target_pairs={{0,6},{1,3},{2,0},{3,5},{4,2},{5,7},{6,4},{7,1},{8,14},{9,11},{10,... | collective-permute-start | bytes 393224 | tf_op jit(solution)/shard_map/ppermute | solution.py:352
  44.4 0.0 collective-permute-start.4
  44.4 1.5 %collective-permute-start.2 = (bf16[128,512]{1,0:T(8,128)(2,1)S(1)}, bf16[128,512]{1,0:T(8,128)(2,1)S(1)}, u32[]{:S(2)}, u32[]{:S(2)}) collective-permute-start(bf16[128,512]{1,0:T(8,128)(2,1)S(1)} %get-tuple-element.29), channel_id=1, source_target_pairs={{0,7},{1,2},{2,1},{3,4},{4,3},{5,6},{6,5},{7,0},{8,15},{9,10},{10,... | collective-permute-start | bytes 393224 | tf_op jit(solution)/shard_map/ppermute | solution.py:352
  45.9 0.5 shard_map.95
  46.4 1.3 %collective-permute-start = (bf16[128,512]{1,0:T(8,128)(2,1)S(1)}, bf16[128,512]{1,0:T(8,128)(2,1)S(1)}, u32[]{:S(2)}, u32[]{:S(2)}) collective-permute-start(bf16[128,512]{1,0:T(8,128)(2,1)S(1)} %get-tuple-element.26), channel_id=1, source_target_pairs={{0,7},{1,2},{2,1},{3,4},{4,3},{5,6},{6,5},{7,0},{8,15},{9,10},{10,... | collective-permute-start | bytes 393224 | tf_op jit(solution)/shard_map/ppermute | solution.py:352
  47.7 0.3 collective-permute-start.1
  48.0 0.0 collective-permute-done.5.refs_2_
  48.0 1.9 %collective-permute-done.4.refs_1_ = bf16[128,512]{1,0:T(8,128)(2,1)S(1)} collective-permute-done((bf16[128,512]{1,0:T(8,128)(2,1)S(1)}, bf16[128,512]{1,0:T(8,128)(2,1)S(1)}, u32[]{:S(2)}, u32[]{:S(2)}) %collective-permute-start.4) | collective-permute-done | bytes 131104 | tf_op jit(solution)/shard_map/ppermute | solution.py:352
  49.8 0.1 shard_map.98
  49.9 3.7 %collective-permute-start.6 = (bf16[128,512]{1,0:T(8,128)(2,1)S(1)}, bf16[128,512]{1,0:T(8,128)(2,1)S(1)}, u32[]{:S(2)}, u32[]{:S(2)}) collective-permute-start(bf16[128,512]{1,0:T(8,128)(2,1)S(1)} %shard_map.98), channel_id=1, source_target_pairs={{0,6},{1,3},{2,0},{3,5},{4,2},{5,7},{6,4},{7,1},{8,14},{9,11},{10,... | collective-permute-start | bytes 393224 | tf_op jit(solution)/shard_map/ppermute | solution.py:352
  53.6 0.0 collective-permute-done.2.refs_1_
  53.6 0.1 collective-permute-start.3
  53.7 0.4 shard_map.94
  54.1 0.0 collective-permute-done.refs_2_
  54.1 0.0 collective-permute-done.1.refs_3_
  54.1 2.1 %collective-permute-done.6.refs_5_ = bf16[128,512]{1,0:T(8,128)(2,1)S(1)} collective-permute-done((bf16[128,512]{1,0:T(8,128)(2,1)S(1)}, bf16[128,512]{1,0:T(8,128)(2,1)S(1)}, u32[]{:S(2)}, u32[]{:S(2)}) %collective-permute-start.6) | collective-permute-done | bytes 131104 | tf_op jit(solution)/shard_map/ppermute | solution.py:352
  56.2 4.9 %collective-permute-done.3.refs_4_ = bf16[128,512]{1,0:T(8,128)(2,1)S(1)} collective-permute-done((bf16[128,512]{1,0:T(8,128)(2,1)S(1)}, bf16[128,512]{1,0:T(8,128)(2,1)S(1)}, u32[]{:S(2)}, u32[]{:S(2)}) %collective-permute-start.3) | collective-permute-done | bytes 131104 | tf_op jit(solution)/shard_map/ppermute | solution.py:352
  61.1 0.3 shard_map.99
  61.4 13.8 %all_to_all.17 = bf16[32,8,512]{2,1,0:T(8,128)(2,1)S(1)} all-to-all(bf16[32,8,512]{2,1,0:T(8,128)(2,1)S(1)} %bitcast.18), channel_id=1, replica_groups=mesh['rep'=32,'tp'=8] {'rep'}, dimensions={0} | all-to-all | bytes 524288 | tf_op jit(solution)/shard_map/all_to_all | solution.py:391
  75.1 0.8 %shard_map.100 = bf16[32,4,512]{2,1,0:T(4,128)(2,1)} custom-call(bf16[128,256]{1,0:T(8,128)(2,1)S(1)} %get-tuple-element.23.refs_0_, bf16[256,512]{1,0:T(8,128)(2,1)S(1)} %bitcast.17), custom_call_target="tpu_custom_call" | custom-call | tf_op jit(solution)/shard_map/pallas_call | solution.py:392
  (2 shorter events, 0.0 us)
Async XLA Ops:
  0.0 33.8 %copy-start = (bf16[32,1,256,128]{3,2,1,0:T(8,128)(2,1)S(1)}, bf16[32,1,256,128]{3,2,1,0:T(8,128)(2,1)}, u32[]{:S(2)}) copy-start(bf16[32,1,256,128]{3,2,1,0:T(8,128)(2,1)} %param.9) | copy-start | bytes 6291460
  0.0 33.8 %copy-start.1 = (s32[32]{0:T(128)S(1)}, s32[32]{0:T(128)}, u32[]{:S(2)}) copy-start(s32[32]{0:T(128)} %refs_0_.1) | copy-start | bytes 388
  16.6 21.1 %slice-start = ((s8[8388608]{0:T(1024)(128)(4,1)}), s8[4194304]{0:T(1024)(128)(4,1)S(1)}, s32[]{:S(2)}) async-start(s8[8388608]{0:T(1024)(128)(4,1)} %bitcast.12), calls=%async_computation.3 | async-start | bytes 8388608
  33.8 3.9 %slice-start.1 = ((s8[8388608]{0:T(1024)(128)(4,1)}), s8[4194304]{0:T(1024)(128)(4,1)S(1)}, s32[]{:S(2)}) async-start(s8[8388608]{0:T(1024)(128)(4,1)} %bitcast.12), calls=%async_computation.4 | async-start | bytes 8388608
  38.3 9.6 %collective-permute-start.5 = (bf16[128,512]{1,0:T(8,128)(2,1)S(1)}, bf16[128,512]{1,0:T(8,128)(2,1)S(1)}, u32[]{:S(2)}, u32[]{:S(2)}) collective-permute-start(bf16[128,512]{1,0:T(8,128)(2,1)S(1)} %get-tuple-element.32), channel_id=1, source_target_pairs={{0,6},{1,3},{2,0},{3,5},{4,2},{5,7},{6,4},{7,1},{8,14},{9,11},{10,... | collective-permute-start | bytes 393224 | tf_op jit(solution)/shard_map/ppermute | solution.py:352
  44.4 5.4 %collective-permute-start.4 = (bf16[128,512]{1,0:T(8,128)(2,1)S(1)}, bf16[128,512]{1,0:T(8,128)(2,1)S(1)}, u32[]{:S(2)}, u32[]{:S(2)}) collective-permute-start(bf16[128,512]{1,0:T(8,128)(2,1)S(1)} %get-tuple-element.31), channel_id=1, source_target_pairs={{0,1},{1,0},{2,3},{3,2},{4,5},{5,4},{6,7},{7,6},{8,9},{9,8},{10,11... | collective-permute-start | bytes 393224 | tf_op jit(solution)/shard_map/ppermute | solution.py:352
  44.4 9.2 %collective-permute-start.2 = (bf16[128,512]{1,0:T(8,128)(2,1)S(1)}, bf16[128,512]{1,0:T(8,128)(2,1)S(1)}, u32[]{:S(2)}, u32[]{:S(2)}) collective-permute-start(bf16[128,512]{1,0:T(8,128)(2,1)S(1)} %get-tuple-element.29), channel_id=1, source_target_pairs={{0,7},{1,2},{2,1},{3,4},{4,3},{5,6},{6,5},{7,0},{8,15},{9,10},{10,... | collective-permute-start | bytes 393224 | tf_op jit(solution)/shard_map/ppermute | solution.py:352
  46.4 7.7 %collective-permute-start = (bf16[128,512]{1,0:T(8,128)(2,1)S(1)}, bf16[128,512]{1,0:T(8,128)(2,1)S(1)}, u32[]{:S(2)}, u32[]{:S(2)}) collective-permute-start(bf16[128,512]{1,0:T(8,128)(2,1)S(1)} %get-tuple-element.26), channel_id=1, source_target_pairs={{0,7},{1,2},{2,1},{3,4},{4,3},{5,6},{6,5},{7,0},{8,15},{9,10},{10,... | collective-permute-start | bytes 393224 | tf_op jit(solution)/shard_map/ppermute | solution.py:352
  47.7 6.4 %collective-permute-start.1 = (bf16[128,512]{1,0:T(8,128)(2,1)S(1)}, bf16[128,512]{1,0:T(8,128)(2,1)S(1)}, u32[]{:S(2)}, u32[]{:S(2)}) collective-permute-start(bf16[128,512]{1,0:T(8,128)(2,1)S(1)} %get-tuple-element.27), channel_id=1, source_target_pairs={{0,1},{1,0},{2,3},{3,2},{4,5},{5,4},{6,7},{7,6},{8,9},{9,8},{10,11... | collective-permute-start | bytes 393224 | tf_op jit(solution)/shard_map/ppermute | solution.py:352
  49.9 6.3 %collective-permute-start.6 = (bf16[128,512]{1,0:T(8,128)(2,1)S(1)}, bf16[128,512]{1,0:T(8,128)(2,1)S(1)}, u32[]{:S(2)}, u32[]{:S(2)}) collective-permute-start(bf16[128,512]{1,0:T(8,128)(2,1)S(1)} %shard_map.98), channel_id=1, source_target_pairs={{0,6},{1,3},{2,0},{3,5},{4,2},{5,7},{6,4},{7,1},{8,14},{9,11},{10,... | collective-permute-start | bytes 393224 | tf_op jit(solution)/shard_map/ppermute | solution.py:352
  53.6 7.4 %collective-permute-start.3 = (bf16[128,512]{1,0:T(8,128)(2,1)S(1)}, bf16[128,512]{1,0:T(8,128)(2,1)S(1)}, u32[]{:S(2)}, u32[]{:S(2)}) collective-permute-start(bf16[128,512]{1,0:T(8,128)(2,1)S(1)} %shard_map.97), channel_id=1, source_target_pairs={{0,2},{1,7},{2,4},{3,1},{4,6},{5,3},{6,0},{7,5},{8,10},{9,15},{10,... | collective-permute-start | bytes 393224 | tf_op jit(solution)/shard_map/ppermute | solution.py:352

commit v8 on v5

--- a/solution.py
+++ b/solution.py
@@ -10,8 +10,7 @@
 MASKED = -1e30
 FIRST = ((3, 5),)
 SECOND = (4, (6, 2))
-THIRD = ((1, 7),)
-LAST = (0,)
+THIRD = ((1, 7), 0)
 VMEM_BYTES = 24 * 1024 * 1024
 
 
@@ -368,8 +367,8 @@
 
     far, first, second = projected(SECOND)
     far = cross(far, 2)
-    near = [cross(block, by) for block, by in zip(projected(THIRD), (1, -1))]
-    (own,) = projected(LAST)
+    *near, own = projected(THIRD)
+    near = [cross(block, by) for block, by in zip(near, (1, -1))]
 
     def relay(*blocks):
         return kernel(relay_kernel, chunk, [vmem_spec()] * len(blocks))(*blocks)

time: 74.3 us -> 74.3 us (level)
  transfers between devices with their start and end apart: 7 -> 7, of which waited for: 2 -> 3; matrix products, arithmetic and copies ran while one was open for 0% -> 0% of each run, Pallas kernels for 2% -> 2%
where the time goes in v8:
time: 74.3 us; the launch traced here: 74.1 us
  blocking collectives  46.8 us (63%)
  starting transfers between devices  14 us (19%)
  Pallas kernels  7.87 us (11%)
  waiting for transfers between devices  5.37 us (7%)
    all_to_all x1, blocking collectives, on_device(): lax.all_to_all(packed.reshape(replicas, 2 * steps, full), 'rep', 0, 0, ti...  16.9 us
    all_to_all x1, blocking collectives, on_device(): lax.all_to_all(wire.reshape(replicas, 1, tokens), 'rep', 0, 0, tiled=True)  15.3 us
    all_to_all x1, blocking collectives, on_device(): lax.all_to_all(back.reshape(replicas, 2 * steps, width), 'rep', 0, 0, til...  14.5 us
    ppermute x7, starting transfers between devices, cross(): lax.ppermute(block, 'tp', [(i, (i + (by if i % 2 else -by)) % groups) for...  14 us
    ppermute x7, waiting for transfers between devices, cross(): lax.ppermute(block, 'tp', [(i, (i + (by if i % 2 else -by)) % groups) for...  5.37 us
    pallas_call x1, Pallas kernels, on_device(): kernel(attend_kernel, (out((tokens, features)), chunk, chunk), [smem_spec...  3.86 us
  transfers between devices with their start and end apart: 7, of which 3 were waited for; matrix products, arithmetic and copies ran while one was open for 0% of the time, Pallas kernels for 2%

profile of v8, /device:TPU:1, one launch (start us, length us, event | category | flops | bytes accessed | tf_op | source)
XLA Modules:
  0.0 74.1 jit_solution(9402703812650056777)
XLA Ops:
  0.0 0.0 copy-start.1
  0.0 0.0 copy-start
  0.0 1.2 %shard_map.91 = (s32[32,128]{1,0:T(8,128)S(1)}, s32[32,128]{1,0:T(8,128)S(1)}, bf16[128,1280]{1,0:T(8,128)(2,1)S(1)}) custom-call(s32[1,32]{1,0:T(1,128)} %bitcast.23, s32[1,32]{1,0:T(1,128)} %bitcast.24, bf16[32,4,1024]{2,1,0:T(4,128)(2,1)} %refs_2_.1, bf16[32,4,128]{2,1,0:T(4,128)(2,1)} %refs_3_.1, bf16[32,4,128]{2,1,0:T(4,128)(2,1)} %refs_4_.1), custom_call_target="tpu_custom_call" | custom-call | tf_op jit(solution)/shard_map/pallas_call | solution.py:300
  1.2 15.3 %all_to_all.15 = s32[32,1,128]{2,1,0:T(1,128)S(1)} all-to-all(s32[32,1,128]{2,1,0:T(1,128)S(1)} %bitcast.21), channel_id=1, replica_groups=mesh['rep'=32,'tp'=8] {'rep'}, dimensions={0} | all-to-all | bytes 32768 | tf_op jit(solution)/shard_map/all_to_all | solution.py:312
  16.6 0.0 slice-start
  16.6 0.3 shard_map.92
  16.9 16.9 %all_to_all.16 = bf16[32,8,1280]{2,1,0:T(8,128)(2,1)S(1)} all-to-all(bf16[32,8,1280]{2,1,0:T(8,128)(2,1)S(1)} %bitcast.15), channel_id=1, replica_groups=mesh['rep'=32,'tp'=8] {'rep'}, dimensions={0} | all-to-all | bytes 1310720 | tf_op jit(solution)/shard_map/all_to_all | solution.py:316
  33.8 0.0 copy-done.1
  33.8 0.0 copy-done
  33.8 0.0 slice-start.1
  33.8 3.9 %shard_map.93 = (bf16[128,1024]{1,0:T(8,128)(2,1)S(1)}, bf16[128,512]{1,0:T(8,128)(2,1)S(1)}, bf16[128,512]{1,0:T(8,128)(2,1)S(1)}) custom-call(s32[32]{0:T(128)S(1)} %copy-done.1, s32[32,128]{1,0:T(8,128)S(1)} %get-tuple-element.18.refs_1_.refs_0_, bf16[256,1280]{1,0:T(8,128)(2,1)S(1)} %bitcast.14, bf16[32,256,128]{2,1,0:T(8,128)(2,1)S(1)} %bitcast.16, ...), custom_call_target="tpu_custom_call" | custom-call | tf_op jit(solution)/shard_map/pallas_call | solution.py:320
  37.7 5.7 %collective-permute-start.2 = (bf16[128,512]{1,0:T(8,128)(2,1)S(1)}, bf16[128,512]{1,0:T(8,128)(2,1)S(1)}, u32[]{:S(2)}, u32[]{:S(2)}) collective-permute-start(bf16[128,512]{1,0:T(8,128)(2,1)S(1)} %get-tuple-element.25), channel_id=1, source_target_pairs={{0,7},{1,2},{2,1},{3,4},{4,3},{5,6},{6,5},{7,0},{8,15},{9,10},{10,... | collective-permute-start | bytes 393224 | tf_op jit(solution)/shard_map/ppermute | solution.py:347
  43.3 0.0 collective-permute-start.4
  43.4 0.0 slice-done
  43.4 0.0 slice-done.1
  43.4 0.6 shard_map.95
  44.0 1.4 %collective-permute-start.5 = (bf16[128,512]{1,0:T(8,128)(2,1)S(1)}, bf16[128,512]{1,0:T(8,128)(2,1)S(1)}, u32[]{:S(2)}, u32[]{:S(2)}) collective-permute-start(bf16[128,512]{1,0:T(8,128)(2,1)S(1)} %get-tuple-element.28), channel_id=1, source_target_pairs={{0,6},{1,3},{2,0},{3,5},{4,2},{5,7},{6,4},{7,1},{8,14},{9,11},{10,... | collective-permute-start | bytes 393224 | tf_op jit(solution)/shard_map/ppermute | solution.py:347
  45.3 0.6 shard_map.94
  46.0 2.7 %collective-permute-start = (bf16[128,512]{1,0:T(8,128)(2,1)S(1)}, bf16[128,512]{1,0:T(8,128)(2,1)S(1)}, u32[]{:S(2)}, u32[]{:S(2)}) collective-permute-start(bf16[128,512]{1,0:T(8,128)(2,1)S(1)} %get-tuple-element.22), channel_id=1, source_target_pairs={{0,7},{1,2},{2,1},{3,4},{4,3},{5,6},{6,5},{7,0},{8,15},{9,10},{10,... | collective-permute-start | bytes 393224 | tf_op jit(solution)/shard_map/ppermute | solution.py:347
  48.6 0.0 collective-permute-start.1
  48.6 0.0 collective-permute-done.2.refs_1_
  48.7 2.0 %collective-permute-start.3 = (bf16[128,512]{1,0:T(8,128)(2,1)S(1)}, bf16[128,512]{1,0:T(8,128)(2,1)S(1)}, u32[]{:S(2)}, u32[]{:S(2)}) collective-permute-start(bf16[128,512]{1,0:T(8,128)(2,1)S(1)} %shard_map.96), channel_id=1, source_target_pairs={{0,2},{1,7},{2,4},{3,1},{4,6},{5,3},{6,0},{7,5},{8,10},{9,15},{10,... | collective-permute-start | bytes 393224 | tf_op jit(solution)/shard_map/ppermute | solution.py:347
  50.6 0.6 collective-permute-done.4.refs_1_
  51.2 0.0 collective-permute-done.5.refs_2_
  51.2 0.1 shard_map.97
  51.3 2.3 %collective-permute-start.6 = (bf16[128,512]{1,0:T(8,128)(2,1)S(1)}, bf16[128,512]{1,0:T(8,128)(2,1)S(1)}, u32[]{:S(2)}, u32[]{:S(2)}) collective-permute-start(bf16[128,512]{1,0:T(8,128)(2,1)S(1)} %shard_map.97), channel_id=1, source_target_pairs={{0,6},{1,3},{2,0},{3,5},{4,2},{5,7},{6,4},{7,1},{8,14},{9,11},{10,... | collective-permute-start | bytes 393224 | tf_op jit(solution)/shard_map/ppermute | solution.py:347
  53.6 0.4 collective-permute-done.refs_2_
  54.0 0.0 collective-permute-done.1.refs_3_
  54.0 4.4 %collective-permute-done.3.refs_4_ = bf16[128,512]{1,0:T(8,128)(2,1)S(1)} collective-permute-done((bf16[128,512]{1,0:T(8,128)(2,1)S(1)}, bf16[128,512]{1,0:T(8,128)(2,1)S(1)}, u32[]{:S(2)}, u32[]{:S(2)}) %collective-permute-start.3) | collective-permute-done | bytes 131104 | tf_op jit(solution)/shard_map/ppermute | solution.py:347
  58.4 0.0 collective-permute-done.6.refs_5_
  58.4 0.3 shard_map.98
  58.7 14.5 %all_to_all.17 = bf16[32,8,512]{2,1,0:T(8,128)(2,1)S(1)} all-to-all(bf16[32,8,512]{2,1,0:T(8,128)(2,1)S(1)} %bitcast.17), channel_id=1, replica_groups=mesh['rep'=32,'tp'=8] {'rep'}, dimensions={0} | all-to-all | bytes 524288 | tf_op jit(solution)/shard_map/all_to_all | solution.py:381
  73.2 0.9 %shard_map.99 = bf16[32,4,512]{2,1,0:T(4,128)(2,1)} custom-call(s32[32,128]{1,0:T(8,128)S(1)} %bitcast.20, bf16[256,512]{1,0:T(8,128)(2,1)S(1)} %bitcast.18), custom_call_target="tpu_custom_call" | custom-call | tf_op jit(solution)/shard_map/pallas_call | solution.py:382
  (2 shorter events, 0.0 us)
Async XLA Ops:
  0.0 33.8 %copy-start.1 = (s32[32]{0:T(128)S(1)}, s32[32]{0:T(128)}, u32[]{:S(2)}) copy-start(s32[32]{0:T(128)} %refs_0_.1) | copy-start | bytes 388
  0.0 33.8 %copy-start = (bf16[32,1,256,128]{3,2,1,0:T(8,128)(2,1)S(1)}, bf16[32,1,256,128]{3,2,1,0:T(8,128)(2,1)}, u32[]{:S(2)}) copy-start(bf16[32,1,256,128]{3,2,1,0:T(8,128)(2,1)} %param.9) | copy-start | bytes 6291460
  16.6 26.8 %slice-start = ((s8[8388608]{0:T(1024)(128)(4,1)}), s8[4194304]{0:T(1024)(128)(4,1)S(1)}, s32[]{:S(2)}) async-start(s8[8388608]{0:T(1024)(128)(4,1)} %bitcast.12), calls=%async_computation.3 | async-start | bytes 8388608
  33.8 9.5 %slice-start.1 = ((s8[8388608]{0:T(1024)(128)(4,1)}), s8[4194304]{0:T(1024)(128)(4,1)S(1)}, s32[]{:S(2)}) async-start(s8[8388608]{0:T(1024)(128)(4,1)} %bitcast.12), calls=%async_computation.4 | async-start | bytes 8388608
  37.7 10.9 %collective-permute-start.2 = (bf16[128,512]{1,0:T(8,128)(2,1)S(1)}, bf16[128,512]{1,0:T(8,128)(2,1)S(1)}, u32[]{:S(2)}, u32[]{:S(2)}) collective-permute-start(bf16[128,512]{1,0:T(8,128)(2,1)S(1)} %get-tuple-element.25), channel_id=1, source_target_pairs={{0,7},{1,2},{2,1},{3,4},{4,3},{5,6},{6,5},{7,0},{8,15},{9,10},{10,... | collective-permute-start | bytes 393224 | tf_op jit(solution)/shard_map/ppermute | solution.py:347
  43.3 7.9 %collective-permute-start.4 = (bf16[128,512]{1,0:T(8,128)(2,1)S(1)}, bf16[128,512]{1,0:T(8,128)(2,1)S(1)}, u32[]{:S(2)}, u32[]{:S(2)}) collective-permute-start(bf16[128,512]{1,0:T(8,128)(2,1)S(1)} %get-tuple-element.27), channel_id=1, source_target_pairs={{0,1},{1,0},{2,3},{3,2},{4,5},{5,4},{6,7},{7,6},{8,9},{9,8},{10,11... | collective-permute-start | bytes 393224 | tf_op jit(solution)/shard_map/ppermute | solution.py:347
  44.0 7.2 %collective-permute-start.5 = (bf16[128,512]{1,0:T(8,128)(2,1)S(1)}, bf16[128,512]{1,0:T(8,128)(2,1)S(1)}, u32[]{:S(2)}, u32[]{:S(2)}) collective-permute-start(bf16[128,512]{1,0:T(8,128)(2,1)S(1)} %get-tuple-element.28), channel_id=1, source_target_pairs={{0,6},{1,3},{2,0},{3,5},{4,2},{5,7},{6,4},{7,1},{8,14},{9,11},{10,... | collective-permute-start | bytes 393224 | tf_op jit(solution)/shard_map/ppermute | solution.py:347
  46.0 8.1 %collective-permute-start = (bf16[128,512]{1,0:T(8,128)(2,1)S(1)}, bf16[128,512]{1,0:T(8,128)(2,1)S(1)}, u32[]{:S(2)}, u32[]{:S(2)}) collective-permute-start(bf16[128,512]{1,0:T(8,128)(2,1)S(1)} %get-tuple-element.22), channel_id=1, source_target_pairs={{0,7},{1,2},{2,1},{3,4},{4,3},{5,6},{6,5},{7,0},{8,15},{9,10},{10,... | collective-permute-start | bytes 393224 | tf_op jit(solution)/shard_map/ppermute | solution.py:347
  48.6 5.4 %collective-permute-start.1 = (bf16[128,512]{1,0:T(8,128)(2,1)S(1)}, bf16[128,512]{1,0:T(8,128)(2,1)S(1)}, u32[]{:S(2)}, u32[]{:S(2)}) collective-permute-start(bf16[128,512]{1,0:T(8,128)(2,1)S(1)} %get-tuple-element.23), channel_id=1, source_target_pairs={{0,1},{1,0},{2,3},{3,2},{4,5},{5,4},{6,7},{7,6},{8,9},{9,8},{10,11... | collective-permute-start | bytes 393224 | tf_op jit(solution)/shard_map/ppermute | solution.py:347
  48.7 9.7 %collective-permute-start.3 = (bf16[128,512]{1,0:T(8,128)(2,1)S(1)}, bf16[128,512]{1,0:T(8,128)(2,1)S(1)}, u32[]{:S(2)}, u32[]{:S(2)}) collective-permute-start(bf16[128,512]{1,0:T(8,128)(2,1)S(1)} %shard_map.96), channel_id=1, source_target_pairs={{0,2},{1,7},{2,4},{3,1},{4,6},{5,3},{6,0},{7,5},{8,10},{9,15},{10,... | collective-permute-start | bytes 393224 | tf_op jit(solution)/shard_map/ppermute | solution.py:347
  51.3 7.1 %collective-permute-start.6 = (bf16[128,512]{1,0:T(8,128)(2,1)S(1)}, bf16[128,512]{1,0:T(8,128)(2,1)S(1)}, u32[]{:S(2)}, u32[]{:S(2)}) collective-permute-start(bf16[128,512]{1,0:T(8,128)(2,1)S(1)} %shard_map.97), channel_id=1, source_target_pairs={{0,6},{1,3},{2,0},{3,5},{4,2},{5,7},{6,4},{7,1},{8,14},{9,11},{10,... | collective-permute-start | bytes 393224 | tf_op jit(solution)/shard_map/ppermute | solution.py:347
